TPU v7x, 32 devices: a whole 2x2x4 slice. The times are simulated.
32 devices in a mesh: src: 4 (over y, x), rcv: 4 (over z), freq: 2 (over core).
Axes of the slice: x: 2, y: 2, z: 4, core: 2. Of those that a mesh axis runs over, the one named last changes fastest.
Arguments:
- wavefield: float32 [2, 2, 512, 512], P(None, 'freq', 'src', 'rcv'), may hold values from -6 to 6
- op_table: float32 [2, 64, 19], replicated, may hold values from -1.2 to 1.2
- vel_index: int32 [32], replicated, may hold values from 0 to 15
- interp_index: int32 [16, 2], replicated, may hold values from 0 to 62
- interp_weight: float32 [16, 2], replicated, may hold values from 0 to 1
- freq_perm: int32 [2], P('freq'), may hold values from 0 to 1, each once
Outputs:
- sunk: float32 [2, 2, 512, 512], P(None, 'freq', 'src', 'rcv')
- image: float32 [512], P('rcv')
Inputs may be any that keep to these rules, and one draw needn't show every extreme that they name: `freq_perm`: each of the 2 frequencies is held by exactly one slot.
All inputs are finite; a program needn't handle non-finite values.
Results may differ from a plain program's by a relative error of at most 0.00012.
Values sent between devices are 32-bit elements; how exact they have to be, the bound alone decides.
No kernel may reach another device: no remote copies, remote signals or barrier semaphores. Data moves between devices by JAX's collectives and lax.ppermute only.
A program may use at most 64 MiB of HBM per device.

v0:
```python
import jax
import jax.numpy as jnp
from jax import lax
from jax.sharding import PartitionSpec as P

SUBSTEPS = 4
TILE = 16


def extended(shard, sides, width):
    for axis, dim in sides:
        size, length = (lax.axis_size(axis), shard.shape[dim])
        up = [(i, (i + 1) % size) for i in range(size - 1)]
        down = [(j, i) for i, j in up]
        last = lax.slice_in_dim(shard, length - width, length, axis=dim)
        first = lax.slice_in_dim(shard, 0, width, axis=dim)
        before = lax.ppermute(last, axis, up)
        after = lax.ppermute(first, axis, down)
        shard = jnp.concatenate([before, shard, after], axis=dim)
    return shard


def convolve(padded, coefficients, along_axis, span_width):
    out_shape = list(padded.shape[1:])
    out_shape[along_axis - 1] = span_width
    zeros_init = jnp.zeros(tuple(out_shape), jnp.float32)

    def add_tap(tap_index, totals):
        window = lax.dynamic_slice_in_dim(padded, tap_index, span_width, axis=along_axis)
        coef_tap = lax.dynamic_index_in_dim(coefficients, tap_index, axis=2, keepdims=False)
        coef_real = coef_tap[0]
        coef_imag = coef_tap[1]
        if along_axis == 3:
            coef_real = coef_real[:, None, :]
            coef_imag = coef_imag[:, None, :]
        else:
            coef_real = coef_real[:, :, None]
            coef_imag = coef_imag[:, :, None]
        real_sum = totals[0] + (coef_real * window[0] - coef_imag * window[1])
        imag_sum = totals[1] + (coef_real * window[1] + coef_imag * window[0])
        return (real_sum, imag_sum)

    real_acc, imag_acc = lax.fori_loop(0, coefficients.shape[2], add_tap, (zeros_init, zeros_init))
    return jnp.stack([real_acc, imag_acc])


def build_taps(op_table, interp_index, interp_weight, freq_ids):
    freq_count = interp_index.shape[1]
    table_len = op_table.shape[1]
    pick_freq = freq_ids[:, None] == jnp.arange(freq_count, dtype=jnp.int32)[None, :]
    table_row = jnp.sum(jnp.where(pick_freq[None], interp_index[:, None, :], 0), axis=2)
    weights = jnp.sum(jnp.where(pick_freq[None], interp_weight[:, None, :], 0.0), axis=2)
    rows_iota = jnp.arange(table_len, dtype=jnp.int32)
    pick_lower = table_row[:, :, None] == rows_iota
    pick_upper = (table_row + 1)[:, :, None] == rows_iota
    lower_taps = jnp.sum(
        jnp.where(pick_lower[None, :, :, :, None], op_table[:, None, None, :, :], 0.0), axis=3
    )
    upper_taps = jnp.sum(
        jnp.where(pick_upper[None, :, :, :, None], op_table[:, None, None, :, :], 0.0), axis=3
    )
    mixed = lower_taps * (1.0 - weights)[None, :, :, None] + upper_taps * weights[None, :, :, None]
    return jnp.transpose(mixed, (0, 2, 3, 1))


def coefficients_at(mixed_taps, vel_index, positions, lateral):
    tile_count = vel_index.shape[0]
    vel_count = mixed_taps.shape[3]
    tile_of = jnp.clip(positions, 0, lateral - 1) // TILE
    pick_tile = tile_of[:, None] == jnp.arange(tile_count, dtype=jnp.int32)[None, :]
    velocity = jnp.sum(jnp.where(pick_tile, vel_index[None, :], 0), axis=1)
    pick_velocity = (velocity[:, None] == jnp.arange(vel_count, dtype=jnp.int32)[None, :]).astype(
        jnp.float32
    )
    return jnp.einsum("cfkv,xv->cfkx", mixed_taps, pick_velocity, precision=lax.Precision.HIGHEST)


def body(wavefield, op_table, vel_index, interp_index, interp_weight, freq_perm):
    src_rows = wavefield.shape[2]
    rcv_cols = wavefield.shape[3]
    lateral = rcv_cols * lax.axis_size("rcv")
    half_taps = op_table.shape[2] // 2
    mixed_taps = build_taps(op_table, interp_index, interp_weight, freq_perm)
    col_start = lax.axis_index("rcv") * rcv_cols
    row_start = lax.axis_index("src") * src_rows
    wave_field = wavefield
    rim_depth = SUBSTEPS * half_taps
    current = extended(wave_field, (("rcv", 3),), rim_depth)
    for substep in range(SUBSTEPS):
        remain = rim_depth - (substep + 1) * half_taps
        span_width = rcv_cols + 2 * remain
        positions = col_start - remain + jnp.arange(span_width, dtype=jnp.int32)
        step_coefficients = coefficients_at(mixed_taps, vel_index, positions, lateral)
        current = convolve(current, step_coefficients, 3, span_width)
        if remain > 0:
            inside = (positions >= 0) & (positions < lateral)
            current = jnp.where(inside, current, 0.0)
    wave_field = current
    row_positions = row_start + jnp.arange(src_rows, dtype=jnp.int32)
    src_coefficients = coefficients_at(mixed_taps, vel_index, row_positions, lateral)
    for substep in range(SUBSTEPS):
        padded = extended(wave_field, (("src", 2),), half_taps)
        wave_field = convolve(padded, src_coefficients, 2, src_rows)
    offset = col_start - row_start
    valid = (offset >= 0) & (offset < src_rows)
    start = jnp.clip(offset, 0, src_rows - rcv_cols)
    diag_block = lax.dynamic_slice_in_dim(wave_field[0], start, rcv_cols, axis=1)
    diagonal_sum = jnp.sum(jnp.diagonal(diag_block, axis1=1, axis2=2), axis=0)
    local_image = jnp.where(valid, diagonal_sum, 0.0)
    zero_image = lax.psum(local_image, ("src", "freq"))
    return (wave_field, zero_image)


def solution(mesh):
    in_specs = (P(None, "freq", "src", "rcv"), P(), P(), P(), P(), P("freq"))
    out_specs = (P(None, "freq", "src", "rcv"), P("rcv"))
    return jax.shard_map(body, mesh=mesh, in_specs=in_specs, out_specs=out_specs, check_vma=False)
```

profile of v0, /device:TPU:0, one launch (start us, length us, event | category | flops | bytes accessed | tf_op | source)
XLA Modules:
  0.0 93.2 jit_solution(10032633201003680663)
XLA Ops:
  0.6 1.1 %fusion.31 = (f32[2,1,128,36]{3,2,1,0:T(8,128)S(1)}, f32[2,1,128,36]{3,2,1,0:T(8,128)S(1)}) fusion(f32[2,1,128,128]{3,2,1,0:T(8,128)} %param.22), kind=kLoop, calls=%fused_computation.151 | loop fusion | bytes 147456 | tf_op jit(solution)/shard_map/slice | solution.py:15
  1.7 4.9 %collective-permute-start = (f32[2,1,128,36]{3,2,1,0:T(8,128)S(1)}, f32[2,1,128,36]{3,2,1,0:T(8,128)S(1)}, u32[]{:S(2)}, u32[]{:S(2)}) collective-permute-start(f32[2,1,128,36]{3,2,1,0:T(8,128)S(1)} %get-tuple-element.1166), channel_id=1, source_target_pairs={{0,2},{2,4},{4,6},{1,3},{3,5},{5,7},{8,10},{10,12},{12,14},{9,11},... | collective-permute-start | bytes 110600 | tf_op jit(solution)/shard_map/ppermute | solution.py:17
  6.7 1.3 %collective-permute-start.1 = (f32[2,1,128,36]{3,2,1,0:T(8,128)S(1)}, f32[2,1,128,36]{3,2,1,0:T(8,128)S(1)}, u32[]{:S(2)}, u32[]{:S(2)}) collective-permute-start(f32[2,1,128,36]{3,2,1,0:T(8,128)S(1)} %get-tuple-element.1167), channel_id=1, source_target_pairs={{2,0},{4,2},{6,4},{3,1},{5,3},{7,5},{10,8},{12,10},{14,12},{11,9},... | collective-permute-start | bytes 110600 | tf_op jit(solution)/shard_map/ppermute | solution.py:18
  8.7 0.7 copy-done.3
  9.6 0.7 copy-done.4
  10.3 0.6 copy-done.2
  11.1 0.2 select_reduce_fusion.1
  12.3 1.2 %collective-permute-done.1 = f32[2,1,128,36]{3,2,1,0:T(8,128)S(1)} collective-permute-done((f32[2,1,128,36]{3,2,1,0:T(8,128)S(1)}, f32[2,1,128,36]{3,2,1,0:T(8,128)S(1)}, u32[]{:S(2)}, u32[]{:S(2)}) %collective-permute-start.1) | collective-permute-done | bytes 36896 | tf_op jit(solution)/shard_map/ppermute | solution.py:18
  13.7 4.2 %while.128 = (s32[]{:T(128)}, f32[1,128,182]{2,1,0:T(8,128)S(1)}, f32[1,128,182]{2,1,0:T(8,128)S(1)}, f32[2,1,19,182]{3,2,1,0:T(8,128)S(1)}, f32[2,1,128,200]{3,2,1,0:T(8,128)S(1)}, /*index=5*/s32[]{:T(128)}, s32[]{:T(128)}, s32[]{}) while((s32[]{:T(128)}, f32[1,128,182]{2,1,0:T(8,128)S(1)}, f32[1,128,182]{2,1,0:T(8,128)S(1)}, ...), condition=%wide.region_6.7_spmd.clone, body=%wide.region_5.6_spmd.clone.sunk | while | flops 232964 | bytes 563595 | solution.py:43
  13.7 0.2 select_add_fusion.24
  14.0 0.2 select_add_fusion.24
  14.2 0.2 select_add_fusion.24
  14.4 0.2 select_add_fusion.24
  14.6 0.2 select_add_fusion.24
  14.8 0.2 select_add_fusion.24
  15.1 0.2 select_add_fusion.24
  15.5 0.2 select_add_fusion.24
  15.7 0.2 select_add_fusion.24
  15.9 0.2 select_add_fusion.24
  16.1 0.2 select_add_fusion.24
  16.4 0.2 select_add_fusion.24
  16.6 0.2 select_add_fusion.24
  16.8 0.2 select_add_fusion.24
  17.0 0.2 select_add_fusion.24
  17.2 0.2 select_add_fusion.24
  17.5 0.2 select_add_fusion.24
  17.7 0.2 select_add_fusion.24
  17.9 4.2 %while.129 = (s32[]{:T(128)}, f32[1,128,164]{2,1,0:T(8,128)S(1)}, f32[1,128,164]{2,1,0:T(8,128)S(1)}, f32[2,1,19,164]{3,2,1,0:T(8,128)S(1)}, f32[2,1,128,182]{3,2,1,0:T(8,128)S(1)}, /*index=5*/s32[]{:T(128)}, s32[]{:T(128)}, s32[]{}) while((s32[]{:T(128)}, f32[1,128,164]{2,1,0:T(8,128)S(1)}, f32[1,128,164]{2,1,0:T(8,128)S(1)}, ...), condition=%wide.region_9.10_spmd.clone, body=%wide.region_8.9_spmd.clone.sunk | while | flops 209924 | bytes 507867 | solution.py:43
  17.9 0.2 select_add_fusion.25
  18.2 0.2 select_add_fusion.25
  18.4 0.2 select_add_fusion.25
  18.6 0.2 select_add_fusion.25
  18.8 0.2 select_add_fusion.25
  19.0 0.2 select_add_fusion.25
  19.5 0.2 select_add_fusion.25
  19.7 0.2 select_add_fusion.25
  19.9 0.2 select_add_fusion.25
  20.1 0.2 select_add_fusion.25
  20.3 0.2 select_add_fusion.25
  20.6 0.2 select_add_fusion.25
  20.8 0.2 select_add_fusion.25
  21.0 0.2 select_add_fusion.25
  21.2 0.2 select_add_fusion.25
  22.1 4.2 %while.130 = (s32[]{:T(128)}, f32[1,128,146]{2,1,0:T(8,128)S(1)}, f32[1,128,146]{2,1,0:T(8,128)S(1)}, f32[2,1,19,146]{3,2,1,0:T(8,128)S(1)}, f32[2,1,128,164]{3,2,1,0:T(8,128)S(1)}, /*index=5*/s32[]{:T(128)}, s32[]{:T(128)}, s32[]{}) while((s32[]{:T(128)}, f32[1,128,146]{2,1,0:T(8,128)S(1)}, f32[1,128,146]{2,1,0:T(8,128)S(1)}, ...), condition=%wide.region_12.13_spmd.clone, body=%wide.region_11.12_spmd.clone.sunk | while | flops 186884 | bytes 452139 | solution.py:43
  26.3 3.2 %while.131 = (s32[]{:T(128)}, f32[1,128,128]{2,1,0:T(8,128)S(1)}, f32[1,128,128]{2,1,0:T(8,128)S(1)}, f32[2,1,19,128]{3,2,1,0:T(8,128)S(1)}, f32[2,1,128,146]{3,2,1,0:T(8,128)S(1)}, /*index=5*/s32[]{:T(128)}, s32[]{:T(128)}, s32[]{}) while((s32[]{:T(128)}, f32[1,128,128]{2,1,0:T(8,128)S(1)}, f32[1,128,128]{2,1,0:T(8,128)S(1)}, ...), condition=%wide.region_15.16_spmd.clone, body=%wide.region_14.15_spmd.clone.sunk | while | flops 163844 | bytes 396411 | solution.py:43
  29.6 3.4 %collective-permute-start.2 = (f32[2,1,9,128]{3,2,1,0:T(8,128)S(1)}, f32[2,1,9,128]{3,2,1,0:T(8,128)S(1)}, u32[]{:S(2)}, u32[]{:S(2)}) collective-permute-start(f32[2,1,9,128]{3,2,1,0:T(8,128)S(1)} %get-tuple-element.1164), channel_id=1, source_target_pairs={{0,8},{8,16},{16,24},{1,9},{9,17},{17,25},{2,10},{10,18},{18,26},{... | collective-permute-start | bytes 27656 | tf_op jit(solution)/shard_map/ppermute | solution.py:17
  33.0 1.3 %collective-permute-start.3 = (f32[2,1,9,128]{3,2,1,0:T(8,128)S(1)}, f32[2,1,9,128]{3,2,1,0:T(8,128)S(1)}, u32[]{:S(2)}, u32[]{:S(2)}) collective-permute-start(f32[2,1,9,128]{3,2,1,0:T(8,128)S(1)} %get-tuple-element.1165), channel_id=1, source_target_pairs={{8,0},{16,8},{24,16},{9,1},{17,9},{25,17},{10,2},{18,10},{26,18},{... | collective-permute-start | bytes 27656 | tf_op jit(solution)/shard_map/ppermute | solution.py:18
  34.5 4.2 %collective-permute-done.3 = f32[2,1,9,128]{3,2,1,0:T(8,128)S(1)} collective-permute-done((f32[2,1,9,128]{3,2,1,0:T(8,128)S(1)}, f32[2,1,9,128]{3,2,1,0:T(8,128)S(1)}, u32[]{:S(2)}, u32[]{:S(2)}) %collective-permute-start.3) | collective-permute-done | bytes 9248 | tf_op jit(solution)/shard_map/ppermute | solution.py:18
  38.7 3.2 %while.132 = (s32[]{:T(128)}, f32[1,128,128]{2,1,0:T(8,128)S(1)}, f32[1,128,128]{2,1,0:T(8,128)S(1)}, f32[2,1,19,128]{3,2,1,0:T(8,128)S(1)}, f32[2,1,146,128]{3,2,1,0:T(8,128)S(1)}, /*index=5*/s32[]{:T(128)}, s32[]{:T(128)}, s32[]{}) while((s32[]{:T(128)}, f32[1,128,128]{2,1,0:T(8,128)S(1)}, f32[1,128,128]{2,1,0:T(8,128)S(1)}, ...), condition=%wide.region_18.19_spmd.clone, body=%wide.region_17.18_spmd.clone.sunk | while | flops 163844 | bytes 396411 | solution.py:43
  41.9 4.3 %collective-permute-start.4 = (f32[2,1,9,128]{3,2,1,0:T(8,128)S(1)}, f32[2,1,9,128]{3,2,1,0:T(8,128)S(1)}, u32[]{:S(2)}, u32[]{:S(2)}) collective-permute-start(f32[2,1,9,128]{3,2,1,0:T(8,128)S(1)} %get-tuple-element.1162), channel_id=1, source_target_pairs={{0,8},{8,16},{16,24},{1,9},{9,17},{17,25},{2,10},{10,18},{18,26},{... | collective-permute-start | bytes 27656 | tf_op jit(solution)/shard_map/ppermute | solution.py:17
  46.2 1.3 %collective-permute-start.5 = (f32[2,1,9,128]{3,2,1,0:T(8,128)S(1)}, f32[2,1,9,128]{3,2,1,0:T(8,128)S(1)}, u32[]{:S(2)}, u32[]{:S(2)}) collective-permute-start(f32[2,1,9,128]{3,2,1,0:T(8,128)S(1)} %get-tuple-element.1163), channel_id=1, source_target_pairs={{8,0},{16,8},{24,16},{9,1},{17,9},{25,17},{10,2},{18,10},{26,18},{... | collective-permute-start | bytes 27656 | tf_op jit(solution)/shard_map/ppermute | solution.py:18
  47.6 4.2 %collective-permute-done.5 = f32[2,1,9,128]{3,2,1,0:T(8,128)S(1)} collective-permute-done((f32[2,1,9,128]{3,2,1,0:T(8,128)S(1)}, f32[2,1,9,128]{3,2,1,0:T(8,128)S(1)}, u32[]{:S(2)}, u32[]{:S(2)}) %collective-permute-start.5) | collective-permute-done | bytes 9248 | tf_op jit(solution)/shard_map/ppermute | solution.py:18
  51.8 3.2 %while.133 = (s32[]{:T(128)}, f32[1,128,128]{2,1,0:T(8,128)S(1)}, f32[1,128,128]{2,1,0:T(8,128)S(1)}, f32[2,1,19,128]{3,2,1,0:T(8,128)S(1)}, f32[2,1,146,128]{3,2,1,0:T(8,128)S(1)}, /*index=5*/s32[]{:T(128)}, s32[]{:T(128)}, s32[]{}) while((s32[]{:T(128)}, f32[1,128,128]{2,1,0:T(8,128)S(1)}, f32[1,128,128]{2,1,0:T(8,128)S(1)}, ...), condition=%wide.region_20.21_spmd.clone, body=%wide.region_19.20_spmd.clone.sunk | while | flops 163844 | bytes 396411 | solution.py:43
  55.0 3.4 %collective-permute-start.6 = (f32[2,1,9,128]{3,2,1,0:T(8,128)S(1)}, f32[2,1,9,128]{3,2,1,0:T(8,128)S(1)}, u32[]{:S(2)}, u32[]{:S(2)}) collective-permute-start(f32[2,1,9,128]{3,2,1,0:T(8,128)S(1)} %get-tuple-element.1160), channel_id=1, source_target_pairs={{0,8},{8,16},{16,24},{1,9},{9,17},{17,25},{2,10},{10,18},{18,26},{... | collective-permute-start | bytes 27656 | tf_op jit(solution)/shard_map/ppermute | solution.py:17
  58.4 1.3 %collective-permute-start.7 = (f32[2,1,9,128]{3,2,1,0:T(8,128)S(1)}, f32[2,1,9,128]{3,2,1,0:T(8,128)S(1)}, u32[]{:S(2)}, u32[]{:S(2)}) collective-permute-start(f32[2,1,9,128]{3,2,1,0:T(8,128)S(1)} %get-tuple-element.1161), channel_id=1, source_target_pairs={{8,0},{16,8},{24,16},{9,1},{17,9},{25,17},{10,2},{18,10},{26,18},{... | collective-permute-start | bytes 27656 | tf_op jit(solution)/shard_map/ppermute | solution.py:18
  59.9 4.2 %collective-permute-done.7 = f32[2,1,9,128]{3,2,1,0:T(8,128)S(1)} collective-permute-done((f32[2,1,9,128]{3,2,1,0:T(8,128)S(1)}, f32[2,1,9,128]{3,2,1,0:T(8,128)S(1)}, u32[]{:S(2)}, u32[]{:S(2)}) %collective-permute-start.7) | collective-permute-done | bytes 9248 | tf_op jit(solution)/shard_map/ppermute | solution.py:18
  64.1 3.2 %while.134 = (s32[]{:T(128)}, f32[1,128,128]{2,1,0:T(8,128)S(1)}, f32[1,128,128]{2,1,0:T(8,128)S(1)}, f32[2,1,19,128]{3,2,1,0:T(8,128)S(1)}, f32[2,1,146,128]{3,2,1,0:T(8,128)S(1)}, /*index=5*/s32[]{:T(128)}, s32[]{:T(128)}, s32[]{}) while((s32[]{:T(128)}, f32[1,128,128]{2,1,0:T(8,128)S(1)}, f32[1,128,128]{2,1,0:T(8,128)S(1)}, ...), condition=%wide.region_22.23_spmd.clone, body=%wide.region_21.22_spmd.clone.sunk | while | flops 163844 | bytes 396411 | solution.py:43
  67.3 2.8 %collective-permute-start.8 = (f32[2,1,9,128]{3,2,1,0:T(8,128)S(1)}, f32[2,1,9,128]{3,2,1,0:T(8,128)S(1)}, u32[]{:S(2)}, u32[]{:S(2)}) collective-permute-start(f32[2,1,9,128]{3,2,1,0:T(8,128)S(1)} %get-tuple-element.1158), channel_id=1, source_target_pairs={{0,8},{8,16},{16,24},{1,9},{9,17},{17,25},{2,10},{10,18},{18,26},{... | collective-permute-start | bytes 27656 | tf_op jit(solution)/shard_map/ppermute | solution.py:17
  70.1 1.3 %collective-permute-start.9 = (f32[2,1,9,128]{3,2,1,0:T(8,128)S(1)}, f32[2,1,9,128]{3,2,1,0:T(8,128)S(1)}, u32[]{:S(2)}, u32[]{:S(2)}) collective-permute-start(f32[2,1,9,128]{3,2,1,0:T(8,128)S(1)} %get-tuple-element.1159), channel_id=1, source_target_pairs={{8,0},{16,8},{24,16},{9,1},{17,9},{25,17},{10,2},{18,10},{26,18},{... | collective-permute-start | bytes 27656 | tf_op jit(solution)/shard_map/ppermute | solution.py:18
  71.5 4.2 %collective-permute-done.9 = f32[2,1,9,128]{3,2,1,0:T(8,128)S(1)} collective-permute-done((f32[2,1,9,128]{3,2,1,0:T(8,128)S(1)}, f32[2,1,9,128]{3,2,1,0:T(8,128)S(1)}, u32[]{:S(2)}, u32[]{:S(2)}) %collective-permute-start.9) | collective-permute-done | bytes 9248 | tf_op jit(solution)/shard_map/ppermute | solution.py:18
  75.8 3.2 %while.135 = (s32[]{:T(128)}, f32[1,128,128]{2,1,0:T(8,128)S(1)}, f32[1,128,128]{2,1,0:T(8,128)S(1)}, f32[2,1,19,128]{3,2,1,0:T(8,128)S(1)}, f32[2,1,146,128]{3,2,1,0:T(8,128)S(1)}, /*index=5*/s32[]{:T(128)}, s32[]{:T(128)}, s32[]{}) while((s32[]{:T(128)}, f32[1,128,128]{2,1,0:T(8,128)S(1)}, f32[1,128,128]{2,1,0:T(8,128)S(1)}, ...), condition=%wide.region_24.25_spmd.clone, body=%wide.region_23.24_spmd.clone.sunk | while | flops 163844 | bytes 396411 | solution.py:43
  79.0 1.2 %gather_fusion = f32[128]{0:T(128)S(1)} fusion(f32[128,128]{1,0:T(8,128)S(1)} %bitcast.256, s32[128]{0:T(128)S(1)} %or_bitcast_fusion), kind=kCustom, calls=%fused_computation | custom fusion | bytes 2048 | tf_op jit(solution)/shard_map/jit(diagonal)/gather | solution.py:108
  80.3 12.3 %psum.7 = f32[128]{0:T(128)} all-reduce(f32[128]{0:T(128)S(1)} %broadcast_select_fusion), channel_id=1, replica_groups=mesh['src'=4,'rcv'=4,'freq'=2] {'src','freq'}, use_global_device_ids=true, to_apply=%region_25.26 | all-reduce | flops 128 | bytes 1024 | tf_op jit(solution)/shard_map/psum | solution.py:110
  92.6 0.7 pad_maximum_fusion.5
  (337 shorter events, 19.7 us)
Async XLA Ops:
  1.7 10.6 %collective-permute-start = (f32[2,1,128,36]{3,2,1,0:T(8,128)S(1)}, f32[2,1,128,36]{3,2,1,0:T(8,128)S(1)}, u32[]{:S(2)}, u32[]{:S(2)}) collective-permute-start(f32[2,1,128,36]{3,2,1,0:T(8,128)S(1)} %get-tuple-element.1166), channel_id=1, source_target_pairs={{0,2},{2,4},{4,6},{1,3},{3,5},{5,7},{8,10},{10,12},{12,14},{9,11},... | collective-permute-start | bytes 110600 | tf_op jit(solution)/shard_map/ppermute | solution.py:17
  6.7 2.9 %copy-start.1 = (f32[2,64,19]{1,0,2:T(2,128)S(1)}, f32[2,64,19]{1,0,2:T(2,128)}, u32[]{:S(2)}) copy-start(f32[2,64,19]{1,0,2:T(2,128)} %param.23) | copy-start | bytes 29188
  6.7 6.9 %collective-permute-start.1 = (f32[2,1,128,36]{3,2,1,0:T(8,128)S(1)}, f32[2,1,128,36]{3,2,1,0:T(8,128)S(1)}, u32[]{:S(2)}, u32[]{:S(2)}) collective-permute-start(f32[2,1,128,36]{3,2,1,0:T(8,128)S(1)} %get-tuple-element.1167), channel_id=1, source_target_pairs={{2,0},{4,2},{6,4},{3,1},{5,3},{7,5},{10,8},{12,10},{14,12},{11,9},... | collective-permute-start | bytes 110600 | tf_op jit(solution)/shard_map/ppermute | solution.py:18
  8.7 0.7 copy-start.3
  9.5 0.7 copy-start.4
  10.3 0.7 copy-start.2
  11.6 2.0 %copy-start = (f32[2,1,128,128]{3,2,1,0:T(8,128)S(1)}, f32[2,1,128,128]{3,2,1,0:T(8,128)}, u32[]{:S(2)}) copy-start(f32[2,1,128,128]{3,2,1,0:T(8,128)} %param.22) | copy-start | bytes 393220
  29.6 4.9 %collective-permute-start.2 = (f32[2,1,9,128]{3,2,1,0:T(8,128)S(1)}, f32[2,1,9,128]{3,2,1,0:T(8,128)S(1)}, u32[]{:S(2)}, u32[]{:S(2)}) collective-permute-start(f32[2,1,9,128]{3,2,1,0:T(8,128)S(1)} %get-tuple-element.1164), channel_id=1, source_target_pairs={{0,8},{8,16},{16,24},{1,9},{9,17},{17,25},{2,10},{10,18},{18,26},{... | collective-permute-start | bytes 27656 | tf_op jit(solution)/shard_map/ppermute | solution.py:17
  33.0 5.6 %collective-permute-start.3 = (f32[2,1,9,128]{3,2,1,0:T(8,128)S(1)}, f32[2,1,9,128]{3,2,1,0:T(8,128)S(1)}, u32[]{:S(2)}, u32[]{:S(2)}) collective-permute-start(f32[2,1,9,128]{3,2,1,0:T(8,128)S(1)} %get-tuple-element.1165), channel_id=1, source_target_pairs={{8,0},{16,8},{24,16},{9,1},{17,9},{25,17},{10,2},{18,10},{26,18},{... | collective-permute-start | bytes 27656 | tf_op jit(solution)/shard_map/ppermute | solution.py:18
  41.9 5.7 %collective-permute-start.4 = (f32[2,1,9,128]{3,2,1,0:T(8,128)S(1)}, f32[2,1,9,128]{3,2,1,0:T(8,128)S(1)}, u32[]{:S(2)}, u32[]{:S(2)}) collective-permute-start(f32[2,1,9,128]{3,2,1,0:T(8,128)S(1)} %get-tuple-element.1162), channel_id=1, source_target_pairs={{0,8},{8,16},{16,24},{1,9},{9,17},{17,25},{2,10},{10,18},{18,26},{... | collective-permute-start | bytes 27656 | tf_op jit(solution)/shard_map/ppermute | solution.py:17
  46.2 5.6 %collective-permute-start.5 = (f32[2,1,9,128]{3,2,1,0:T(8,128)S(1)}, f32[2,1,9,128]{3,2,1,0:T(8,128)S(1)}, u32[]{:S(2)}, u32[]{:S(2)}) collective-permute-start(f32[2,1,9,128]{3,2,1,0:T(8,128)S(1)} %get-tuple-element.1163), channel_id=1, source_target_pairs={{8,0},{16,8},{24,16},{9,1},{17,9},{25,17},{10,2},{18,10},{26,18},{... | collective-permute-start | bytes 27656 | tf_op jit(solution)/shard_map/ppermute | solution.py:18
  55.0 4.8 %collective-permute-start.6 = (f32[2,1,9,128]{3,2,1,0:T(8,128)S(1)}, f32[2,1,9,128]{3,2,1,0:T(8,128)S(1)}, u32[]{:S(2)}, u32[]{:S(2)}) collective-permute-start(f32[2,1,9,128]{3,2,1,0:T(8,128)S(1)} %get-tuple-element.1160), channel_id=1, source_target_pairs={{0,8},{8,16},{16,24},{1,9},{9,17},{17,25},{2,10},{10,18},{18,26},{... | collective-permute-start | bytes 27656 | tf_op jit(solution)/shard_map/ppermute | solution.py:17
  58.4 5.6 %collective-permute-start.7 = (f32[2,1,9,128]{3,2,1,0:T(8,128)S(1)}, f32[2,1,9,128]{3,2,1,0:T(8,128)S(1)}, u32[]{:S(2)}, u32[]{:S(2)}) collective-permute-start(f32[2,1,9,128]{3,2,1,0:T(8,128)S(1)} %get-tuple-element.1161), channel_id=1, source_target_pairs={{8,0},{16,8},{24,16},{9,1},{17,9},{25,17},{10,2},{18,10},{26,18},{... | collective-permute-start | bytes 27656 | tf_op jit(solution)/shard_map/ppermute | solution.py:18
  67.3 4.3 %collective-permute-start.8 = (f32[2,1,9,128]{3,2,1,0:T(8,128)S(1)}, f32[2,1,9,128]{3,2,1,0:T(8,128)S(1)}, u32[]{:S(2)}, u32[]{:S(2)}) collective-permute-start(f32[2,1,9,128]{3,2,1,0:T(8,128)S(1)} %get-tuple-element.1158), channel_id=1, source_target_pairs={{0,8},{8,16},{16,24},{1,9},{9,17},{17,25},{2,10},{10,18},{18,26},{... | collective-permute-start | bytes 27656 | tf_op jit(solution)/shard_map/ppermute | solution.py:17
  70.1 5.6 %collective-permute-start.9 = (f32[2,1,9,128]{3,2,1,0:T(8,128)S(1)}, f32[2,1,9,128]{3,2,1,0:T(8,128)S(1)}, u32[]{:S(2)}, u32[]{:S(2)}) collective-permute-start(f32[2,1,9,128]{3,2,1,0:T(8,128)S(1)} %get-tuple-element.1159), channel_id=1, source_target_pairs={{8,0},{16,8},{24,16},{9,1},{17,9},{25,17},{10,2},{18,10},{26,18},{... | collective-permute-start | bytes 27656 | tf_op jit(solution)/shard_map/ppermute | solution.py:18
where the time goes:
time: 93.7 us; the launch traced here: 93.2 us
  starting transfers between devices  25.3 us (27%)
  other arithmetic  23.3 us (25%)
  waiting for transfers between devices  18.3 us (20%)
  blocking collectives  12.3 us (13%)
  local copies, waits for them, and re-layouts  6.28 us (7%)
  loops' own time  5.27 us (6%)
  between operations  1.81 us (2%)
    add x152, other arithmetic, add_tap(): imag_sum = totals[1] + (coef_real * window[1] + coef_imag * window[0])  21.3 us
    ppermute x5, starting transfers between devices, extended(): before = lax.ppermute(last, axis, up)  18.8 us
    ppermute x5, waiting for transfers between devices, extended(): after = lax.ppermute(first, axis, down)  18 us
    psum x1, blocking collectives, body(): zero_image = lax.psum(local_image, ('src', 'freq'))  12.3 us
    ppermute x5, starting transfers between devices, extended(): after = lax.ppermute(first, axis, down)  6.46 us
    another operation x8, loops' own time, convolve(): lax.fori_loop(0, coefficients.shape[2], add_tap, (zeros_init, zeros_init))  5.27 us
    unnamed x11, local copies, waits for them, and re-layouts  1.99 us
  transfers between devices with their start and end apart: 10, of which 8 were waited for; matrix products, arithmetic and copies ran while one was open for 2% of the time, Pallas kernels for 0%

commit v1 on v0

v1 whole, which is shorter than its diff:
```python
import functools

import jax
import jax.numpy as jnp
from jax import lax
from jax.experimental import pallas as pl
from jax.experimental.pallas import tpu as pltpu
from jax.sharding import PartitionSpec as P

SUBSTEPS = 4
TILE = 16
VMEM_LIMIT = 32 * 1024 * 1024
F32 = jnp.float32
BF16 = jnp.bfloat16


def halves(value):
    high = value.astype(BF16)
    low = (value - high.astype(F32)).astype(BF16)
    return high, low


def dot(left, right):
    return jnp.dot(left, right, preferred_element_type=F32)


def dot3(left, right):
    left_high, left_low = left
    right_high, right_low = right
    return dot(left_high, right_high) + (dot(left_high, right_low) + dot(left_low, right_high))


def square_product(left, right):
    rows, cols = left[0].shape[0], right[0].shape[1]
    stacked = halves(jnp.concatenate(left, axis=0))
    beside = halves(jnp.concatenate(right, axis=1))
    full = dot3(stacked, beside)
    real = full[:rows, :cols] - full[rows:, cols:]
    imag = full[:rows, cols:] + full[rows:, :cols]
    return real, imag


def build_operator(start, lateral, width, taps, vel_ref, index_ref, weight_ref, perm_ref, table, band):
    window = 2 * width
    count = window // TILE
    seam = count - count // 4
    tiles = vel_ref.shape[0]
    slot = perm_ref[0]
    for position in range(count):
        tile = start // TILE + position - (count if position >= seam else 0)
        inside = jnp.logical_and(tile >= 0, tile < tiles).astype(F32)
        velocity = vel_ref[jnp.clip(tile, 0, tiles - 1)]
        row = index_ref[velocity, slot]
        weight = weight_ref[velocity, slot]
        low_weight = (1.0 - weight) * inside
        high_weight = weight * inside
        shift = (position * TILE - taps // 2) % window
        for part in range(2):
            mixed = table[part, pl.ds(row, 1), :] * low_weight + table[part, pl.ds(row + 1, 1), :] * high_weight
            spread = jnp.broadcast_to(mixed, (TILE, mixed.shape[1]))
            slanted = pltpu.roll(spread, 0, 1, stride=1, stride_axis=0)
            wide = jnp.concatenate([slanted, jnp.zeros((TILE, window - slanted.shape[1]), F32)], axis=1)
            band[part, pl.ds(position * TILE, TILE), :] = pltpu.roll(wide, shift, 1)
    once = (band[0], band[1])
    twice = square_product(once, once)
    four = square_product((twice[0][:width], twice[1][:width]), twice)
    place = lax.broadcasted_iota(jnp.int32, (width, window), 1)
    cell = start + jnp.where(place < window - width // 2, place, place - window)
    inside = jnp.logical_and(cell >= 0, cell < lateral)
    return jnp.where(inside, four[0], 0.0), jnp.where(inside, four[1], 0.0)


def fill_table(table_ref, table):
    table[...] = jnp.zeros_like(table)
    table[:, :, : table_ref.shape[2]] = table_ref[...]


def rcv_operator_kernel(lateral, vel_ref, index_ref, weight_ref, perm_ref, table_ref, full_ref, high_ref, low_ref, table, band):
    width = full_ref.shape[1] // 2
    fill_table(table_ref, table)
    start = lax.axis_index("rcv") * width
    real, imag = build_operator(
        start, lateral, width, table_ref.shape[2], vel_ref, index_ref, weight_ref, perm_ref, table, band
    )
    turned = jnp.concatenate([real.T, imag.T], axis=1)
    full_ref[...] = turned
    high_ref[...], low_ref[...] = halves(turned)


def src_operator_kernel(lateral, vel_ref, index_ref, weight_ref, perm_ref, table_ref, high_ref, low_ref, table, band):
    chunks, width = high_ref.shape[0], high_ref.shape[2] // 2
    fill_table(table_ref, table)
    for chunk in range(chunks):
        start = (lax.axis_index("src") * chunks + chunk) * width
        real, imag = build_operator(
            start, lateral, width, table_ref.shape[2], vel_ref, index_ref, weight_ref, perm_ref, table, band
        )
        high_ref[chunk], low_ref[chunk] = halves(jnp.concatenate([real, imag], axis=0))


def receiver_kernel(rim, wave_ref, first_ref, second_ref, full_ref, high_ref, low_ref, sunk_ref, head_ref, tail_ref, image_ref):
    rows, width = wave_ref.shape[1], wave_ref.shape[2]
    half = width // 2
    odd = lax.axis_index("freq") % 2 == 1
    lane = lax.broadcasted_iota(jnp.int32, (rows // 2, width), 1)
    extended = []
    for part in range(2):
        first, second = first_ref[part], second_ref[part]
        before = jnp.where(odd, second, first)
        after = jnp.where(odd, first, second)
        top = jnp.where(lane < half, after, before)
        bottom = pltpu.roll(jnp.where(lane < half, before, after), half, 1)
        halo = jnp.concatenate([top, bottom], axis=0)
        extended.append(jnp.concatenate([wave_ref[part], halo], axis=1))
    full = dot3(halves(jnp.concatenate(extended, axis=0)), (high_ref[...], low_ref[...]))
    real = full[:rows, :width] - full[rows:, width:]
    imag = full[:rows, width:] + full[rows:, :width]
    sunk_ref[0] = real
    sunk_ref[1] = imag
    chunks = rows // width
    ahead = lax.axis_index("src") * chunks - lax.axis_index("rcv")
    line = lax.broadcasted_iota(jnp.int32, (width, 2 * width), 0)
    image = jnp.zeros((1, width), F32)
    for chunk in range(chunks):
        away = ahead + chunk
        beside = jnp.logical_or(
            jnp.logical_and(away == 1, line < half), jnp.logical_and(away == -1, line >= half)
        )
        weights = jnp.where(away == 0, full_ref[:width], jnp.where(beside, full_ref[width:], 0.0))
        piece = slice(chunk * width, (chunk + 1) * width)
        terms = weights[:, :width] * real[piece] - weights[:, width:] * imag[piece]
        image = image + jnp.sum(terms, axis=0, keepdims=True)
    image_ref[...] = image
    edge = head_ref.shape[1]
    head_ref[0] = real[:edge]
    head_ref[1] = imag[:edge]
    tail_ref[0] = real[rows - edge :]
    tail_ref[1] = imag[rows - edge :]
    head_ref[0, edge - 1 :, :] = image
    tail_ref[0, :1, :] = image


def source_kernel(field_ref, before_ref, after_ref, high_ref, low_ref, out_ref):
    rows, width = field_ref.shape[1], field_ref.shape[2]
    half = width // 2
    chunks = rows // width
    edge = before_ref.shape[1]
    gap = jnp.zeros((half - edge, width), F32)
    for chunk in range(chunks):
        low, high = chunk * width, (chunk + 1) * width
        extended = []
        for part in range(2):
            if chunk + 1 < chunks:
                after = field_ref[part, high : high + half]
            else:
                after = jnp.concatenate([after_ref[part], gap], axis=0)
            if chunk > 0:
                before = field_ref[part, low - half : low]
            else:
                before = jnp.concatenate([gap, before_ref[part]], axis=0)
            extended.append(jnp.concatenate([field_ref[part, low:high], after, before], axis=0))
        full = dot3((high_ref[chunk], low_ref[chunk]), halves(jnp.concatenate(extended, axis=1)))
        out_ref[0, low:high] = full[:width, :width] - full[width:, width:]
        out_ref[1, low:high] = full[:width, width:] + full[width:, :width]


def around(axis_sizes, sign):
    rcv, freq = axis_sizes
    pairs = []
    for at in range(rcv):
        for slot in range(freq):
            target = at + (sign if slot % 2 == 0 else -sign)
            to_slot = slot
            if not 0 <= target < rcv:
                target, to_slot = at, slot ^ 1
            pairs.append((at * freq + slot, target * freq + to_slot))
    return pairs


def body(wavefield, op_table, vel_index, interp_index, interp_weight, freq_perm):
    rows, width = wavefield.shape[2], wavefield.shape[3]
    n_src, n_rcv, n_freq = (lax.axis_size(axis) for axis in ("src", "rcv", "freq"))
    lateral = width * n_rcv
    taps = op_table.shape[2]
    rim = SUBSTEPS * (taps // 2)
    edge = -(-(rim + 1) // 8) * 8
    half = width // 2
    chunks = rows // width
    wave = wavefield.reshape(2, rows, width)

    vmem = pl.BlockSpec(memory_space=pltpu.VMEM)
    smem = pl.BlockSpec(memory_space=pltpu.SMEM)
    params = pltpu.CompilerParams(vmem_limit_bytes=VMEM_LIMIT)
    tables = (vel_index, interp_index, interp_weight, freq_perm, op_table)
    scratch = [
        pltpu.VMEM((2, op_table.shape[1], width), F32),
        pltpu.VMEM((2, 2 * width, 2 * width), F32),
    ]
    cost = pl.CostEstimate(flops=6 * 2**28, bytes_accessed=2**20, transcendentals=0)

    top, bottom = wave[:, : rows // 2], wave[:, rows // 2 :]
    lower = jnp.concatenate([top[:, :, :half], bottom[:, :, :half]], axis=2)
    upper = jnp.concatenate([bottom[:, :, half:], top[:, :, half:]], axis=2)
    odd = lax.axis_index("freq") % 2 == 1
    backward = jnp.where(odd, upper, lower)
    forward = jnp.where(odd, lower, upper)
    second = lax.ppermute(backward, ("rcv", "freq"), around((n_rcv, n_freq), -1))
    first = lax.ppermute(forward, ("rcv", "freq"), around((n_rcv, n_freq), 1))

    square = (2 * width, 2 * width)
    rcv_full, rcv_high, rcv_low = pl.pallas_call(
        functools.partial(rcv_operator_kernel, lateral),
        out_shape=[
            jax.ShapeDtypeStruct(square, F32),
            jax.ShapeDtypeStruct(square, BF16),
            jax.ShapeDtypeStruct(square, BF16),
        ],
        in_specs=[smem] * 4 + [vmem],
        out_specs=[vmem] * 3,
        scratch_shapes=scratch,
        compiler_params=params,
        cost_estimate=cost,
        name="rcv_operator",
    )(*tables)
    field, head, tail, image = pl.pallas_call(
        functools.partial(receiver_kernel, rim),
        out_shape=[
            jax.ShapeDtypeStruct((2, rows, width), F32),
            jax.ShapeDtypeStruct((2, edge, width), F32),
            jax.ShapeDtypeStruct((2, edge, width), F32),
            jax.ShapeDtypeStruct((1, width), F32),
        ],
        in_specs=[vmem] * 6,
        out_specs=[vmem] * 4,
        compiler_params=params,
        name="receivers",
    )(wave, first, second, rcv_full, rcv_high, rcv_low)

    def from_src(value, distance):
        return lax.ppermute(value, "src", [(i, (i + distance) % n_src) for i in range(n_src)])

    before = from_src(tail, 1)
    after = from_src(head, -1)
    if n_src >= 3:
        parts = [image, before[0, :1], after[0, edge - 1 :]]
        parts += [from_src(image, distance) for distance in range(2, n_src - 1)]
        image = functools.reduce(jnp.add, parts)
    else:
        image = lax.psum(image, "src")
    src_high, src_low = pl.pallas_call(
        functools.partial(src_operator_kernel, lateral),
        out_shape=[jax.ShapeDtypeStruct((chunks,) + square, BF16)] * 2,
        in_specs=[smem] * 4 + [vmem],
        out_specs=[vmem] * 2,
        scratch_shapes=scratch,
        compiler_params=params,
        cost_estimate=cost,
        name="src_operator",
    )(*tables)
    if n_freq == 2:
        image = image + lax.ppermute(image, "freq", [(0, 1), (1, 0)])
    else:
        image = lax.psum(image, "freq")
    sunk = pl.pallas_call(
        source_kernel,
        out_shape=jax.ShapeDtypeStruct((2, rows, width), F32),
        in_specs=[vmem] * 5,
        out_specs=vmem,
        compiler_params=params,
        name="sources",
    )(field, before, after, src_high, src_low)
    return sunk.reshape(wavefield.shape), image.reshape(width)


def solution(mesh):
    in_specs = (P(None, "freq", "src", "rcv"), P(), P(), P(), P(), P("freq"))
    out_specs = (P(None, "freq", "src", "rcv"), P("rcv"))
    return jax.shard_map(body, mesh=mesh, in_specs=in_specs, out_specs=out_specs, check_vma=False)
```

time: 93.7 us -> 20.5 us (0.22)
  other arithmetic: 23.3 us -> 0.62 us
  starting transfers between devices: 25.3 us -> 7.61 us
  waiting for transfers between devices: 18.3 us -> 2.03 us
  blocking collectives: 12.3 us -> 0 us
  Pallas kernels: 0 us -> 6.07 us
  loops' own time: 5.27 us -> 0 us
  local copies, waits for them, and re-layouts: 6.28 us -> 2.48 us
    add x154 -> x1, other arithmetic: 21.3 us -> 0.01 us  [body(): image = functools.reduce(jnp.add, parts)]
    ppermute x10 -> x6, starting transfers between devices: 25.3 us -> 7.61 us  [the longest x3 4.5 us: from_src(): lax.ppermute(value, 'src', [(i, (i + distance) % n_src) for i in range(n_...]
    ppermute x10 -> x6, waiting for transfers between devices: 18.3 us -> 2.03 us  [the longest x3 2.02 us: from_src(): lax.ppermute(value, 'src', [(i, (i + distance) % n_src) for i in range(n_...]
    psum x1 -> x0, blocking collectives: 12.3 us -> none  [body(): zero_image = lax.psum(local_image, ('src', 'freq'))]
    pallas_call x0 -> x4, Pallas kernels: none -> 6.07 us  [the longest x1 2.46 us: body(): pl.pallas_call(functools.partial(rcv_operator_kernel, lateral), out_shape...]
    another operation x8 -> x0, loops' own time: 5.27 us -> none  [convolve(): lax.fori_loop(0, coefficients.shape[2], add_tap, (zeros_init, zeros_init))]
    gather x1 -> x0, local copies, waits for them, and re-layouts: 1.25 us -> none  [body(): diagonal_sum = jnp.sum(jnp.diagonal(diag_block, axis1=1, axis2=2), axis=0)]
    mul x95 -> x0, local copies, waits for them, and re-layouts: 1.2 us -> none  [add_tap(): real_sum = totals[0] + (coef_real * window[0] - coef_imag * window[1])]
  transfers between devices with their start and end apart: 10 -> 6, of which waited for: 8 -> 1; matrix products, arithmetic and copies ran while one was open for 2% -> 1% of each run, Pallas kernels for 0% -> 28%
where the time goes in v1:
time: 20.5 us; the launch traced here: 20.2 us
  starting transfers between devices  7.61 us (37%)
  Pallas kernels  6.07 us (30%)
  local copies, waits for them, and re-layouts  2.48 us (12%)
  waiting for transfers between devices  2.03 us (10%)
  between operations  1.41 us (7%)
  other arithmetic  0.62 us (3%)
    ppermute x3, starting transfers between devices, from_src(): lax.ppermute(value, 'src', [(i, (i + distance) % n_src) for i in range(n_...  4.5 us
    ppermute x1, starting transfers between devices, body(): first = lax.ppermute(forward, ('rcv', 'freq'), around((n_rcv, n_freq), 1))  3.04 us
    pallas_call x1, Pallas kernels, body(): pl.pallas_call(functools.partial(rcv_operator_kernel, lateral), out_shape...  2.46 us
    pallas_call x1, Pallas kernels, body(): pl.pallas_call(functools.partial(src_operator_kernel, lateral), out_shape...  2.36 us
    ppermute x3, waiting for transfers between devices, from_src(): lax.ppermute(value, 'src', [(i, (i + distance) % n_src) for i in range(n_...  2.02 us
    unnamed x13, local copies, waits for them, and re-layouts  1.45 us
    slice x1, local copies, waits for them, and re-layouts, body(): lower = jnp.concatenate([top[:, :, :half], bottom[:, :, :half]], axis=2)  1.04 us
    pallas_call x1, Pallas kernels, body(): pl.pallas_call(source_kernel, out_shape=jax.ShapeDtypeStruct((2, rows, wi...  0.93 us
  transfers between devices with their start and end apart: 6, of which 1 were waited for; matrix products, arithmetic and copies ran while one was open for 1% of the time, Pallas kernels for 28%

profile of v1, /device:TPU:0, one launch (start us, length us, event | category | flops | bytes accessed | tf_op | source)
XLA Modules:
  0.0 20.2 jit_solution(10160046621521900585)
XLA Ops:
  0.6 1.0 %fusion.3 = (f32[2,64,64]{2,1,0:T(8,128)S(1)}, f32[2,64,64]{2,1,0:T(8,128)S(1)}, f32[2,64,64]{2,1,0:T(8,128)S(1)}, f32[2,64,64]{2,1,0:T(8,128)S(1)}) fusion(f32[2,128,128]{2,1,0:T(8,128)} %bitcast.18), kind=kLoop, calls=%fused_computation.10 | loop fusion | bytes 262144 | tf_op jit(solution)/shard_map/slice | solution.py:202
  1.7 0.0 copy-start.2
  1.7 0.1 broadcast_select_fusion
  1.8 3.0 %collective-permute-start = (f32[2,64,128]{2,1,0:T(8,128)S(1)}, f32[2,64,128]{2,1,0:T(8,128)S(1)}, u32[]{:S(2)}, u32[]{:S(2)}) collective-permute-start(f32[2,64,128]{2,1,0:T(8,128)S(1)} %get-tuple-element.23), channel_id=1, source_target_pairs={{0,2},{1,0},{2,4},{3,1},{4,6},{5,3},{6,7},{7,5},{8,10},{9,8},{10,1... | collective-permute-start | bytes 196616 | tf_op jit(solution)/shard_map/ppermute | solution.py:208
  4.8 0.0 copy-start.3
  4.8 0.0 collective-permute-start.1
  4.9 0.0 copy-done.2
  4.9 0.1 copy.10.table_ref
  5.0 0.6 %copy-done.3 = s32[16,2]{0,1:T(2,128)S(1)} copy-done((s32[16,2]{0,1:T(2,128)S(1)}, s32[16,2]{0,1:T(2,128)}, u32[]{:S(2)}) %copy-start.3) | copy-done | bytes 152
  5.5 0.0 copy-start.4
  5.5 0.1 copy.8.index_ref
  5.6 0.6 %copy-done.4 = f32[16,2]{0,1:T(2,128)S(1)} copy-done((f32[16,2]{0,1:T(2,128)S(1)}, f32[16,2]{0,1:T(2,128)}, u32[]{:S(2)}) %copy-start.4) | copy-done | bytes 152
  6.2 0.1 copy.9.weight_ref
  6.3 0.0 copy-start.1
  7.0 0.0 copy-done.1
  7.0 0.0 copy-start
  7.0 2.5 %rcv_operator.1 = (f32[256,256]{1,0:T(8,128)S(1)}, bf16[256,256]{1,0:T(8,128)(2,1)S(1)}, bf16[256,256]{1,0:T(8,128)(2,1)S(1)}) custom-call(s32[32]{0:T(128)S(1)} %copy-done.1, s32[16,2]{1,0:T(8,128)S(1)} %copy.8.index_ref, f32[16,2]{1,0:T(8,128)S(1)} %copy.9.weight_ref, s32[1]{0:T(128)S(6)} %copy.15.perm_ref, f32[2,64,19]{2,1,0:T(8,128)S(1)} %copy.10.table_ref), custom_call_target="tpu_custom_call" | custom-call | flops 1610612736 | bytes 1048576 | tf_op jit(solution)/shard_map/rcv_operator/pallas_call | solution.py:211
  9.4 0.0 collective-permute-done.first_ref
  9.5 0.0 collective-permute-done.1.second_ref
  9.5 0.0 copy-done
  9.5 0.3 %receivers.1 = (f32[2,128,128]{2,1,0:T(8,128)S(1)}, f32[2,40,128]{2,1,0:T(8,128)S(1)}, f32[2,40,128]{2,1,0:T(8,128)S(1)}, f32[1,128]{1,0:T(1,128)S(1)}) custom-call(f32[2,128,128]{2,1,0:T(8,128)S(1)} %bitcast.19, f32[2,64,128]{2,1,0:T(8,128)S(1)} %collective-permute-done.first_ref, f32[2,64,128]{2,1,0:T(8,128)S(1)} %collective-permute-done.1.second_ref, ...), custom_call_target="tpu_custom_call" | custom-call | tf_op jit(solution)/shard_map/receivers/pallas_call | solution.py:225
  9.8 1.5 %collective-permute-start.2 = (f32[2,40,128]{2,1,0:T(8,128)S(1)}, f32[2,40,128]{2,1,0:T(8,128)S(1)}, u32[]{:S(2)}, u32[]{:S(2)}) collective-permute-start(f32[2,40,128]{2,1,0:T(8,128)S(1)} %get-tuple-element.15), channel_id=1, source_target_pairs={{0,8},{8,16},{16,24},{24,0},{1,9},{9,17},{17,25},{25,1},{2,10},{10... | collective-permute-start | bytes 122888 | tf_op jit(solution)/shard_map/ppermute | solution.py:240
  11.3 1.4 %collective-permute-start.3 = (f32[2,40,128]{2,1,0:T(8,128)S(1)}, f32[2,40,128]{2,1,0:T(8,128)S(1)}, u32[]{:S(2)}, u32[]{:S(2)}) collective-permute-start(f32[2,40,128]{2,1,0:T(8,128)S(1)} %get-tuple-element.16), channel_id=1, source_target_pairs={{0,24},{8,0},{16,8},{24,16},{1,25},{9,1},{17,9},{25,17},{2,26},{10... | collective-permute-start | bytes 122888 | tf_op jit(solution)/shard_map/ppermute | solution.py:240
  12.8 1.5 %collective-permute-start.4 = (f32[1,128]{1,0:T(1,128)S(1)}, f32[1,128]{1,0:T(1,128)S(1)}, u32[]{:S(2)}, u32[]{:S(2)}) collective-permute-start(f32[1,128]{1,0:T(1,128)S(1)} %get-tuple-element.19), channel_id=1, source_target_pairs={{0,16},{8,24},{16,0},{24,8},{1,17},{9,25},{17,1},{25,9},{2,18},{10... | collective-permute-start | bytes 1544 | tf_op jit(solution)/shard_map/ppermute | solution.py:240
  14.3 2.0 %collective-permute-done.4 = f32[1,128]{1,0:T(1,128)S(1)} collective-permute-done((f32[1,128]{1,0:T(1,128)S(1)}, f32[1,128]{1,0:T(1,128)S(1)}, u32[]{:S(2)}, u32[]{:S(2)}) %collective-permute-start.4) | collective-permute-done | bytes 544 | tf_op jit(solution)/shard_map/ppermute | solution.py:240
  16.3 0.0 collective-permute-done.2.before_ref
  16.3 0.0 collective-permute-done.3.after_ref
  16.3 0.1 collective-permute-start.5
  16.4 2.4 %src_operator.1 = (bf16[1,256,256]{2,1,0:T(8,128)(2,1)S(1)}, bf16[1,256,256]{2,1,0:T(8,128)(2,1)S(1)}) custom-call(s32[32]{0:T(128)S(1)} %copy-done.1, s32[16,2]{1,0:T(8,128)S(1)} %copy.8.index_ref, f32[16,2]{1,0:T(8,128)S(1)} %copy.9.weight_ref, s32[1]{0:T(128)S(6)} %copy.15.perm_ref, f32[2,64,19]{2,1,0:T(8,128)S(1)} %copy.10.table_ref), custom_call_target="tpu_custom_call" | custom-call | flops 1610612736 | bytes 1048576 | tf_op jit(solution)/shard_map/src_operator/pallas_call | solution.py:250
  18.8 0.9 %sources.1 = f32[2,128,128]{2,1,0:T(8,128)} custom-call(f32[2,128,128]{2,1,0:T(8,128)S(1)} %get-tuple-element.14.field_ref, f32[2,40,128]{2,1,0:T(8,128)S(1)} %collective-permute-done.2.before_ref, f32[2,40,128]{2,1,0:T(8,128)S(1)} %collective-permute-done.3.after_ref, bf16[1,256,256]{2,1,0:T(8,128)(2,1)S(1)} %get-tuple-element.17.high_ref, ...), custom_call_target="tpu_custom_call" | custom-call | tf_op jit(solution)/shard_map/sources/pallas_call | solution.py:264
  19.7 0.0 collective-permute-done.5
  19.7 0.5 %add_bitcast_fusion = f32[128]{0:T(128)} fusion(f32[1,128]{1,0:T(1,128)S(1)} %fusion.1, f32[1,128]{1,0:T(1,128)S(1)} %collective-permute-done.5), kind=kLoop, calls=%fused_computation.9 | loop fusion | flops 128 | bytes 1536 | tf_op jit(solution)/shard_map/reshape | solution.py:272
  (1 shorter events, 0.0 us)
Async XLA Ops:
  1.7 3.2 %copy-start.2 = (f32[2,64,19]{1,0,2:T(2,128)S(1)}, f32[2,64,19]{1,0,2:T(2,128)}, u32[]{:S(2)}) copy-start(f32[2,64,19]{1,0,2:T(2,128)} %param.7) | copy-start | bytes 29188
  1.8 7.6 %collective-permute-start = (f32[2,64,128]{2,1,0:T(8,128)S(1)}, f32[2,64,128]{2,1,0:T(8,128)S(1)}, u32[]{:S(2)}, u32[]{:S(2)}) collective-permute-start(f32[2,64,128]{2,1,0:T(8,128)S(1)} %get-tuple-element.23), channel_id=1, source_target_pairs={{0,2},{1,0},{2,4},{3,1},{4,6},{5,3},{6,7},{7,5},{8,10},{9,8},{10,1... | collective-permute-start | bytes 196616 | tf_op jit(solution)/shard_map/ppermute | solution.py:208
  4.8 0.7 %copy-start.3 = (s32[16,2]{0,1:T(2,128)S(1)}, s32[16,2]{0,1:T(2,128)}, u32[]{:S(2)}) copy-start(s32[16,2]{0,1:T(2,128)} %param.9) | copy-start | bytes 388
  4.8 4.6 %collective-permute-start.1 = (f32[2,64,128]{2,1,0:T(8,128)S(1)}, f32[2,64,128]{2,1,0:T(8,128)S(1)}, u32[]{:S(2)}, u32[]{:S(2)}) collective-permute-start(f32[2,64,128]{2,1,0:T(8,128)S(1)} %get-tuple-element.22), channel_id=1, source_target_pairs={{0,1},{1,3},{2,0},{3,5},{4,2},{5,7},{6,4},{7,6},{8,9},{9,11},{10,8... | collective-permute-start | bytes 196616 | tf_op jit(solution)/shard_map/ppermute | solution.py:207
  5.5 0.7 %copy-start.4 = (f32[16,2]{0,1:T(2,128)S(1)}, f32[16,2]{0,1:T(2,128)}, u32[]{:S(2)}) copy-start(f32[16,2]{0,1:T(2,128)} %param.10) | copy-start | bytes 388
  6.3 0.7 %copy-start.1 = (s32[32]{0:T(128)S(1)}, s32[32]{0:T(128)}, u32[]{:S(2)}) copy-start(s32[32]{0:T(128)} %vel_ref.3) | copy-start | bytes 388
  7.0 2.5 %copy-start = (f32[2,1,128,128]{3,2,1,0:T(8,128)S(1)}, f32[2,1,128,128]{3,2,1,0:T(8,128)}, u32[]{:S(2)}) copy-start(f32[2,1,128,128]{3,2,1,0:T(8,128)} %param.6) | copy-start | bytes 393220
  9.8 6.5 %collective-permute-start.2 = (f32[2,40,128]{2,1,0:T(8,128)S(1)}, f32[2,40,128]{2,1,0:T(8,128)S(1)}, u32[]{:S(2)}, u32[]{:S(2)}) collective-permute-start(f32[2,40,128]{2,1,0:T(8,128)S(1)} %get-tuple-element.15), channel_id=1, source_target_pairs={{0,8},{8,16},{16,24},{24,0},{1,9},{9,17},{17,25},{25,1},{2,10},{10... | collective-permute-start | bytes 122888 | tf_op jit(solution)/shard_map/ppermute | solution.py:240
  11.3 5.0 %collective-permute-start.3 = (f32[2,40,128]{2,1,0:T(8,128)S(1)}, f32[2,40,128]{2,1,0:T(8,128)S(1)}, u32[]{:S(2)}, u32[]{:S(2)}) collective-permute-start(f32[2,40,128]{2,1,0:T(8,128)S(1)} %get-tuple-element.16), channel_id=1, source_target_pairs={{0,24},{8,0},{16,8},{24,16},{1,25},{9,1},{17,9},{25,17},{2,26},{10... | collective-permute-start | bytes 122888 | tf_op jit(solution)/shard_map/ppermute | solution.py:240
  12.8 3.5 %collective-permute-start.4 = (f32[1,128]{1,0:T(1,128)S(1)}, f32[1,128]{1,0:T(1,128)S(1)}, u32[]{:S(2)}, u32[]{:S(2)}) collective-permute-start(f32[1,128]{1,0:T(1,128)S(1)} %get-tuple-element.19), channel_id=1, source_target_pairs={{0,16},{8,24},{16,0},{24,8},{1,17},{9,25},{17,1},{25,9},{2,18},{10... | collective-permute-start | bytes 1544 | tf_op jit(solution)/shard_map/ppermute | solution.py:240
  16.3 3.4 %collective-permute-start.5 = (f32[1,128]{1,0:T(1,128)S(1)}, f32[1,128]{1,0:T(1,128)S(1)}, u32[]{:S(2)}, u32[]{:S(2)}) collective-permute-start(f32[1,128]{1,0:T(1,128)S(1)} %fusion.1), channel_id=1, source_target_pairs={{0,1},{1,0},{2,3},{3,2},{4,5},{5,4},{6,7},{7,6},{8,9},{9,8},{10,11... | collective-permute-start | bytes 1544 | tf_op jit(solution)/shard_map/ppermute | solution.py:261

commit v2 on v1

v2 whole, which is shorter than its diff:
```python
import functools

import jax
import jax.numpy as jnp
from jax import lax
from jax.experimental import pallas as pl
from jax.experimental.pallas import tpu as pltpu
from jax.sharding import PartitionSpec as P

SUBSTEPS = 4
TILE = 16
VMEM_LIMIT = 32 * 1024 * 1024
F32 = jnp.float32
BF16 = jnp.bfloat16


def halves(value):
    high = value.astype(BF16)
    low = (value - high.astype(F32)).astype(BF16)
    return high, low


def dot(left, right):
    return jnp.dot(left, right, preferred_element_type=F32)


def dot3(left, right):
    left_high, left_low = left
    right_high, right_low = right
    return dot(left_high, right_high) + (dot(left_high, right_low) + dot(left_low, right_high))


def square_product(left, right):
    rows, cols = left[0].shape[0], right[0].shape[1]
    stacked = halves(jnp.concatenate(left, axis=0))
    beside = halves(jnp.concatenate(right, axis=1))
    full = dot3(stacked, beside)
    real = full[:rows, :cols] - full[rows:, cols:]
    imag = full[:rows, cols:] + full[rows:, :cols]
    return real, imag


def tile_taps(starts, window, vel_ref, index_ref, weight_ref, perm_ref, table_ref, table):
    count = window // TILE
    tiles, slots = vel_ref.shape[1], index_ref.shape[0]
    velocities, entries, taps = index_ref.shape[1], table_ref.shape[2], table_ref.shape[0]
    place = lax.broadcasted_iota(jnp.int32, (count, tiles), 0)
    place = place - jnp.where(place >= count - count // 4, count, 0)
    tile = jnp.concatenate([start // TILE + place for start in starts], axis=0)
    lane = lax.broadcasted_iota(jnp.int32, tile.shape, 1)
    velocity = jnp.sum(jnp.where(lane == tile, vel_ref[...].astype(F32), 0.0), axis=1, keepdims=True)
    inside = jnp.sum(jnp.where(lane == tile, 1.0, 0.0), axis=1, keepdims=True)
    chosen = lax.broadcasted_iota(jnp.int32, (slots, velocities), 0) == perm_ref[...]
    index = jnp.sum(jnp.where(chosen, index_ref[...].astype(F32), 0.0), axis=0, keepdims=True)
    weight = jnp.sum(jnp.where(chosen, weight_ref[...], 0.0), axis=0, keepdims=True)
    rows = tile.shape[0]
    hit = lax.broadcasted_iota(jnp.int32, (rows, velocities), 1).astype(F32) == velocity
    index = jnp.sum(jnp.where(hit, index, 0.0), axis=1, keepdims=True)
    weight = jnp.sum(jnp.where(hit, weight, 0.0), axis=1, keepdims=True)
    entry = lax.broadcasted_iota(jnp.int32, (rows, entries), 1).astype(F32)
    mix = jnp.where(entry == index, 1.0 - weight, 0.0) + jnp.where(entry == index + 1.0, weight, 0.0)
    mix = mix * inside
    table[...] = jnp.zeros_like(table)
    found = []
    for part in range(2):
        table[part, :taps, :] = table_ref[:, part, :]
        found.append(
            lax.dot_general(
                mix, table[part], (((1,), (1,)), ((), ())), precision=lax.Precision.HIGHEST, preferred_element_type=F32
            )
        )
    return found


def fill_band(found, first, taps, band):
    window = band.shape[1]
    for position in range(window // TILE):
        shift = (position * TILE - taps // 2) % window
        for part in range(2):
            row = found[part][first + position : first + position + 1]
            spread = jnp.broadcast_to(row, (TILE, row.shape[1]))
            slanted = pltpu.roll(spread, 0, 1, stride=1, stride_axis=0)
            wide = jnp.concatenate([slanted, jnp.zeros((TILE, window - slanted.shape[1]), F32)], axis=1)
            band[part, pl.ds(position * TILE, TILE), :] = pltpu.roll(wide, shift, 1)


def four_substeps(start, lateral, once):
    window = once[0].shape[0]
    width = window // 2
    twice = square_product(once, once)
    four = square_product((twice[0][:width], twice[1][:width]), twice)
    place = lax.broadcasted_iota(jnp.int32, (width, window), 1)
    cell = start + jnp.where(place < window - width // 2, place, place - window)
    inside = jnp.logical_and(cell >= 0, cell < lateral)
    return jnp.where(inside, four[0], 0.0), jnp.where(inside, four[1], 0.0)


def pack_kernel(wave_ref, one_ref, two_ref):
    rows, width = wave_ref.shape[1], wave_ref.shape[2]
    half = width // 2
    odd = lax.axis_index("freq") % 2 == 1
    lane = lax.broadcasted_iota(jnp.int32, (rows // 2, width), 1)
    own = jnp.logical_xor(lane < half, odd)
    for part in range(2):
        top = wave_ref[part, : rows // 2]
        bottom = pltpu.roll(wave_ref[part, rows // 2 :], half, 1)
        one_ref[part] = jnp.where(own, top, bottom)
        two_ref[part] = jnp.where(own, bottom, top)


def rcv_operator_kernel(
    lateral, vel_ref, index_ref, weight_ref, perm_ref, table_ref, full_ref, high_ref, low_ref, src_ref, table, band
):
    width = full_ref.shape[1] // 2
    taps, window = table_ref.shape[0], 2 * width
    chunks = src_ref.shape[0]
    starts = [lax.axis_index("rcv") * width]
    starts += [(lax.axis_index("src") * chunks + chunk) * width for chunk in range(chunks)]
    found = tile_taps(starts, window, vel_ref, index_ref, weight_ref, perm_ref, table_ref, table)
    fill_band(found, 0, taps, band)
    for chunk in range(chunks):
        fill_band(found, (chunk + 1) * window // TILE, taps, src_ref.at[chunk])
    real, imag = four_substeps(starts[0], lateral, (band[0], band[1]))
    turned = jnp.concatenate([real.T, imag.T], axis=1)
    full_ref[...] = turned
    high_ref[...], low_ref[...] = halves(turned)


def src_operator_kernel(lateral, band_ref, high_ref, low_ref):
    chunks, width = high_ref.shape[0], high_ref.shape[2] // 2
    for chunk in range(chunks):
        start = (lax.axis_index("src") * chunks + chunk) * width
        real, imag = four_substeps(start, lateral, (band_ref[chunk, 0], band_ref[chunk, 1]))
        high_ref[chunk], low_ref[chunk] = halves(jnp.concatenate([real, imag], axis=0))


def receiver_kernel(wave_ref, first_ref, second_ref, full_ref, high_ref, low_ref, sunk_ref, one_ref, two_ref, image_ref):
    rows, width = wave_ref.shape[1], wave_ref.shape[2]
    half = width // 2
    odd = lax.axis_index("freq") % 2 == 1
    lane = lax.broadcasted_iota(jnp.int32, (rows // 2, width), 1)
    extended = []
    for part in range(2):
        first, second = first_ref[part], second_ref[part]
        before = jnp.where(odd, first, second)
        after = jnp.where(odd, second, first)
        top = jnp.where(lane < half, after, before)
        bottom = pltpu.roll(jnp.where(lane < half, before, after), half, 1)
        halo = jnp.concatenate([top, bottom], axis=0)
        extended.append(jnp.concatenate([wave_ref[part], halo], axis=1))
    full = dot3(halves(jnp.concatenate(extended, axis=0)), (high_ref[...], low_ref[...]))
    real = full[:rows, :width] - full[rows:, width:]
    imag = full[:rows, width:] + full[rows:, :width]
    sunk_ref[0] = real
    sunk_ref[1] = imag
    chunks = rows // width
    ahead = lax.axis_index("src") * chunks - lax.axis_index("rcv")
    line = lax.broadcasted_iota(jnp.int32, (width, 2 * width), 0)
    image = jnp.zeros((1, width), F32)
    for chunk in range(chunks):
        away = ahead + chunk
        beside = jnp.logical_or(
            jnp.logical_and(away == 1, line < half), jnp.logical_and(away == -1, line >= half)
        )
        weights = jnp.where(away == 0, full_ref[:width], jnp.where(beside, full_ref[width:], 0.0))
        piece = slice(chunk * width, (chunk + 1) * width)
        terms = weights[:, :width] * real[piece] - weights[:, width:] * imag[piece]
        image = image + jnp.sum(terms, axis=0, keepdims=True)
    image_ref[...] = image
    edge = one_ref.shape[1]
    row = lax.broadcasted_iota(jnp.int32, (edge, width), 0)
    head = (jnp.where(row == edge - 1, image, real[:edge]), imag[:edge])
    tail = (jnp.where(row == 0, image, real[rows - edge :]), imag[rows - edge :])
    up = lax.axis_index("src") % 2 == 0
    for part in range(2):
        one_ref[part] = jnp.where(up, tail[part], head[part])
        two_ref[part] = jnp.where(up, head[part], tail[part])


def source_kernel(field_ref, one_ref, two_ref, high_ref, low_ref, out_ref):
    rows, width = field_ref.shape[1], field_ref.shape[2]
    half = width // 2
    chunks = rows // width
    edge = one_ref.shape[1]
    up = lax.axis_index("src") % 2 == 0
    gap = jnp.zeros((half - edge, width), F32)
    for chunk in range(chunks):
        low, high = chunk * width, (chunk + 1) * width
        extended = []
        for part in range(2):
            if chunk + 1 < chunks:
                after = field_ref[part, high : high + half]
            else:
                after = jnp.concatenate([jnp.where(up, one_ref[part], two_ref[part]), gap], axis=0)
            if chunk > 0:
                before = field_ref[part, low - half : low]
            else:
                before = jnp.concatenate([gap, jnp.where(up, two_ref[part], one_ref[part])], axis=0)
            extended.append(jnp.concatenate([field_ref[part, low:high], after, before], axis=0))
        full = dot3((high_ref[chunk], low_ref[chunk]), halves(jnp.concatenate(extended, axis=1)))
        out_ref[0, low:high] = full[:width, :width] - full[width:, width:]
        out_ref[1, low:high] = full[:width, width:] + full[width:, :width]


def around(rcv, freq, sign):
    pairs = []
    for at in range(rcv):
        for slot in range(freq):
            target = at + (sign if slot % 2 == 0 else -sign)
            to_slot = slot
            if not 0 <= target < rcv:
                target, to_slot = at, slot ^ 1
            pairs.append((at * freq + slot, target * freq + to_slot))
    return pairs


def body(wavefield, op_table, vel_index, interp_index, interp_weight, freq_perm):
    rows, width = wavefield.shape[2], wavefield.shape[3]
    n_src, n_rcv, n_freq = (lax.axis_size(axis) for axis in ("src", "rcv", "freq"))
    lateral = width * n_rcv
    rim = SUBSTEPS * (op_table.shape[2] // 2)
    edge = -(-(rim + 1) // 8) * 8
    half = width // 2
    chunks = rows // width
    wave = wavefield.reshape(2, rows, width)

    vmem = pl.BlockSpec(memory_space=pltpu.VMEM)
    anywhere = pl.BlockSpec(memory_space=pltpu.HBM)
    params = pltpu.CompilerParams(vmem_limit_bytes=VMEM_LIMIT)
    cost = pl.CostEstimate(flops=6 * 2**28, bytes_accessed=2**20, transcendentals=0)

    tables = [
        vel_index.reshape(1, -1),
        interp_index.T,
        interp_weight.T,
        freq_perm.reshape(1, 1),
        op_table.transpose(2, 0, 1),
    ]
    packed = jax.ShapeDtypeStruct((2, rows // 2, width), F32)
    first, second = pl.pallas_call(
        pack_kernel,
        out_shape=[packed, packed],
        in_specs=[pl.BlockSpec(wave.shape, lambda: (0, 0, 0))],
        out_specs=[vmem] * 2,
        compiler_params=params,
        name="pack",
    )(wave)
    first = lax.ppermute(first, ("rcv", "freq"), around(n_rcv, n_freq, -1))
    second = lax.ppermute(second, ("rcv", "freq"), around(n_rcv, n_freq, 1))

    square = (2 * width, 2 * width)
    rcv_full, rcv_high, rcv_low, src_band = pl.pallas_call(
        functools.partial(rcv_operator_kernel, lateral),
        out_shape=[
            jax.ShapeDtypeStruct(square, F32),
            jax.ShapeDtypeStruct(square, BF16),
            jax.ShapeDtypeStruct(square, BF16),
            jax.ShapeDtypeStruct((chunks, 2) + square, F32),
        ],
        in_specs=[pl.BlockSpec(a.shape, lambda n=len(a.shape): (0,) * n) for a in tables],
        out_specs=[vmem] * 4,
        scratch_shapes=[pltpu.VMEM((2, width, op_table.shape[1]), F32), pltpu.VMEM((2,) + square, F32)],
        compiler_params=params,
        cost_estimate=cost,
        name="rcv_operator",
    )(*tables)
    field, one, two, image = pl.pallas_call(
        receiver_kernel,
        out_shape=[
            jax.ShapeDtypeStruct((2, rows, width), F32),
            jax.ShapeDtypeStruct((2, edge, width), F32),
            jax.ShapeDtypeStruct((2, edge, width), F32),
            jax.ShapeDtypeStruct((1, width), F32),
        ],
        in_specs=[vmem] * 6,
        out_specs=[vmem] * 4,
        compiler_params=params,
        name="receivers",
    )(wave, first, second, rcv_full, rcv_high, rcv_low)

    two = lax.ppermute(two, "src", [(i, (i - 1 if i % 2 == 0 else i + 1) % n_src) for i in range(n_src)])
    one = lax.ppermute(one, "src", [(i, i + 1 if i % 2 == 0 else i - 1) for i in range(n_src)])
    if n_src == 4:
        far = lax.ppermute(image, "src", [(i, i ^ 2) for i in range(n_src)])
    src_high, src_low = pl.pallas_call(
        functools.partial(src_operator_kernel, lateral),
        out_shape=[jax.ShapeDtypeStruct((chunks,) + square, BF16)] * 2,
        in_specs=[vmem],
        out_specs=[vmem] * 2,
        compiler_params=params,
        cost_estimate=pl.CostEstimate(flops=2**20, bytes_accessed=2**10, transcendentals=0),
        name="src_operator",
    )(src_band)
    if n_src == 4:
        up = lax.axis_index("src") % 2 == 0
        from_one = jnp.where(up, one[0, edge - 1 :], one[0, :1])
        from_two = jnp.where(up, two[0, :1], two[0, edge - 1 :])
        image = (image + from_one) + (from_two + far)
    else:
        image = lax.psum(image, "src")
    image, src_high = lax.optimization_barrier((image, src_high))
    if n_freq == 2:
        image = image + lax.ppermute(image, "freq", [(0, 1), (1, 0)])
    else:
        image = lax.psum(image, "freq")
    sunk = pl.pallas_call(
        source_kernel,
        out_shape=jax.ShapeDtypeStruct((2, rows, width), F32),
        in_specs=[vmem] * 5,
        out_specs=vmem,
        compiler_params=params,
        name="sources",
    )(field, one, two, src_high, src_low)
    return sunk.reshape(wavefield.shape), image.reshape(width)


def solution(mesh):
    in_specs = (P(None, "freq", "src", "rcv"), P(), P(), P(), P(), P("freq"))
    out_specs = (P(None, "freq", "src", "rcv"), P("rcv"))
    return jax.shard_map(body, mesh=mesh, in_specs=in_specs, out_specs=out_specs, check_vma=False)
```

time: 20.5 us -> 17.4 us (0.85)
  Pallas kernels: 6.07 us -> 4.69 us
  starting transfers between devices: 7.61 us -> 6.69 us
  local copies, waits for them, and re-layouts: 2.48 us -> 1.57 us
  waiting for transfers between devices: 2.03 us -> 2.33 us
    pallas_call x1, Pallas kernels: 2.36 us -> 1.3 us  [body(): pl.pallas_call(functools.partial(src_operator_kernel, lateral), out_shape...]
    slice x1 -> x0, local copies, waits for them, and re-layouts: 1.04 us -> none  [body(): lower = jnp.concatenate([top[:, :, :half], bottom[:, :, :half]], axis=2)]
    ppermute x5, starting transfers between devices: 7.54 us -> 6.62 us  [the longest x1 2.6 us: body(): second = lax.ppermute(second, ('rcv', 'freq'), around(n_rcv, n_freq, 1))]
    pallas_call x1, Pallas kernels: 2.46 us -> 2.06 us  [body(): pl.pallas_call(functools.partial(rcv_operator_kernel, lateral), out_shape...]
    unnamed x13 -> x12, local copies, waits for them, and re-layouts: 1.45 us -> 1.57 us
  transfers between devices with their start and end apart: 6 -> 6, of which waited for: 1 -> 2; matrix products, arithmetic and copies ran while one was open for 1% -> 0% of each run, Pallas kernels for 28% -> 25%
where the time goes in v2:
time: 17.4 us; the launch traced here: 17.2 us
  starting transfers between devices  6.69 us (38%)
  Pallas kernels  4.69 us (27%)
  waiting for transfers between devices  2.33 us (13%)
  local copies, waits for them, and re-layouts  1.57 us (9%)
  between operations  1.39 us (8%)
  other arithmetic  0.52 us (3%)
    ppermute x1, starting transfers between devices, body(): second = lax.ppermute(second, ('rcv', 'freq'), around(n_rcv, n_freq, 1))  2.6 us
    ppermute x1, waiting for transfers between devices, body(): far = lax.ppermute(image, 'src', [(i, i ^ 2) for i in range(n_src)])  2.14 us
    pallas_call x1, Pallas kernels, body(): pl.pallas_call(functools.partial(rcv_operator_kernel, lateral), out_shape...  2.06 us
    ppermute x1, starting transfers between devices, body(): lax.ppermute(one, 'src', [(i, i + 1 if i % 2 == 0 else i - 1) for i in ra...  1.98 us
    unnamed x12, local copies, waits for them, and re-layouts  1.57 us
    ppermute x1, starting transfers between devices, body(): lax.ppermute(two, 'src', [(i, (i - 1 if i % 2 == 0 else i + 1) % n_src) f...  1.49 us
    pallas_call x1, Pallas kernels, body(): pl.pallas_call(functools.partial(src_operator_kernel, lateral), out_shape...  1.3 us
    pallas_call x1, Pallas kernels, body(): pl.pallas_call(source_kernel, out_shape=jax.ShapeDtypeStruct((2, rows, wi...  0.93 us
  transfers between devices with their start and end apart: 6, of which 2 were waited for; matrix products, arithmetic and copies ran while one was open for 0% of the time, Pallas kernels for 25%

profile of v2, /device:TPU:0, one launch (start us, length us, event | category | flops | bytes accessed | tf_op | source)
XLA Modules:
  0.0 17.2 jit_solution(16272150144545916575)
XLA Ops:
  0.6 0.0 copy-start
  0.6 0.9 %copy-done = f32[2,1,128,128]{3,2,1,0:T(8,128)S(1)} copy-done((f32[2,1,128,128]{3,2,1,0:T(8,128)S(1)}, f32[2,1,128,128]{3,2,1,0:T(8,128)}, u32[]{:S(2)}) %copy-start) | copy-done | bytes 131096
  1.5 0.0 copy-start.2
  1.5 0.1 pack.1
  1.6 0.5 %collective-permute-start = (f32[2,64,128]{2,1,0:T(8,128)S(1)}, f32[2,64,128]{2,1,0:T(8,128)S(1)}, u32[]{:S(2)}, u32[]{:S(2)}) collective-permute-start(f32[2,64,128]{2,1,0:T(8,128)S(1)} %get-tuple-element.16), channel_id=1, source_target_pairs={{0,1},{1,3},{2,0},{3,5},{4,2},{5,7},{6,4},{7,6},{8,9},{9,11},{10,8... | collective-permute-start | bytes 196616 | tf_op jit(solution)/shard_map/ppermute | solution.py:248
  2.1 2.6 %collective-permute-start.1 = (f32[2,64,128]{2,1,0:T(8,128)S(1)}, f32[2,64,128]{2,1,0:T(8,128)S(1)}, u32[]{:S(2)}, u32[]{:S(2)}) collective-permute-start(f32[2,64,128]{2,1,0:T(8,128)S(1)} %get-tuple-element.17), channel_id=1, source_target_pairs={{0,2},{1,0},{2,4},{3,1},{4,6},{5,3},{6,7},{7,5},{8,10},{9,8},{10,1... | collective-permute-start | bytes 196616 | tf_op jit(solution)/shard_map/ppermute | solution.py:249
  5.3 0.0 copy-start.4
  5.4 0.0 copy-start.3
  5.4 0.0 copy-start.5
  5.4 0.0 copy-done.2
  5.4 0.6 %copy-done.4 = f32[16,2]{0,1:T(2,128)S(1)} copy-done((f32[16,2]{0,1:T(2,128)S(1)}, f32[16,2]{0,1:T(2,128)}, u32[]{:S(2)}) %copy-start.4) | copy-done | bytes 152
  6.0 0.0 copy-done.3
  6.0 0.0 copy-done.5
  6.0 0.0 copy-start.1
  6.1 2.1 %rcv_operator.1 = (f32[256,256]{1,0:T(8,128)S(1)}, bf16[256,256]{1,0:T(8,128)(2,1)S(1)}, bf16[256,256]{1,0:T(8,128)(2,1)S(1)}, f32[1,2,256,256]{3,2,1,0:T(8,128)S(1)}) custom-call(s32[1,32]{1,0:T(1,128)S(1)} %bitcast.29, s32[2,16]{1,0:T(2,128)S(1)} %bitcast.27, f32[2,16]{1,0:T(2,128)S(1)} %bitcast.28, s32[1,1]{1,0:T(1,128)} %bitcast.23.perm_ref, ...), custom_call_target="tpu_custom_call" | custom-call | flops 1610612736 | bytes 1048576 | tf_op jit(solution)/shard_map/rcv_operator/pallas_call | solution.py:252
  8.1 0.0 collective-permute-done.first_ref
  8.1 0.0 collective-permute-done.1.second_ref
  8.1 0.0 copy-done.1
  8.2 0.3 %receivers.1 = (f32[2,128,128]{2,1,0:T(8,128)S(1)}, f32[2,40,128]{2,1,0:T(8,128)S(1)}, f32[2,40,128]{2,1,0:T(8,128)S(1)}, f32[1,128]{1,0:T(1,128)S(1)}) custom-call(f32[2,128,128]{2,1,0:T(8,128)S(1)} %bitcast.25, f32[2,64,128]{2,1,0:T(8,128)S(1)} %collective-permute-done.first_ref, f32[2,64,128]{2,1,0:T(8,128)S(1)} %collective-permute-done.1.second_ref, ...), custom_call_target="tpu_custom_call" | custom-call | tf_op jit(solution)/shard_map/receivers/pallas_call | solution.py:267
  8.5 2.0 %collective-permute-start.2 = (f32[2,40,128]{2,1,0:T(8,128)S(1)}, f32[2,40,128]{2,1,0:T(8,128)S(1)}, u32[]{:S(2)}, u32[]{:S(2)}) collective-permute-start(f32[2,40,128]{2,1,0:T(8,128)S(1)} %get-tuple-element.22), channel_id=1, source_target_pairs={{0,8},{8,0},{16,24},{24,16},{1,9},{9,1},{17,25},{25,17},{2,10},{10... | collective-permute-start | bytes 122888 | tf_op jit(solution)/shard_map/ppermute | solution.py:282
  10.5 1.5 %collective-permute-start.3 = (f32[2,40,128]{2,1,0:T(8,128)S(1)}, f32[2,40,128]{2,1,0:T(8,128)S(1)}, u32[]{:S(2)}, u32[]{:S(2)}) collective-permute-start(f32[2,40,128]{2,1,0:T(8,128)S(1)} %get-tuple-element.23), channel_id=1, source_target_pairs={{0,24},{8,16},{16,8},{24,0},{1,25},{9,17},{17,9},{25,1},{2,26},{10... | collective-permute-start | bytes 122888 | tf_op jit(solution)/shard_map/ppermute | solution.py:281
  11.9 0.1 collective-permute-start.4
  12.0 1.3 %src_operator.1 = (bf16[1,256,256]{2,1,0:T(8,128)(2,1)S(1)}, bf16[1,256,256]{2,1,0:T(8,128)(2,1)S(1)}) custom-call(f32[1,2,256,256]{3,2,1,0:T(8,128)S(1)} %get-tuple-element.25.band_ref), custom_call_target="tpu_custom_call" | custom-call | flops 1048576 | bytes 1024 | tf_op jit(solution)/shard_map/src_operator/pallas_call | solution.py:285
  13.3 2.1 %collective-permute-done.4 = f32[1,128]{1,0:T(1,128)S(1)} collective-permute-done((f32[1,128]{1,0:T(1,128)S(1)}, f32[1,128]{1,0:T(1,128)S(1)}, u32[]{:S(2)}, u32[]{:S(2)}) %collective-permute-start.4) | collective-permute-done | bytes 544 | tf_op jit(solution)/shard_map/ppermute | solution.py:284
  15.5 0.0 collective-permute-done.2.one_ref
  15.5 0.0 collective-permute-done.3.two_ref
  15.5 0.1 collective-permute-start.5
  15.6 0.9 %sources.1 = f32[2,128,128]{2,1,0:T(8,128)} custom-call(f32[2,128,128]{2,1,0:T(8,128)S(1)} %get-tuple-element.21.field_ref, f32[2,40,128]{2,1,0:T(8,128)S(1)} %collective-permute-done.2.one_ref, f32[2,40,128]{2,1,0:T(8,128)S(1)} %collective-permute-done.3.two_ref, bf16[1,256,256]{2,1,0:T(8,128)(2,1)S(1)} %get-tuple-element.27.high_ref, ...), custom_call_target="tpu_custom_call" | custom-call | tf_op jit(solution)/shard_map/sources/pallas_call | solution.py:306
  16.5 0.2 %collective-permute-done.5 = f32[1,128]{1,0:T(1,128)S(1)} collective-permute-done((f32[1,128]{1,0:T(1,128)S(1)}, f32[1,128]{1,0:T(1,128)S(1)}, u32[]{:S(2)}, u32[]{:S(2)}) %collective-permute-start.5) | collective-permute-done | bytes 544 | tf_op jit(solution)/shard_map/ppermute | solution.py:303
  16.7 0.5 %add_bitcast_fusion = f32[128]{0:T(128)} fusion(f32[1,128]{1,0:T(1,128)S(1)} %fusion.2, f32[1,128]{1,0:T(1,128)S(1)} %collective-permute-done.5), kind=kLoop, calls=%fused_computation.7 | loop fusion | flops 128 | bytes 1536 | tf_op jit(solution)/shard_map/reshape | solution.py:314
  (1 shorter events, 0.0 us)
Async XLA Ops:
  0.6 0.9 %copy-start = (f32[2,1,128,128]{3,2,1,0:T(8,128)S(1)}, f32[2,1,128,128]{3,2,1,0:T(8,128)}, u32[]{:S(2)}) copy-start(f32[2,1,128,128]{3,2,1,0:T(8,128)} %param.6) | copy-start | bytes 393220
  1.5 3.9 %copy-start.2 = (f32[2,64,19]{1,0,2:T(2,128)S(1)}, f32[2,64,19]{1,0,2:T(2,128)}, u32[]{:S(2)}) copy-start(f32[2,64,19]{1,0,2:T(2,128)} %param.7) | copy-start | bytes 29188
  1.6 6.5 %collective-permute-start = (f32[2,64,128]{2,1,0:T(8,128)S(1)}, f32[2,64,128]{2,1,0:T(8,128)S(1)}, u32[]{:S(2)}, u32[]{:S(2)}) collective-permute-start(f32[2,64,128]{2,1,0:T(8,128)S(1)} %get-tuple-element.16), channel_id=1, source_target_pairs={{0,1},{1,3},{2,0},{3,5},{4,2},{5,7},{6,4},{7,6},{8,9},{9,11},{10,8... | collective-permute-start | bytes 196616 | tf_op jit(solution)/shard_map/ppermute | solution.py:248
  2.1 6.0 %collective-permute-start.1 = (f32[2,64,128]{2,1,0:T(8,128)S(1)}, f32[2,64,128]{2,1,0:T(8,128)S(1)}, u32[]{:S(2)}, u32[]{:S(2)}) collective-permute-start(f32[2,64,128]{2,1,0:T(8,128)S(1)} %get-tuple-element.17), channel_id=1, source_target_pairs={{0,2},{1,0},{2,4},{3,1},{4,6},{5,3},{6,7},{7,5},{8,10},{9,8},{10,1... | collective-permute-start | bytes 196616 | tf_op jit(solution)/shard_map/ppermute | solution.py:249
  5.3 0.7 %copy-start.4 = (f32[16,2]{0,1:T(2,128)S(1)}, f32[16,2]{0,1:T(2,128)}, u32[]{:S(2)}) copy-start(f32[16,2]{0,1:T(2,128)} %param.10) | copy-start | bytes 388
  5.4 0.7 %copy-start.3 = (s32[16,2]{0,1:T(2,128)S(1)}, s32[16,2]{0,1:T(2,128)}, u32[]{:S(2)}) copy-start(s32[16,2]{0,1:T(2,128)} %param.9) | copy-start | bytes 388
  5.4 0.7 %copy-start.5 = (s32[32]{0:T(128)S(1)}, s32[32]{0:T(128)}, u32[]{:S(2)}) copy-start(s32[32]{0:T(128)} %param.8) | copy-start | bytes 388
  6.0 2.1 %copy-start.1 = (f32[2,1,128,128]{3,2,1,0:T(8,128)S(1)}, f32[2,1,128,128]{3,2,1,0:T(8,128)}, u32[]{:S(2)}) copy-start(f32[2,1,128,128]{3,2,1,0:T(8,128)} %param.6) | copy-start | bytes 393220
  8.5 7.0 %collective-permute-start.2 = (f32[2,40,128]{2,1,0:T(8,128)S(1)}, f32[2,40,128]{2,1,0:T(8,128)S(1)}, u32[]{:S(2)}, u32[]{:S(2)}) collective-permute-start(f32[2,40,128]{2,1,0:T(8,128)S(1)} %get-tuple-element.22), channel_id=1, source_target_pairs={{0,8},{8,0},{16,24},{24,16},{1,9},{9,1},{17,25},{25,17},{2,10},{10... | collective-permute-start | bytes 122888 | tf_op jit(solution)/shard_map/ppermute | solution.py:282
  10.5 5.0 %collective-permute-start.3 = (f32[2,40,128]{2,1,0:T(8,128)S(1)}, f32[2,40,128]{2,1,0:T(8,128)S(1)}, u32[]{:S(2)}, u32[]{:S(2)}) collective-permute-start(f32[2,40,128]{2,1,0:T(8,128)S(1)} %get-tuple-element.23), channel_id=1, source_target_pairs={{0,24},{8,16},{16,8},{24,0},{1,25},{9,17},{17,9},{25,1},{2,26},{10... | collective-permute-start | bytes 122888 | tf_op jit(solution)/shard_map/ppermute | solution.py:281
  11.9 3.5 %collective-permute-start.4 = (f32[1,128]{1,0:T(1,128)S(1)}, f32[1,128]{1,0:T(1,128)S(1)}, u32[]{:S(2)}, u32[]{:S(2)}) collective-permute-start(f32[1,128]{1,0:T(1,128)S(1)} %get-tuple-element.24), channel_id=1, source_target_pairs={{0,16},{8,24},{16,0},{24,8},{1,17},{9,25},{17,1},{25,9},{2,18},{10... | collective-permute-start | bytes 1544 | tf_op jit(solution)/shard_map/ppermute | solution.py:284
  15.5 1.2 %collective-permute-start.5 = (f32[1,128]{1,0:T(1,128)S(1)}, f32[1,128]{1,0:T(1,128)S(1)}, u32[]{:S(2)}, u32[]{:S(2)}) collective-permute-start(f32[1,128]{1,0:T(1,128)S(1)} %fusion.2), channel_id=1, source_target_pairs={{0,1},{1,0},{2,3},{3,2},{4,5},{5,4},{6,7},{7,6},{8,9},{9,8},{10,11... | collective-permute-start | bytes 1544 | tf_op jit(solution)/shard_map/ppermute | solution.py:303

commit v3 on v2

--- a/solution.py
+++ b/solution.py
@@ -30,29 +30,27 @@
     return dot(left_high, right_high) + (dot(left_high, right_low) + dot(left_low, right_high))
 
 
-def square_product(left, right):
-    rows, cols = left[0].shape[0], right[0].shape[1]
-    stacked = halves(jnp.concatenate(left, axis=0))
-    beside = halves(jnp.concatenate(right, axis=1))
-    full = dot3(stacked, beside)
-    real = full[:rows, :cols] - full[rows:, cols:]
-    imag = full[:rows, cols:] + full[rows:, :cols]
-    return real, imag
-
-
-def tile_taps(starts, window, vel_ref, index_ref, weight_ref, perm_ref, table_ref, table):
+def complex_product(left, right):
+    first = dot3(halves(left[0]), halves(right[0]))
+    second = dot3(halves(left[1]), halves(right[1]))
+    third = dot3(halves(left[0] + left[1]), halves(right[0] + right[1]))
+    return first - second, third - first - second
+
+
+def tile_taps(lateral_tiles, starts, window, small_ref, table_ref, table):
     count = window // TILE
-    tiles, slots = vel_ref.shape[1], index_ref.shape[0]
-    velocities, entries, taps = index_ref.shape[1], table_ref.shape[2], table_ref.shape[0]
+    slots = (small_ref.shape[0] - 2) // 2
+    tiles = velocities = small_ref.shape[1]
+    entries, taps = table_ref.shape[2], table_ref.shape[0]
     place = lax.broadcasted_iota(jnp.int32, (count, tiles), 0)
     place = place - jnp.where(place >= count - count // 4, count, 0)
     tile = jnp.concatenate([start // TILE + place for start in starts], axis=0)
     lane = lax.broadcasted_iota(jnp.int32, tile.shape, 1)
-    velocity = jnp.sum(jnp.where(lane == tile, vel_ref[...].astype(F32), 0.0), axis=1, keepdims=True)
-    inside = jnp.sum(jnp.where(lane == tile, 1.0, 0.0), axis=1, keepdims=True)
-    chosen = lax.broadcasted_iota(jnp.int32, (slots, velocities), 0) == perm_ref[...]
-    index = jnp.sum(jnp.where(chosen, index_ref[...].astype(F32), 0.0), axis=0, keepdims=True)
-    weight = jnp.sum(jnp.where(chosen, weight_ref[...], 0.0), axis=0, keepdims=True)
+    velocity = jnp.sum(jnp.where(lane == tile, small_ref[:1], 0.0), axis=1, keepdims=True)
+    inside = jnp.logical_and(tile[:, :1] >= 0, tile[:, :1] < lateral_tiles).astype(F32)
+    chosen = lax.broadcasted_iota(jnp.int32, (slots, velocities), 0).astype(F32) == small_ref[1:2, :1]
+    index = jnp.sum(jnp.where(chosen, small_ref[2 : 2 + slots], 0.0), axis=0, keepdims=True)
+    weight = jnp.sum(jnp.where(chosen, small_ref[2 + slots :], 0.0), axis=0, keepdims=True)
     rows = tile.shape[0]
     hit = lax.broadcasted_iota(jnp.int32, (rows, velocities), 1).astype(F32) == velocity
     index = jnp.sum(jnp.where(hit, index, 0.0), axis=1, keepdims=True)
@@ -87,67 +85,87 @@
 def four_substeps(start, lateral, once):
     window = once[0].shape[0]
     width = window // 2
-    twice = square_product(once, once)
-    four = square_product((twice[0][:width], twice[1][:width]), twice)
+    twice = complex_product(once, once)
+    four = complex_product((twice[0][:width], twice[1][:width]), twice)
     place = lax.broadcasted_iota(jnp.int32, (width, window), 1)
     cell = start + jnp.where(place < window - width // 2, place, place - window)
     inside = jnp.logical_and(cell >= 0, cell < lateral)
     return jnp.where(inside, four[0], 0.0), jnp.where(inside, four[1], 0.0)
 
 
-def pack_kernel(wave_ref, one_ref, two_ref):
+def groups_of(rows, width, rim):
+    count = width // rim
+    step = -(-rows // (8 * count)) * 8
+    return width // count, [(low, min(low + step, rows)) for low in range(0, rows, step)]
+
+
+def pack_kernel(rim, wave_ref, one_ref, two_ref):
     rows, width = wave_ref.shape[1], wave_ref.shape[2]
-    half = width // 2
+    span, groups = groups_of(rows, width, rim)
     odd = lax.axis_index("freq") % 2 == 1
-    lane = lax.broadcasted_iota(jnp.int32, (rows // 2, width), 1)
-    own = jnp.logical_xor(lane < half, odd)
-    for part in range(2):
-        top = wave_ref[part, : rows // 2]
-        bottom = pltpu.roll(wave_ref[part, rows // 2 :], half, 1)
-        one_ref[part] = jnp.where(own, top, bottom)
-        two_ref[part] = jnp.where(own, bottom, top)
+    lane = lax.broadcasted_iota(jnp.int32, one_ref.shape[1:], 1)
+    for part in range(2):
+        packed = []
+        for sign in (1, -1):
+            message = wave_ref[part, groups[0][0] : groups[0][1]]
+            for index, (low, high) in enumerate(groups[1:], 1):
+                count = high - low
+                place = lane[:count] if sign == 1 else width - 1 - lane[:count]
+                moved = pltpu.roll(wave_ref[part, low:high], sign * index * span % width, 1)
+                top = jnp.where(place // span == index, moved, message[:count])
+                message = top if count == message.shape[0] else jnp.concatenate([top, message[count:]], axis=0)
+            packed.append(message)
+        one_ref[part] = jnp.where(odd, packed[1], packed[0])
+        two_ref[part] = jnp.where(odd, packed[0], packed[1])
 
 
 def rcv_operator_kernel(
-    lateral, vel_ref, index_ref, weight_ref, perm_ref, table_ref, full_ref, high_ref, low_ref, src_ref, table, band
+    lateral, small_ref, table_ref, full_ref, high_ref, low_ref, found_ref, table, band
 ):
     width = full_ref.shape[1] // 2
     taps, window = table_ref.shape[0], 2 * width
-    chunks = src_ref.shape[0]
+    chunks = found_ref.shape[1] * TILE // window - 1
     starts = [lax.axis_index("rcv") * width]
     starts += [(lax.axis_index("src") * chunks + chunk) * width for chunk in range(chunks)]
-    found = tile_taps(starts, window, vel_ref, index_ref, weight_ref, perm_ref, table_ref, table)
+    found = tile_taps(lateral // TILE, starts, window, small_ref, table_ref, table)
     fill_band(found, 0, taps, band)
-    for chunk in range(chunks):
-        fill_band(found, (chunk + 1) * window // TILE, taps, src_ref.at[chunk])
+    for part in range(2):
+        found_ref[part] = found[part]
     real, imag = four_substeps(starts[0], lateral, (band[0], band[1]))
     turned = jnp.concatenate([real.T, imag.T], axis=1)
     full_ref[...] = turned
     high_ref[...], low_ref[...] = halves(turned)
 
 
-def src_operator_kernel(lateral, band_ref, high_ref, low_ref):
+def src_operator_kernel(lateral, taps, found_ref, high_ref, low_ref, band):
     chunks, width = high_ref.shape[0], high_ref.shape[2] // 2
+    found = (found_ref[0], found_ref[1])
     for chunk in range(chunks):
         start = (lax.axis_index("src") * chunks + chunk) * width
-        real, imag = four_substeps(start, lateral, (band_ref[chunk, 0], band_ref[chunk, 1]))
+        fill_band(found, (chunk + 1) * 2 * width // TILE, taps, band)
+        real, imag = four_substeps(start, lateral, (band[0], band[1]))
         high_ref[chunk], low_ref[chunk] = halves(jnp.concatenate([real, imag], axis=0))
 
 
-def receiver_kernel(wave_ref, first_ref, second_ref, full_ref, high_ref, low_ref, sunk_ref, one_ref, two_ref, image_ref):
-    rows, width = wave_ref.shape[1], wave_ref.shape[2]
+def receiver_kernel(rim, wave_ref, first_ref, second_ref, full_ref, high_ref, low_ref, sunk_ref, one_ref, two_ref, image_ref):
+    rows, width = sunk_ref.shape[1], sunk_ref.shape[2]
     half = width // 2
+    span, groups = groups_of(rows, width, rim)
     odd = lax.axis_index("freq") % 2 == 1
-    lane = lax.broadcasted_iota(jnp.int32, (rows // 2, width), 1)
     extended = []
     for part in range(2):
+        halos = []
         first, second = first_ref[part], second_ref[part]
         before = jnp.where(odd, first, second)
         after = jnp.where(odd, second, first)
-        top = jnp.where(lane < half, after, before)
-        bottom = pltpu.roll(jnp.where(lane < half, before, after), half, 1)
-        halo = jnp.concatenate([top, bottom], axis=0)
-        extended.append(jnp.concatenate([wave_ref[part], halo], axis=1))
+        for index, (low, high) in enumerate(groups):
+            left, right = after[: high - low], before[: high - low]
+            if index:
+                left = pltpu.roll(left, -index * span % width, 1)
+                right = pltpu.roll(right, index * span % width, 1)
+            lane = lax.broadcasted_iota(jnp.int32, left.shape, 1)
+            halos.append(jnp.where(lane < half, left, right))
+        extended.append(jnp.concatenate([wave_ref[part], jnp.concatenate(halos, axis=0)], axis=1))
     full = dot3(halves(jnp.concatenate(extended, axis=0)), (high_ref[...], low_ref[...]))
     real = full[:rows, :width] - full[rows:, width:]
     imag = full[:rows, width:] + full[rows:, :width]
@@ -177,7 +195,7 @@
         two_ref[part] = jnp.where(up, head[part], tail[part])
 
 
-def source_kernel(field_ref, one_ref, two_ref, high_ref, low_ref, out_ref):
+def source_kernel(field_ref, two_ref, one_ref, high_ref, low_ref, out_ref):
     rows, width = field_ref.shape[1], field_ref.shape[2]
     half = width // 2
     chunks = rows // width
@@ -229,18 +247,20 @@
     params = pltpu.CompilerParams(vmem_limit_bytes=VMEM_LIMIT)
     cost = pl.CostEstimate(flops=6 * 2**28, bytes_accessed=2**20, transcendentals=0)
 
+    small = max(vel_index.shape[0], interp_index.shape[0], width)
+    rows_of = lambda a: jnp.pad(a.astype(F32), ((0, 0), (0, small - a.shape[1])))
     tables = [
-        vel_index.reshape(1, -1),
-        interp_index.T,
-        interp_weight.T,
-        freq_perm.reshape(1, 1),
+        jnp.concatenate(
+            [rows_of(vel_index.reshape(1, -1)), jnp.pad(freq_perm, (0, small - 1)).astype(F32).reshape(1, -1), rows_of(interp_index.T), rows_of(interp_weight.T)]
+        ),
         op_table.transpose(2, 0, 1),
     ]
-    packed = jax.ShapeDtypeStruct((2, rows // 2, width), F32)
+    _, groups = groups_of(rows, width, rim)
+    packed = jax.ShapeDtypeStruct((2, groups[0][1], width), F32)
     first, second = pl.pallas_call(
-        pack_kernel,
+        functools.partial(pack_kernel, rim),
         out_shape=[packed, packed],
-        in_specs=[pl.BlockSpec(wave.shape, lambda: (0, 0, 0))],
+        in_specs=[vmem],
         out_specs=[vmem] * 2,
         compiler_params=params,
         name="pack",
@@ -249,15 +269,15 @@
     second = lax.ppermute(second, ("rcv", "freq"), around(n_rcv, n_freq, 1))
 
     square = (2 * width, 2 * width)
-    rcv_full, rcv_high, rcv_low, src_band = pl.pallas_call(
+    rcv_full, rcv_high, rcv_low, found = pl.pallas_call(
         functools.partial(rcv_operator_kernel, lateral),
         out_shape=[
             jax.ShapeDtypeStruct(square, F32),
             jax.ShapeDtypeStruct(square, BF16),
             jax.ShapeDtypeStruct(square, BF16),
-            jax.ShapeDtypeStruct((chunks, 2) + square, F32),
+            jax.ShapeDtypeStruct((2, (chunks + 1) * 2 * width // TILE, width), F32),
         ],
-        in_specs=[pl.BlockSpec(a.shape, lambda n=len(a.shape): (0,) * n) for a in tables],
+        in_specs=[vmem] * 2,
         out_specs=[vmem] * 4,
         scratch_shapes=[pltpu.VMEM((2, width, op_table.shape[1]), F32), pltpu.VMEM((2,) + square, F32)],
         compiler_params=params,
@@ -265,7 +285,7 @@
         name="rcv_operator",
     )(*tables)
     field, one, two, image = pl.pallas_call(
-        receiver_kernel,
+        functools.partial(receiver_kernel, rim),
         out_shape=[
             jax.ShapeDtypeStruct((2, rows, width), F32),
             jax.ShapeDtypeStruct((2, edge, width), F32),
@@ -283,14 +303,15 @@
     if n_src == 4:
         far = lax.ppermute(image, "src", [(i, i ^ 2) for i in range(n_src)])
     src_high, src_low = pl.pallas_call(
-        functools.partial(src_operator_kernel, lateral),
+        functools.partial(src_operator_kernel, lateral, op_table.shape[2]),
         out_shape=[jax.ShapeDtypeStruct((chunks,) + square, BF16)] * 2,
         in_specs=[vmem],
         out_specs=[vmem] * 2,
+        scratch_shapes=[pltpu.VMEM((2,) + square, F32)],
         compiler_params=params,
         cost_estimate=pl.CostEstimate(flops=2**20, bytes_accessed=2**10, transcendentals=0),
         name="src_operator",
-    )(src_band)
+    )(found)
     if n_src == 4:
         up = lax.axis_index("src") % 2 == 0
         from_one = jnp.where(up, one[0, edge - 1 :], one[0, :1])
@@ -310,7 +331,7 @@
         out_specs=vmem,
         compiler_params=params,
         name="sources",
-    )(field, one, two, src_high, src_low)
+    )(field, two, one, src_high, src_low)
     return sunk.reshape(wavefield.shape), image.reshape(width)
 
 

time: 17.4 us -> 16.4 us (0.943)
  Pallas kernels: 4.69 us -> 3.85 us
  local copies, waits for them, and re-layouts: 1.57 us -> 0.92 us
  waiting for transfers between devices: 2.33 us -> 2.61 us
  starting transfers between devices: 6.69 us -> 6.89 us
    ppermute x1, starting transfers between devices: 1.49 us -> 3.11 us  [body(): lax.ppermute(two, 'src', [(i, (i - 1 if i % 2 == 0 else i + 1) % n_src) f...]
    ppermute x1, starting transfers between devices: 1.98 us -> 0.53 us  [body(): lax.ppermute(one, 'src', [(i, i + 1 if i % 2 == 0 else i - 1) for i in ra...]
    unnamed x12, local copies, waits for them, and re-layouts: 1.57 us -> 0.92 us
    pallas_call x1, Pallas kernels: 2.06 us -> 1.49 us  [body(): pl.pallas_call(functools.partial(rcv_operator_kernel, lateral), out_shape...]
    ppermute x1, waiting for transfers between devices: 2.14 us -> 2.42 us  [body(): far = lax.ppermute(image, 'src', [(i, i ^ 2) for i in range(n_src)])]
    pallas_call x3, Pallas kernels: 1.7 us -> 1.44 us  [the longest x1 1 us: body(): pl.pallas_call(functools.partial(src_operator_kernel, lateral, op_table.s...]
  transfers between devices with their start and end apart: 6 -> 6, of which waited for: 2 -> 2; matrix products, arithmetic and copies ran while one was open for 0% -> 0% of each run, Pallas kernels for 25% -> 21%
where the time goes in v3:
time: 16.4 us; the launch traced here: 16.2 us
  starting transfers between devices  6.89 us (42%)
  Pallas kernels  3.85 us (23%)
  waiting for transfers between devices  2.61 us (16%)
  between operations  1.41 us (9%)
  local copies, waits for them, and re-layouts  0.92 us (6%)
  other arithmetic  0.54 us (3%)
    ppermute x1, starting transfers between devices, body(): lax.ppermute(two, 'src', [(i, (i - 1 if i % 2 == 0 else i + 1) % n_src) f...  3.11 us
    ppermute x1, starting transfers between devices, body(): second = lax.ppermute(second, ('rcv', 'freq'), around(n_rcv, n_freq, 1))  2.6 us
    ppermute x1, waiting for transfers between devices, body(): far = lax.ppermute(image, 'src', [(i, i ^ 2) for i in range(n_src)])  2.42 us
    pallas_call x1, Pallas kernels, body(): pl.pallas_call(functools.partial(rcv_operator_kernel, lateral), out_shape...  1.49 us
    pallas_call x1, Pallas kernels, body(): pl.pallas_call(functools.partial(src_operator_kernel, lateral, op_table.s...  1 us
    pallas_call x1, Pallas kernels, body(): pl.pallas_call(source_kernel, out_shape=jax.ShapeDtypeStruct((2, rows, wi...  0.93 us
    unnamed x12, local copies, waits for them, and re-layouts  0.92 us
    ppermute x1, starting transfers between devices, body(): lax.ppermute(one, 'src', [(i, i + 1 if i % 2 == 0 else i - 1) for i in ra...  0.53 us
  transfers between devices with their start and end apart: 6, of which 2 were waited for; matrix products, arithmetic and copies ran while one was open for 0% of the time, Pallas kernels for 21%

profile of v3, /device:TPU:0, one launch (start us, length us, event | category | flops | bytes accessed | tf_op | source)
XLA Modules:
  0.0 16.2 jit_solution(14230541731155899618)
XLA Ops:
  0.6 0.0 copy-start
  0.6 0.9 %copy-done = f32[2,1,128,128]{3,2,1,0:T(8,128)S(1)} copy-done((f32[2,1,128,128]{3,2,1,0:T(8,128)S(1)}, f32[2,1,128,128]{3,2,1,0:T(8,128)}, u32[]{:S(2)}) %copy-start) | copy-done | bytes 131096
  1.5 0.0 copy-start.4
  1.5 0.0 copy-start.5
  1.5 0.0 copy-start.3
  1.5 0.1 pack.1
  1.7 0.0 copy-start.2
  1.7 0.5 %collective-permute-start = (f32[2,48,128]{2,1,0:T(8,128)S(1)}, f32[2,48,128]{2,1,0:T(8,128)S(1)}, u32[]{:S(2)}, u32[]{:S(2)}) collective-permute-start(f32[2,48,128]{2,1,0:T(8,128)S(1)} %get-tuple-element.16), channel_id=1, source_target_pairs={{0,1},{1,3},{2,0},{3,5},{4,2},{5,7},{6,4},{7,6},{8,9},{9,11},{10,8... | collective-permute-start | bytes 147464 | tf_op jit(solution)/shard_map/ppermute | solution.py:268
  2.1 2.6 %collective-permute-start.1 = (f32[2,48,128]{2,1,0:T(8,128)S(1)}, f32[2,48,128]{2,1,0:T(8,128)S(1)}, u32[]{:S(2)}, u32[]{:S(2)}) collective-permute-start(f32[2,48,128]{2,1,0:T(8,128)S(1)} %get-tuple-element.17), channel_id=1, source_target_pairs={{0,2},{1,0},{2,4},{3,1},{4,6},{5,3},{6,7},{7,5},{8,10},{9,8},{10,1... | collective-permute-start | bytes 147464 | tf_op jit(solution)/shard_map/ppermute | solution.py:269
  4.7 0.0 copy-done.4
  4.7 0.0 copy-done.5
  5.4 0.0 copy-done.3
  5.4 0.0 copy-done.2
  5.5 0.0 copy-start.1
  5.5 1.5 %rcv_operator.1 = (f32[256,256]{1,0:T(8,128)S(1)}, bf16[256,256]{1,0:T(8,128)(2,1)S(1)}, bf16[256,256]{1,0:T(8,128)(2,1)S(1)}, f32[2,32,128]{2,1,0:T(8,128)S(1)}) custom-call(f32[6,128]{1,0:T(8,128)S(1)} %select_maximum_fusion.small_ref, f32[19,2,64]{2,1,0:T(2,128)S(1)} %bitcast.28), custom_call_target="tpu_custom_call" | custom-call | flops 1610612736 | bytes 1048576 | tf_op jit(solution)/shard_map/rcv_operator/pallas_call | solution.py:272
  7.0 0.0 collective-permute-done.first_ref
  7.0 0.0 collective-permute-done.1.second_ref
  7.0 0.0 copy-done.1
  7.0 0.3 %receivers.1 = (f32[2,128,128]{2,1,0:T(8,128)S(1)}, f32[2,40,128]{2,1,0:T(8,128)S(1)}, f32[2,40,128]{2,1,0:T(8,128)S(1)}, f32[1,128]{1,0:T(1,128)S(1)}) custom-call(f32[2,128,128]{2,1,0:T(8,128)S(1)} %bitcast.27, f32[2,48,128]{2,1,0:T(8,128)S(1)} %collective-permute-done.first_ref, f32[2,48,128]{2,1,0:T(8,128)S(1)} %collective-permute-done.1.second_ref, ...), custom_call_target="tpu_custom_call" | custom-call | tf_op jit(solution)/shard_map/receivers/pallas_call | solution.py:287
  7.3 3.1 %collective-permute-start.2 = (f32[2,40,128]{2,1,0:T(8,128)S(1)}, f32[2,40,128]{2,1,0:T(8,128)S(1)}, u32[]{:S(2)}, u32[]{:S(2)}) collective-permute-start(f32[2,40,128]{2,1,0:T(8,128)S(1)} %get-tuple-element.22), channel_id=1, source_target_pairs={{0,24},{8,16},{16,8},{24,0},{1,25},{9,17},{17,9},{25,1},{2,26},{10... | collective-permute-start | bytes 122888 | tf_op jit(solution)/shard_map/ppermute | solution.py:301
  10.4 0.5 %collective-permute-start.3 = (f32[2,40,128]{2,1,0:T(8,128)S(1)}, f32[2,40,128]{2,1,0:T(8,128)S(1)}, u32[]{:S(2)}, u32[]{:S(2)}) collective-permute-start(f32[2,40,128]{2,1,0:T(8,128)S(1)} %get-tuple-element.23), channel_id=1, source_target_pairs={{0,8},{8,0},{16,24},{24,16},{1,9},{9,1},{17,25},{25,17},{2,10},{10... | collective-permute-start | bytes 122888 | tf_op jit(solution)/shard_map/ppermute | solution.py:302
  11.0 0.1 collective-permute-start.4
  11.1 1.0 %src_operator.1 = (bf16[1,256,256]{2,1,0:T(8,128)(2,1)S(1)}, bf16[1,256,256]{2,1,0:T(8,128)(2,1)S(1)}) custom-call(f32[2,32,128]{2,1,0:T(8,128)S(1)} %get-tuple-element.25.found_ref), custom_call_target="tpu_custom_call" | custom-call | flops 1048576 | bytes 1024 | tf_op jit(solution)/shard_map/src_operator/pallas_call | solution.py:305
  12.1 2.4 %collective-permute-done.4 = f32[1,128]{1,0:T(1,128)S(1)} collective-permute-done((f32[1,128]{1,0:T(1,128)S(1)}, f32[1,128]{1,0:T(1,128)S(1)}, u32[]{:S(2)}, u32[]{:S(2)}) %collective-permute-start.4) | collective-permute-done | bytes 544 | tf_op jit(solution)/shard_map/ppermute | solution.py:304
  14.5 0.0 collective-permute-done.2.two_ref
  14.5 0.0 collective-permute-done.3.one_ref
  14.5 0.1 collective-permute-start.5
  14.6 0.9 %sources.1 = f32[2,128,128]{2,1,0:T(8,128)} custom-call(f32[2,128,128]{2,1,0:T(8,128)S(1)} %get-tuple-element.21.field_ref, f32[2,40,128]{2,1,0:T(8,128)S(1)} %collective-permute-done.2.two_ref, f32[2,40,128]{2,1,0:T(8,128)S(1)} %collective-permute-done.3.one_ref, bf16[1,256,256]{2,1,0:T(8,128)(2,1)S(1)} %get-tuple-element.27.high_ref, ...), custom_call_target="tpu_custom_call" | custom-call | tf_op jit(solution)/shard_map/sources/pallas_call | solution.py:327
  15.5 0.2 %collective-permute-done.5 = f32[1,128]{1,0:T(1,128)S(1)} collective-permute-done((f32[1,128]{1,0:T(1,128)S(1)}, f32[1,128]{1,0:T(1,128)S(1)}, u32[]{:S(2)}, u32[]{:S(2)}) %collective-permute-start.5) | collective-permute-done | bytes 544 | tf_op jit(solution)/shard_map/ppermute | solution.py:324
  15.7 0.5 %add_bitcast_fusion = f32[128]{0:T(128)} fusion(f32[1,128]{1,0:T(1,128)S(1)} %fusion.3, f32[1,128]{1,0:T(1,128)S(1)} %collective-permute-done.5), kind=kLoop, calls=%fused_computation.16 | loop fusion | flops 128 | bytes 1536 | tf_op jit(solution)/shard_map/reshape | solution.py:335
  (5 shorter events, 0.0 us)
Async XLA Ops:
  0.6 0.9 %copy-start = (f32[2,1,128,128]{3,2,1,0:T(8,128)S(1)}, f32[2,1,128,128]{3,2,1,0:T(8,128)}, u32[]{:S(2)}) copy-start(f32[2,1,128,128]{3,2,1,0:T(8,128)} %param.6) | copy-start | bytes 393220
  1.5 3.2 %copy-start.4 = (s32[16,2]{0,1:T(2,128)S(1)}, s32[16,2]{0,1:T(2,128)}, u32[]{:S(2)}) copy-start(s32[16,2]{0,1:T(2,128)} %param.9) | copy-start | bytes 388
  1.5 3.2 %copy-start.5 = (s32[32]{0:T(128)S(1)}, s32[32]{0:T(128)}, u32[]{:S(2)}) copy-start(s32[32]{0:T(128)} %param.8) | copy-start | bytes 388
  1.5 3.9 %copy-start.3 = (f32[16,2]{0,1:T(2,128)S(1)}, f32[16,2]{0,1:T(2,128)}, u32[]{:S(2)}) copy-start(f32[16,2]{0,1:T(2,128)} %param.10) | copy-start | bytes 388
  1.7 3.8 %copy-start.2 = (f32[2,64,19]{1,0,2:T(2,128)S(1)}, f32[2,64,19]{1,0,2:T(2,128)}, u32[]{:S(2)}) copy-start(f32[2,64,19]{1,0,2:T(2,128)} %param.7) | copy-start | bytes 29188
  1.7 5.3 %collective-permute-start = (f32[2,48,128]{2,1,0:T(8,128)S(1)}, f32[2,48,128]{2,1,0:T(8,128)S(1)}, u32[]{:S(2)}, u32[]{:S(2)}) collective-permute-start(f32[2,48,128]{2,1,0:T(8,128)S(1)} %get-tuple-element.16), channel_id=1, source_target_pairs={{0,1},{1,3},{2,0},{3,5},{4,2},{5,7},{6,4},{7,6},{8,9},{9,11},{10,8... | collective-permute-start | bytes 147464 | tf_op jit(solution)/shard_map/ppermute | solution.py:268
  2.1 4.8 %collective-permute-start.1 = (f32[2,48,128]{2,1,0:T(8,128)S(1)}, f32[2,48,128]{2,1,0:T(8,128)S(1)}, u32[]{:S(2)}, u32[]{:S(2)}) collective-permute-start(f32[2,48,128]{2,1,0:T(8,128)S(1)} %get-tuple-element.17), channel_id=1, source_target_pairs={{0,2},{1,0},{2,4},{3,1},{4,6},{5,3},{6,7},{7,5},{8,10},{9,8},{10,1... | collective-permute-start | bytes 147464 | tf_op jit(solution)/shard_map/ppermute | solution.py:269
  5.5 1.5 %copy-start.1 = (f32[2,1,128,128]{3,2,1,0:T(8,128)S(1)}, f32[2,1,128,128]{3,2,1,0:T(8,128)}, u32[]{:S(2)}) copy-start(f32[2,1,128,128]{3,2,1,0:T(8,128)} %param.6) | copy-start | bytes 393220
  7.3 7.2 %collective-permute-start.2 = (f32[2,40,128]{2,1,0:T(8,128)S(1)}, f32[2,40,128]{2,1,0:T(8,128)S(1)}, u32[]{:S(2)}, u32[]{:S(2)}) collective-permute-start(f32[2,40,128]{2,1,0:T(8,128)S(1)} %get-tuple-element.22), channel_id=1, source_target_pairs={{0,24},{8,16},{16,8},{24,0},{1,25},{9,17},{17,9},{25,1},{2,26},{10... | collective-permute-start | bytes 122888 | tf_op jit(solution)/shard_map/ppermute | solution.py:301
  10.4 4.1 %collective-permute-start.3 = (f32[2,40,128]{2,1,0:T(8,128)S(1)}, f32[2,40,128]{2,1,0:T(8,128)S(1)}, u32[]{:S(2)}, u32[]{:S(2)}) collective-permute-start(f32[2,40,128]{2,1,0:T(8,128)S(1)} %get-tuple-element.23), channel_id=1, source_target_pairs={{0,8},{8,0},{16,24},{24,16},{1,9},{9,1},{17,25},{25,17},{2,10},{10... | collective-permute-start | bytes 122888 | tf_op jit(solution)/shard_map/ppermute | solution.py:302
  11.0 3.5 %collective-permute-start.4 = (f32[1,128]{1,0:T(1,128)S(1)}, f32[1,128]{1,0:T(1,128)S(1)}, u32[]{:S(2)}, u32[]{:S(2)}) collective-permute-start(f32[1,128]{1,0:T(1,128)S(1)} %get-tuple-element.24), channel_id=1, source_target_pairs={{0,16},{8,24},{16,0},{24,8},{1,17},{9,25},{17,1},{25,9},{2,18},{10... | collective-permute-start | bytes 1544 | tf_op jit(solution)/shard_map/ppermute | solution.py:304
  14.5 1.2 %collective-permute-start.5 = (f32[1,128]{1,0:T(1,128)S(1)}, f32[1,128]{1,0:T(1,128)S(1)}, u32[]{:S(2)}, u32[]{:S(2)}) collective-permute-start(f32[1,128]{1,0:T(1,128)S(1)} %fusion.3), channel_id=1, source_target_pairs={{0,1},{1,0},{2,3},{3,2},{4,5},{5,4},{6,7},{7,6},{8,9},{9,8},{10,11... | collective-permute-start | bytes 1544 | tf_op jit(solution)/shard_map/ppermute | solution.py:324

commit v4 on v3

--- a/solution.py
+++ b/solution.py
@@ -195,12 +195,14 @@
         two_ref[part] = jnp.where(up, head[part], tail[part])
 
 
-def source_kernel(field_ref, two_ref, one_ref, high_ref, low_ref, out_ref):
+def source_kernel(field_ref, two_ref, one_ref, high_ref, low_ref, *rest):
     rows, width = field_ref.shape[1], field_ref.shape[2]
     half = width // 2
     chunks = rows // width
     edge = one_ref.shape[1]
     up = lax.axis_index("src") % 2 == 0
+    *image_refs, out_ref, image_ref = rest
+    image_ref[...] = functools.reduce(jnp.add, [ref[...] for ref in image_refs])
     gap = jnp.zeros((half - edge, width), F32)
     for chunk in range(chunks):
         low, high = chunk * width, (chunk + 1) * width
@@ -232,6 +234,16 @@
     return pairs
 
 
+def between(src, freq):
+    pairs = []
+    for at in range(src):
+        target = at - 1 if at % 2 == 0 else at + 1
+        for slot in range(freq):
+            ends = not 0 <= target < src
+            pairs.append((at * freq + slot, at * freq + (slot ^ 1) if ends else target * freq + slot))
+    return pairs
+
+
 def body(wavefield, op_table, vel_index, interp_index, interp_weight, freq_perm):
     rows, width = wavefield.shape[2], wavefield.shape[3]
     n_src, n_rcv, n_freq = (lax.axis_size(axis) for axis in ("src", "rcv", "freq"))
@@ -298,10 +310,19 @@
         name="receivers",
     )(wave, first, second, rcv_full, rcv_high, rcv_low)
 
-    two = lax.ppermute(two, "src", [(i, (i - 1 if i % 2 == 0 else i + 1) % n_src) for i in range(n_src)])
+    if n_freq == 2:
+        other = lax.ppermute(one, "freq", [(0, 1), (1, 0)])
+        image = image + jnp.where(lax.axis_index("src") % 2 == 0, other[0, :1], other[0, edge - 1 :])
+    else:
+        image = lax.psum(image, "freq")
     one = lax.ppermute(one, "src", [(i, i + 1 if i % 2 == 0 else i - 1) for i in range(n_src)])
     if n_src == 4:
-        far = lax.ppermute(image, "src", [(i, i ^ 2) for i in range(n_src)])
+        pairs = [(i * n_freq + f, (i ^ (2 + f % 2)) * n_freq + f) for i in range(n_src) for f in range(n_freq)]
+        far = lax.ppermute(image, ("src", "freq"), pairs)
+        if n_freq > 2:
+            far = jnp.where(lax.axis_index("freq") < 2, far, 0.0)
+    two = lax.ppermute(two, ("src", "freq"), between(n_src, n_freq))
+    one, found = lax.optimization_barrier((one, found))
     src_high, src_low = pl.pallas_call(
         functools.partial(src_operator_kernel, lateral, op_table.shape[2]),
         out_shape=[jax.ShapeDtypeStruct((chunks,) + square, BF16)] * 2,
@@ -315,23 +336,21 @@
     if n_src == 4:
         up = lax.axis_index("src") % 2 == 0
         from_one = jnp.where(up, one[0, edge - 1 :], one[0, :1])
-        from_two = jnp.where(up, two[0, :1], two[0, edge - 1 :])
-        image = (image + from_one) + (from_two + far)
+        near, src_high = lax.optimization_barrier((from_one + far, src_high))
+        if n_freq == 2:
+            images = [image, near, lax.ppermute(near, "freq", [(0, 1), (1, 0)])]
+        else:
+            images = [image, lax.psum(near, "freq")]
     else:
-        image = lax.psum(image, "src")
-    image, src_high = lax.optimization_barrier((image, src_high))
-    if n_freq == 2:
-        image = image + lax.ppermute(image, "freq", [(0, 1), (1, 0)])
-    else:
-        image = lax.psum(image, "freq")
-    sunk = pl.pallas_call(
+        images = [lax.psum(image, "src")]
+    sunk, image = pl.pallas_call(
         source_kernel,
-        out_shape=jax.ShapeDtypeStruct((2, rows, width), F32),
-        in_specs=[vmem] * 5,
-        out_specs=vmem,
+        out_shape=[jax.ShapeDtypeStruct((2, rows, width), F32), jax.ShapeDtypeStruct((1, width), F32)],
+        in_specs=[vmem] * (5 + len(images)),
+        out_specs=[vmem] * 2,
         compiler_params=params,
         name="sources",
-    )(field, two, one, src_high, src_low)
+    )(field, two, one, src_high, src_low, *images)
     return sunk.reshape(wavefield.shape), image.reshape(width)
 
 

time: 16.4 us -> 15.4 us (0.939)
  waiting for transfers between devices: 2.61 us -> 1.77 us
  other arithmetic: 0.54 us -> 0.03 us
  starting transfers between devices: 6.89 us -> 7.28 us
    ppermute x1, starting transfers between devices: 0.53 us -> 1.99 us  [body(): lax.ppermute(one, 'src', [(i, i + 1 if i % 2 == 0 else i - 1) for i in ra...]
    ppermute x3 -> x4, starting transfers between devices: 3.29 us -> 2.22 us  [the longest x1 1.58 us: body(): far = lax.ppermute(image, ('src', 'freq'), pairs)]
    ppermute x3 -> x4, waiting for transfers between devices: 2.6 us -> 1.59 us  [the longest x1 1.11 us: body(): images = [image, near, lax.ppermute(near, 'freq', [(0, 1), (1, 0)])]]
    reshape x1 -> x0, other arithmetic: 0.51 us -> none  [body(): return (sunk.reshape(wavefield.shape), image.reshape(width))]
    ppermute x1, waiting for transfers between devices: 0.01 us -> 0.17 us  [body(): lax.ppermute(one, 'src', [(i, i + 1 if i % 2 == 0 else i - 1) for i in ra...]
  transfers between devices with their start and end apart: 6 -> 7, of which waited for: 2 -> 3; matrix products, arithmetic and copies ran while one was open for 0% -> 0% of each run, Pallas kernels for 21% -> 16%
where the time goes in v4:
time: 15.4 us; the launch traced here: 15.3 us
  starting transfers between devices  7.28 us (47%)
  Pallas kernels  3.86 us (25%)
  waiting for transfers between devices  1.77 us (11%)
  between operations  1.41 us (9%)
  local copies, waits for them, and re-layouts  0.92 us (6%)
    ppermute x1, starting transfers between devices, body(): second = lax.ppermute(second, ('rcv', 'freq'), around(n_rcv, n_freq, 1))  2.6 us
    ppermute x1, starting transfers between devices, body(): lax.ppermute(one, 'src', [(i, i + 1 if i % 2 == 0 else i - 1) for i in ra...  1.99 us
    ppermute x1, starting transfers between devices, body(): far = lax.ppermute(image, ('src', 'freq'), pairs)  1.58 us
    pallas_call x1, Pallas kernels, body(): pl.pallas_call(functools.partial(rcv_operator_kernel, lateral), out_shape...  1.49 us
    ppermute x1, waiting for transfers between devices, body(): images = [image, near, lax.ppermute(near, 'freq', [(0, 1), (1, 0)])]  1.11 us
    pallas_call x1, Pallas kernels, body(): pl.pallas_call(functools.partial(src_operator_kernel, lateral, op_table.s...  1 us
    pallas_call x1, Pallas kernels, body(): pl.pallas_call(source_kernel, out_shape=[jax.ShapeDtypeStruct((2, rows, w...  0.93 us
    unnamed x12, local copies, waits for them, and re-layouts  0.92 us
  transfers between devices with their start and end apart: 7, of which 3 were waited for; matrix products, arithmetic and copies ran while one was open for 0% of the time, Pallas kernels for 16%

profile of v4, /device:TPU:0, one launch (start us, length us, event | category | flops | bytes accessed | tf_op | source)
XLA Modules:
  0.0 15.3 jit_solution(6162852522714522868)
XLA Ops:
  0.6 0.0 copy-start
  0.6 0.9 %copy-done = f32[2,1,128,128]{3,2,1,0:T(8,128)S(1)} copy-done((f32[2,1,128,128]{3,2,1,0:T(8,128)S(1)}, f32[2,1,128,128]{3,2,1,0:T(8,128)}, u32[]{:S(2)}) %copy-start) | copy-done | bytes 131096
  1.5 0.0 copy-start.4
  1.5 0.0 copy-start.5
  1.5 0.0 copy-start.3
  1.5 0.1 pack.1
  1.7 0.0 copy-start.2
  1.7 0.5 %collective-permute-start = (f32[2,48,128]{2,1,0:T(8,128)S(1)}, f32[2,48,128]{2,1,0:T(8,128)S(1)}, u32[]{:S(2)}, u32[]{:S(2)}) collective-permute-start(f32[2,48,128]{2,1,0:T(8,128)S(1)} %get-tuple-element.20), channel_id=1, source_target_pairs={{0,1},{1,3},{2,0},{3,5},{4,2},{5,7},{6,4},{7,6},{8,9},{9,11},{10,8... | collective-permute-start | bytes 147464 | tf_op jit(solution)/shard_map/ppermute | solution.py:280
  2.1 2.6 %collective-permute-start.1 = (f32[2,48,128]{2,1,0:T(8,128)S(1)}, f32[2,48,128]{2,1,0:T(8,128)S(1)}, u32[]{:S(2)}, u32[]{:S(2)}) collective-permute-start(f32[2,48,128]{2,1,0:T(8,128)S(1)} %get-tuple-element.21), channel_id=1, source_target_pairs={{0,2},{1,0},{2,4},{3,1},{4,6},{5,3},{6,7},{7,5},{8,10},{9,8},{10,1... | collective-permute-start | bytes 147464 | tf_op jit(solution)/shard_map/ppermute | solution.py:281
  4.7 0.0 copy-done.4
  4.7 0.0 copy-done.5
  5.4 0.0 copy-done.3
  5.4 0.0 copy-done.2
  5.5 0.0 copy-start.1
  5.5 1.5 %rcv_operator.1 = (f32[256,256]{1,0:T(8,128)S(1)}, bf16[256,256]{1,0:T(8,128)(2,1)S(1)}, bf16[256,256]{1,0:T(8,128)(2,1)S(1)}, f32[2,32,128]{2,1,0:T(8,128)S(1)}) custom-call(f32[6,128]{1,0:T(8,128)S(1)} %select_maximum_fusion.small_ref, f32[19,2,64]{2,1,0:T(2,128)S(1)} %bitcast.23), custom_call_target="tpu_custom_call" | custom-call | flops 1610612736 | bytes 1048576 | tf_op jit(solution)/shard_map/rcv_operator/pallas_call | solution.py:284
  7.0 0.0 collective-permute-done.first_ref
  7.0 0.0 collective-permute-done.1.second_ref
  7.0 0.0 copy-done.1
  7.0 0.3 %receivers.1 = (f32[2,128,128]{2,1,0:T(8,128)S(1)}, f32[2,40,128]{2,1,0:T(8,128)S(1)}, f32[2,40,128]{2,1,0:T(8,128)S(1)}, f32[1,128]{1,0:T(1,128)S(1)}) custom-call(f32[2,128,128]{2,1,0:T(8,128)S(1)} %bitcast.22, f32[2,48,128]{2,1,0:T(8,128)S(1)} %collective-permute-done.first_ref, f32[2,48,128]{2,1,0:T(8,128)S(1)} %collective-permute-done.1.second_ref, ...), custom_call_target="tpu_custom_call" | custom-call | tf_op jit(solution)/shard_map/receivers/pallas_call | solution.py:299
  7.3 0.3 %collective-permute-start.4 = (f32[2,40,128]{2,1,0:T(8,128)S(1)}, f32[2,40,128]{2,1,0:T(8,128)S(1)}, u32[]{:S(2)}, u32[]{:S(2)}) collective-permute-start(f32[2,40,128]{2,1,0:T(8,128)S(1)} %get-tuple-element.27), channel_id=1, source_target_pairs={{0,1},{1,0},{2,3},{3,2},{4,5},{5,4},{6,7},{7,6},{8,9},{9,8},{10,11... | collective-permute-start | bytes 122888 | tf_op jit(solution)/shard_map/ppermute | solution.py:314
  7.6 2.0 %collective-permute-start.3 = (f32[2,40,128]{2,1,0:T(8,128)S(1)}, f32[2,40,128]{2,1,0:T(8,128)S(1)}, u32[]{:S(2)}, u32[]{:S(2)}) collective-permute-start(f32[2,40,128]{2,1,0:T(8,128)S(1)} %get-tuple-element.27), channel_id=1, source_target_pairs={{0,8},{8,0},{16,24},{24,16},{1,9},{9,1},{17,25},{25,17},{2,10},{10... | collective-permute-start | bytes 122888 | tf_op jit(solution)/shard_map/ppermute | solution.py:318
  9.6 0.0 collective-permute-done.4
  9.6 1.6 %collective-permute-start.5 = (f32[1,128]{1,0:T(1,128)S(1)}, f32[1,128]{1,0:T(1,128)S(1)}, u32[]{:S(2)}, u32[]{:S(2)}) collective-permute-start(f32[1,128]{1,0:T(1,128)S(1)} %fusion.4.rest_0_), channel_id=1, source_target_pairs={{0,16},{1,25},{8,24},{9,17},{16,0},{17,9},{24,8},{25,1},{2,18},{3,... | collective-permute-start | bytes 1544 | tf_op jit(solution)/shard_map/ppermute | solution.py:321
  11.2 0.4 %collective-permute-start.2 = (f32[2,40,128]{2,1,0:T(8,128)S(1)}, f32[2,40,128]{2,1,0:T(8,128)S(1)}, u32[]{:S(2)}, u32[]{:S(2)}) collective-permute-start(f32[2,40,128]{2,1,0:T(8,128)S(1)} %get-tuple-element.26), channel_id=1, source_target_pairs={{0,1},{1,0},{8,16},{9,17},{16,8},{17,9},{24,25},{25,24},{2,3},{3,2... | collective-permute-start | bytes 122888 | tf_op jit(solution)/shard_map/ppermute | solution.py:324
  11.5 0.2 %collective-permute-done.3.one_ref = f32[2,40,128]{2,1,0:T(8,128)S(1)} collective-permute-done((f32[2,40,128]{2,1,0:T(8,128)S(1)}, f32[2,40,128]{2,1,0:T(8,128)S(1)}, u32[]{:S(2)}, u32[]{:S(2)}) %collective-permute-start.3) | collective-permute-done | bytes 40992 | tf_op jit(solution)/shard_map/ppermute | solution.py:318
  11.7 1.0 %src_operator.1 = (bf16[1,256,256]{2,1,0:T(8,128)(2,1)S(1)}, bf16[1,256,256]{2,1,0:T(8,128)(2,1)S(1)}) custom-call(f32[2,32,128]{2,1,0:T(8,128)S(1)} %get-tuple-element.31.found_ref), custom_call_target="tpu_custom_call" | custom-call | flops 1048576 | bytes 1024 | tf_op jit(solution)/shard_map/src_operator/pallas_call | solution.py:326
  12.7 0.5 %collective-permute-done.5 = f32[1,128]{1,0:T(1,128)S(1)} collective-permute-done((f32[1,128]{1,0:T(1,128)S(1)}, f32[1,128]{1,0:T(1,128)S(1)}, u32[]{:S(2)}, u32[]{:S(2)}) %collective-permute-start.5) | collective-permute-done | bytes 544 | tf_op jit(solution)/shard_map/ppermute | solution.py:321
  13.2 0.0 collective-permute-start.6
  13.2 0.0 collective-permute-done.2.two_ref
  13.2 1.1 %collective-permute-done.6.rest_2_ = f32[1,128]{1,0:T(1,128)S(1)} collective-permute-done((f32[1,128]{1,0:T(1,128)S(1)}, f32[1,128]{1,0:T(1,128)S(1)}, u32[]{:S(2)}, u32[]{:S(2)}) %collective-permute-start.6) | collective-permute-done | bytes 544 | tf_op jit(solution)/shard_map/ppermute | solution.py:341
  14.3 0.9 %sources.1 = (f32[2,128,128]{2,1,0:T(8,128)}, f32[1,128]{1,0:T(1,128)}) custom-call(f32[2,128,128]{2,1,0:T(8,128)S(1)} %get-tuple-element.25.field_ref, f32[2,40,128]{2,1,0:T(8,128)S(1)} %collective-permute-done.2.two_ref, f32[2,40,128]{2,1,0:T(8,128)S(1)} %collective-permute-done.3.one_ref, bf16[1,256,256]{2,1,0:T(8,128)(2,1)S(1)} %get-tuple-element.33.high_ref, ...), custom_call_target="tpu_custom_call" | custom-call | tf_op jit(solution)/shard_map/sources/pallas_call | solution.py:346
  (6 shorter events, 0.0 us)
Async XLA Ops:
  0.6 0.9 %copy-start = (f32[2,1,128,128]{3,2,1,0:T(8,128)S(1)}, f32[2,1,128,128]{3,2,1,0:T(8,128)}, u32[]{:S(2)}) copy-start(f32[2,1,128,128]{3,2,1,0:T(8,128)} %param.6) | copy-start | bytes 393220
  1.5 3.2 %copy-start.4 = (s32[16,2]{0,1:T(2,128)S(1)}, s32[16,2]{0,1:T(2,128)}, u32[]{:S(2)}) copy-start(s32[16,2]{0,1:T(2,128)} %param.9) | copy-start | bytes 388
  1.5 3.2 %copy-start.5 = (s32[32]{0:T(128)S(1)}, s32[32]{0:T(128)}, u32[]{:S(2)}) copy-start(s32[32]{0:T(128)} %param.8) | copy-start | bytes 388
  1.5 3.9 %copy-start.3 = (f32[16,2]{0,1:T(2,128)S(1)}, f32[16,2]{0,1:T(2,128)}, u32[]{:S(2)}) copy-start(f32[16,2]{0,1:T(2,128)} %param.10) | copy-start | bytes 388
  1.7 3.8 %copy-start.2 = (f32[2,64,19]{1,0,2:T(2,128)S(1)}, f32[2,64,19]{1,0,2:T(2,128)}, u32[]{:S(2)}) copy-start(f32[2,64,19]{1,0,2:T(2,128)} %param.7) | copy-start | bytes 29188
  1.7 5.3 %collective-permute-start = (f32[2,48,128]{2,1,0:T(8,128)S(1)}, f32[2,48,128]{2,1,0:T(8,128)S(1)}, u32[]{:S(2)}, u32[]{:S(2)}) collective-permute-start(f32[2,48,128]{2,1,0:T(8,128)S(1)} %get-tuple-element.20), channel_id=1, source_target_pairs={{0,1},{1,3},{2,0},{3,5},{4,2},{5,7},{6,4},{7,6},{8,9},{9,11},{10,8... | collective-permute-start | bytes 147464 | tf_op jit(solution)/shard_map/ppermute | solution.py:280
  2.1 4.8 %collective-permute-start.1 = (f32[2,48,128]{2,1,0:T(8,128)S(1)}, f32[2,48,128]{2,1,0:T(8,128)S(1)}, u32[]{:S(2)}, u32[]{:S(2)}) collective-permute-start(f32[2,48,128]{2,1,0:T(8,128)S(1)} %get-tuple-element.21), channel_id=1, source_target_pairs={{0,2},{1,0},{2,4},{3,1},{4,6},{5,3},{6,7},{7,5},{8,10},{9,8},{10,1... | collective-permute-start | bytes 147464 | tf_op jit(solution)/shard_map/ppermute | solution.py:281
  5.5 1.5 %copy-start.1 = (f32[2,1,128,128]{3,2,1,0:T(8,128)S(1)}, f32[2,1,128,128]{3,2,1,0:T(8,128)}, u32[]{:S(2)}) copy-start(f32[2,1,128,128]{3,2,1,0:T(8,128)} %param.6) | copy-start | bytes 393220
  7.3 2.3 %collective-permute-start.4 = (f32[2,40,128]{2,1,0:T(8,128)S(1)}, f32[2,40,128]{2,1,0:T(8,128)S(1)}, u32[]{:S(2)}, u32[]{:S(2)}) collective-permute-start(f32[2,40,128]{2,1,0:T(8,128)S(1)} %get-tuple-element.27), channel_id=1, source_target_pairs={{0,1},{1,0},{2,3},{3,2},{4,5},{5,4},{6,7},{7,6},{8,9},{9,8},{10,11... | collective-permute-start | bytes 122888 | tf_op jit(solution)/shard_map/ppermute | solution.py:314
  7.6 4.1 %collective-permute-start.3 = (f32[2,40,128]{2,1,0:T(8,128)S(1)}, f32[2,40,128]{2,1,0:T(8,128)S(1)}, u32[]{:S(2)}, u32[]{:S(2)}) collective-permute-start(f32[2,40,128]{2,1,0:T(8,128)S(1)} %get-tuple-element.27), channel_id=1, source_target_pairs={{0,8},{8,0},{16,24},{24,16},{1,9},{9,1},{17,25},{25,17},{2,10},{10... | collective-permute-start | bytes 122888 | tf_op jit(solution)/shard_map/ppermute | solution.py:318
  9.6 3.6 %collective-permute-start.5 = (f32[1,128]{1,0:T(1,128)S(1)}, f32[1,128]{1,0:T(1,128)S(1)}, u32[]{:S(2)}, u32[]{:S(2)}) collective-permute-start(f32[1,128]{1,0:T(1,128)S(1)} %fusion.4.rest_0_), channel_id=1, source_target_pairs={{0,16},{1,25},{8,24},{9,17},{16,0},{17,9},{24,8},{25,1},{2,18},{3,... | collective-permute-start | bytes 1544 | tf_op jit(solution)/shard_map/ppermute | solution.py:321
  11.2 2.0 %collective-permute-start.2 = (f32[2,40,128]{2,1,0:T(8,128)S(1)}, f32[2,40,128]{2,1,0:T(8,128)S(1)}, u32[]{:S(2)}, u32[]{:S(2)}) collective-permute-start(f32[2,40,128]{2,1,0:T(8,128)S(1)} %get-tuple-element.26), channel_id=1, source_target_pairs={{0,1},{1,0},{8,16},{9,17},{16,8},{17,9},{24,25},{25,24},{2,3},{3,2... | collective-permute-start | bytes 122888 | tf_op jit(solution)/shard_map/ppermute | solution.py:324
  13.2 1.1 %collective-permute-start.6 = (f32[1,128]{1,0:T(1,128)S(1)}, f32[1,128]{1,0:T(1,128)S(1)}, u32[]{:S(2)}, u32[]{:S(2)}) collective-permute-start(f32[1,128]{1,0:T(1,128)S(1)} %fusion.2.rest_1_), channel_id=1, source_target_pairs={{0,1},{1,0},{2,3},{3,2},{4,5},{5,4},{6,7},{7,6},{8,9},{9,8},{10,11... | collective-permute-start | bytes 1544 | tf_op jit(solution)/shard_map/ppermute | solution.py:341

commit v5 on v4

--- a/solution.py
+++ b/solution.py
@@ -100,23 +100,22 @@
 
 
 def pack_kernel(rim, wave_ref, one_ref, two_ref):
-    rows, width = wave_ref.shape[1], wave_ref.shape[2]
+    rows, width = wave_ref.shape
     span, groups = groups_of(rows, width, rim)
     odd = lax.axis_index("freq") % 2 == 1
-    lane = lax.broadcasted_iota(jnp.int32, one_ref.shape[1:], 1)
-    for part in range(2):
-        packed = []
-        for sign in (1, -1):
-            message = wave_ref[part, groups[0][0] : groups[0][1]]
-            for index, (low, high) in enumerate(groups[1:], 1):
-                count = high - low
-                place = lane[:count] if sign == 1 else width - 1 - lane[:count]
-                moved = pltpu.roll(wave_ref[part, low:high], sign * index * span % width, 1)
-                top = jnp.where(place // span == index, moved, message[:count])
-                message = top if count == message.shape[0] else jnp.concatenate([top, message[count:]], axis=0)
-            packed.append(message)
-        one_ref[part] = jnp.where(odd, packed[1], packed[0])
-        two_ref[part] = jnp.where(odd, packed[0], packed[1])
+    lane = lax.broadcasted_iota(jnp.int32, one_ref.shape, 1)
+    packed = []
+    for sign in (1, -1):
+        message = wave_ref[: groups[0][1]]
+        for index, (low, high) in enumerate(groups[1:], 1):
+            count = high - low
+            place = lane[:count] if sign == 1 else width - 1 - lane[:count]
+            moved = pltpu.roll(wave_ref[low:high], sign * index * span % width, 1)
+            top = jnp.where(place // span == index, moved, message[:count])
+            message = top if count == message.shape[0] else jnp.concatenate([top, message[count:]], axis=0)
+        packed.append(message)
+    one_ref[...] = jnp.where(odd, packed[1], packed[0])
+    two_ref[...] = jnp.where(odd, packed[0], packed[1])
 
 
 def rcv_operator_kernel(
@@ -150,23 +149,20 @@
 def receiver_kernel(rim, wave_ref, first_ref, second_ref, full_ref, high_ref, low_ref, sunk_ref, one_ref, two_ref, image_ref):
     rows, width = sunk_ref.shape[1], sunk_ref.shape[2]
     half = width // 2
-    span, groups = groups_of(rows, width, rim)
+    span, groups = groups_of(2 * rows, width, rim)
     odd = lax.axis_index("freq") % 2 == 1
-    extended = []
-    for part in range(2):
-        halos = []
-        first, second = first_ref[part], second_ref[part]
-        before = jnp.where(odd, first, second)
-        after = jnp.where(odd, second, first)
-        for index, (low, high) in enumerate(groups):
-            left, right = after[: high - low], before[: high - low]
-            if index:
-                left = pltpu.roll(left, -index * span % width, 1)
-                right = pltpu.roll(right, index * span % width, 1)
-            lane = lax.broadcasted_iota(jnp.int32, left.shape, 1)
-            halos.append(jnp.where(lane < half, left, right))
-        extended.append(jnp.concatenate([wave_ref[part], jnp.concatenate(halos, axis=0)], axis=1))
-    full = dot3(halves(jnp.concatenate(extended, axis=0)), (high_ref[...], low_ref[...]))
+    before = jnp.where(odd, first_ref[...], second_ref[...])
+    after = jnp.where(odd, second_ref[...], first_ref[...])
+    halos = []
+    for index, (low, high) in enumerate(groups):
+        left, right = after[: high - low], before[: high - low]
+        if index:
+            left = pltpu.roll(left, -index * span % width, 1)
+            right = pltpu.roll(right, index * span % width, 1)
+        lane = lax.broadcasted_iota(jnp.int32, left.shape, 1)
+        halos.append(jnp.where(lane < half, left, right))
+    extended = jnp.concatenate([wave_ref[...], jnp.concatenate(halos, axis=0)], axis=1)
+    full = dot3(halves(extended), (high_ref[...], low_ref[...]))
     real = full[:rows, :width] - full[rows:, width:]
     imag = full[:rows, width:] + full[rows:, :width]
     sunk_ref[0] = real
@@ -195,14 +191,12 @@
         two_ref[part] = jnp.where(up, head[part], tail[part])
 
 
-def source_kernel(field_ref, two_ref, one_ref, high_ref, low_ref, *rest):
+def source_kernel(field_ref, two_ref, one_ref, high_ref, low_ref, out_ref):
     rows, width = field_ref.shape[1], field_ref.shape[2]
     half = width // 2
     chunks = rows // width
     edge = one_ref.shape[1]
     up = lax.axis_index("src") % 2 == 0
-    *image_refs, out_ref, image_ref = rest
-    image_ref[...] = functools.reduce(jnp.add, [ref[...] for ref in image_refs])
     gap = jnp.zeros((half - edge, width), F32)
     for chunk in range(chunks):
         low, high = chunk * width, (chunk + 1) * width
@@ -222,6 +216,22 @@
         out_ref[1, low:high] = full[:width, width:] + full[width:, :width]
 
 
+def store_kernel(sunk_ref, two_ref, *rest):
+    *image_refs, sunk_hbm, image_hbm, image_ref, sems = rest
+    sunk_copy = pltpu.make_async_copy(sunk_ref, sunk_hbm, sems.at[0])
+    sunk_copy.start()
+    image = functools.reduce(jnp.add, [ref[...] for ref in image_refs])
+    if len(image_refs) > 1:
+        at, edge = lax.axis_index("src"), two_ref.shape[1]
+        from_two = jnp.where(at % 2 == 0, two_ref[0, :1], two_ref[0, edge - 1 :])
+        image = image + jnp.where(jnp.logical_and(at > 0, at < lax.axis_size("src") - 1), from_two, 0.0)
+    image_ref[...] = image
+    image_copy = pltpu.make_async_copy(image_ref, image_hbm, sems.at[1])
+    image_copy.start()
+    sunk_copy.wait()
+    image_copy.wait()
+
+
 def around(rcv, freq, sign):
     pairs = []
     for at in range(rcv):
@@ -244,6 +254,19 @@
     return pairs
 
 
+def far_pairs(freq):
+    pairs = []
+    for slot in range(0, freq, 2):
+        moves = {
+            (1, 0): (1, 1), (1, 1): (3, 0), (3, 0): (1, 0),
+            (0, 0): (2, 1), (2, 1): (2, 0), (2, 0): (0, 0),
+            (0, 1): (3, 1), (3, 1): (0, 1),
+        }
+        for (at, side), (to, to_side) in sorted(moves.items()):
+            pairs.append((at * freq + slot + side, to * freq + slot + to_side))
+    return pairs
+
+
 def body(wavefield, op_table, vel_index, interp_index, interp_weight, freq_perm):
     rows, width = wavefield.shape[2], wavefield.shape[3]
     n_src, n_rcv, n_freq = (lax.axis_size(axis) for axis in ("src", "rcv", "freq"))
@@ -252,7 +275,7 @@
     edge = -(-(rim + 1) // 8) * 8
     half = width // 2
     chunks = rows // width
-    wave = wavefield.reshape(2, rows, width)
+    wave = wavefield.reshape(2 * rows, width)
 
     vmem = pl.BlockSpec(memory_space=pltpu.VMEM)
     anywhere = pl.BlockSpec(memory_space=pltpu.HBM)
@@ -267,8 +290,8 @@
         ),
         op_table.transpose(2, 0, 1),
     ]
-    _, groups = groups_of(rows, width, rim)
-    packed = jax.ShapeDtypeStruct((2, groups[0][1], width), F32)
+    _, groups = groups_of(2 * rows, width, rim)
+    packed = jax.ShapeDtypeStruct((groups[0][1], width), F32)
     first, second = pl.pallas_call(
         functools.partial(pack_kernel, rim),
         out_shape=[packed, packed],
@@ -316,11 +339,10 @@
     else:
         image = lax.psum(image, "freq")
     one = lax.ppermute(one, "src", [(i, i + 1 if i % 2 == 0 else i - 1) for i in range(n_src)])
+    up = lax.axis_index("src") % 2 == 0
     if n_src == 4:
-        pairs = [(i * n_freq + f, (i ^ (2 + f % 2)) * n_freq + f) for i in range(n_src) for f in range(n_freq)]
-        far = lax.ppermute(image, ("src", "freq"), pairs)
-        if n_freq > 2:
-            far = jnp.where(lax.axis_index("freq") < 2, far, 0.0)
+        far = lax.ppermute(image, ("src", "freq"), far_pairs(n_freq))
+        two = lax.dynamic_update_slice(two, image[None], (0, jnp.where(up, edge - 1, 0), 0))
     two = lax.ppermute(two, ("src", "freq"), between(n_src, n_freq))
     one, found = lax.optimization_barrier((one, found))
     src_high, src_low = pl.pallas_call(
@@ -334,23 +356,35 @@
         name="src_operator",
     )(found)
     if n_src == 4:
-        up = lax.axis_index("src") % 2 == 0
+        at, slot = lax.axis_index("src"), lax.axis_index("freq")
         from_one = jnp.where(up, one[0, edge - 1 :], one[0, :1])
-        near, src_high = lax.optimization_barrier((from_one + far, src_high))
+        other = jnp.logical_or(jnp.logical_and(at == 1, slot == 1), jnp.logical_and(at == 2, slot == 0))
+        from_far = jnp.where(jnp.logical_or(other, slot > 1), 0.0, far)
+        near, src_high = lax.optimization_barrier((from_one + from_far, src_high))
         if n_freq == 2:
             images = [image, near, lax.ppermute(near, "freq", [(0, 1), (1, 0)])]
         else:
             images = [image, lax.psum(near, "freq")]
     else:
         images = [lax.psum(image, "src")]
+    sunk = pl.pallas_call(
+        source_kernel,
+        out_shape=jax.ShapeDtypeStruct((2, rows, width), F32),
+        in_specs=[vmem] * 5,
+        out_specs=vmem,
+        compiler_params=params,
+        cost_estimate=cost,
+        name="sources",
+    )(field, two, one, src_high, src_low)
     sunk, image = pl.pallas_call(
-        source_kernel,
+        store_kernel,
         out_shape=[jax.ShapeDtypeStruct((2, rows, width), F32), jax.ShapeDtypeStruct((1, width), F32)],
-        in_specs=[vmem] * (5 + len(images)),
-        out_specs=[vmem] * 2,
-        compiler_params=params,
-        name="sources",
-    )(field, two, one, src_high, src_low, *images)
+        in_specs=[vmem] * (2 + len(images)),
+        out_specs=[pl.BlockSpec(memory_space=pl.ANY)] * 2,
+        scratch_shapes=[pltpu.VMEM((1, width), F32), pltpu.SemaphoreType.DMA((2,))],
+        compiler_params=params,
+        name="store",
+    )(sunk, two, *images)
     return sunk.reshape(wavefield.shape), image.reshape(width)
 
 

time: 15.4 us -> 15.1 us (0.981)
  waiting for transfers between devices: 1.77 us -> 1.41 us
    ppermute x1, starting transfers between devices: 0.36 us -> 0.66 us  [body(): two = lax.ppermute(two, ('src', 'freq'), between(n_src, n_freq))]
    ppermute x1, waiting for transfers between devices: 1.11 us -> 0.83 us  [body(): images = [image, near, lax.ppermute(near, 'freq', [(0, 1), (1, 0)])]]
    ppermute x1, starting transfers between devices: 1.58 us -> 1.33 us  [body(): far = lax.ppermute(image, ('src', 'freq'), far_pairs(n_freq))]
    pallas_call x1 -> x2, Pallas kernels: 0.93 us -> 0.95 us  [the longest x1 0.67 us: body(): pl.pallas_call(store_kernel, out_shape=[jax.ShapeDtypeStruct((2, rows, wi...]
  transfers between devices with their start and end apart: 7 -> 7, of which waited for: 3 -> 3; matrix products, arithmetic and copies ran while one was open for 0% -> 0% of each run, Pallas kernels for 16% -> 19%
where the time goes in v5:
time: 15.1 us; the launch traced here: 14.9 us
  starting transfers between devices  7.24 us (48%)
  Pallas kernels  3.87 us (26%)
  between operations  1.42 us (9%)
  waiting for transfers between devices  1.41 us (9%)
  local copies, waits for them, and re-layouts  0.95 us (6%)
    ppermute x1, starting transfers between devices, body(): second = lax.ppermute(second, ('rcv', 'freq'), around(n_rcv, n_freq, 1))  2.6 us
    ppermute x1, starting transfers between devices, body(): lax.ppermute(one, 'src', [(i, i + 1 if i % 2 == 0 else i - 1) for i in ra...  1.94 us
    pallas_call x1, Pallas kernels, body(): pl.pallas_call(functools.partial(rcv_operator_kernel, lateral), out_shape...  1.49 us
    ppermute x1, starting transfers between devices, body(): far = lax.ppermute(image, ('src', 'freq'), far_pairs(n_freq))  1.33 us
    pallas_call x1, Pallas kernels, body(): pl.pallas_call(functools.partial(src_operator_kernel, lateral, op_table.s...  1 us
    unnamed x12, local copies, waits for them, and re-layouts  0.92 us
    ppermute x1, waiting for transfers between devices, body(): images = [image, near, lax.ppermute(near, 'freq', [(0, 1), (1, 0)])]  0.83 us
    pallas_call x1, Pallas kernels, body(): pl.pallas_call(store_kernel, out_shape=[jax.ShapeDtypeStruct((2, rows, wi...  0.67 us
  transfers between devices with their start and end apart: 7, of which 3 were waited for; matrix products, arithmetic and copies ran while one was open for 0% of the time, Pallas kernels for 19%

profile of v5, /device:TPU:0, one launch (start us, length us, event | category | flops | bytes accessed | tf_op | source)
XLA Modules:
  0.0 14.9 jit_solution(6011317006585540043)
XLA Ops:
  0.6 0.0 copy-start
  0.6 0.9 %copy-done = f32[2,1,128,128]{3,2,1,0:T(8,128)S(1)} copy-done((f32[2,1,128,128]{3,2,1,0:T(8,128)S(1)}, f32[2,1,128,128]{3,2,1,0:T(8,128)}, u32[]{:S(2)}) %copy-start) | copy-done | bytes 131096
  1.5 0.0 copy-start.4
  1.5 0.0 copy-start.5
  1.5 0.0 copy-start.3
  1.5 0.1 pack.1
  1.7 0.0 copy-start.2
  1.7 0.5 %collective-permute-start = (f32[88,128]{1,0:T(8,128)S(1)}, f32[88,128]{1,0:T(8,128)S(1)}, u32[]{:S(2)}, u32[]{:S(2)}) collective-permute-start(f32[88,128]{1,0:T(8,128)S(1)} %get-tuple-element.20), channel_id=1, source_target_pairs={{0,1},{1,3},{2,0},{3,5},{4,2},{5,7},{6,4},{7,6},{8,9},{9,11},{10,8... | collective-permute-start | bytes 135176 | tf_op jit(solution)/shard_map/ppermute | solution.py:303
  2.1 2.6 %collective-permute-start.1 = (f32[88,128]{1,0:T(8,128)S(1)}, f32[88,128]{1,0:T(8,128)S(1)}, u32[]{:S(2)}, u32[]{:S(2)}) collective-permute-start(f32[88,128]{1,0:T(8,128)S(1)} %get-tuple-element.21), channel_id=1, source_target_pairs={{0,2},{1,0},{2,4},{3,1},{4,6},{5,3},{6,7},{7,5},{8,10},{9,8},{10,1... | collective-permute-start | bytes 135176 | tf_op jit(solution)/shard_map/ppermute | solution.py:304
  4.7 0.0 copy-done.4
  4.7 0.0 copy-done.5
  5.4 0.0 copy-done.3
  5.4 0.0 copy-done.2
  5.5 0.0 copy-start.1
  5.5 1.5 %rcv_operator.1 = (f32[256,256]{1,0:T(8,128)S(1)}, bf16[256,256]{1,0:T(8,128)(2,1)S(1)}, bf16[256,256]{1,0:T(8,128)(2,1)S(1)}, f32[2,32,128]{2,1,0:T(8,128)S(1)}) custom-call(f32[6,128]{1,0:T(8,128)S(1)} %select_maximum_fusion.small_ref, f32[19,2,64]{2,1,0:T(2,128)S(1)} %bitcast.25), custom_call_target="tpu_custom_call" | custom-call | flops 1610612736 | bytes 1048576 | tf_op jit(solution)/shard_map/rcv_operator/pallas_call | solution.py:307
  7.0 0.0 collective-permute-done.first_ref
  7.0 0.0 collective-permute-done.1.second_ref
  7.0 0.0 copy-done.1
  7.0 0.3 %receivers.1 = (f32[2,128,128]{2,1,0:T(8,128)S(1)}, f32[2,40,128]{2,1,0:T(8,128)S(1)}, f32[2,40,128]{2,1,0:T(8,128)S(1)}, f32[1,128]{1,0:T(1,128)S(1)}) custom-call(f32[256,128]{1,0:T(8,128)S(1)} %bitcast.23, f32[88,128]{1,0:T(8,128)S(1)} %collective-permute-done.first_ref, f32[88,128]{1,0:T(8,128)S(1)} %collective-permute-done.1.second_ref, ...), custom_call_target="tpu_custom_call" | custom-call | tf_op jit(solution)/shard_map/receivers/pallas_call | solution.py:322
  7.3 0.2 %collective-permute-start.2 = (f32[2,40,128]{2,1,0:T(8,128)S(1)}, f32[2,40,128]{2,1,0:T(8,128)S(1)}, u32[]{:S(2)}, u32[]{:S(2)}) collective-permute-start(f32[2,40,128]{2,1,0:T(8,128)S(1)} %get-tuple-element.28), channel_id=1, source_target_pairs={{0,1},{1,0},{2,3},{3,2},{4,5},{5,4},{6,7},{7,6},{8,9},{9,8},{10,11... | collective-permute-start | bytes 122888 | tf_op jit(solution)/shard_map/ppermute | solution.py:337
  7.6 1.9 %collective-permute-start.4 = (f32[2,40,128]{2,1,0:T(8,128)S(1)}, f32[2,40,128]{2,1,0:T(8,128)S(1)}, u32[]{:S(2)}, u32[]{:S(2)}) collective-permute-start(f32[2,40,128]{2,1,0:T(8,128)S(1)} %get-tuple-element.28), channel_id=1, source_target_pairs={{0,8},{8,0},{16,24},{24,16},{1,9},{9,1},{17,25},{25,17},{2,10},{10... | collective-permute-start | bytes 122888 | tf_op jit(solution)/shard_map/ppermute | solution.py:341
  9.5 0.0 collective-permute-done.2
  9.5 1.3 %collective-permute-start.5 = (f32[1,128]{1,0:T(1,128)S(1)}, f32[1,128]{1,0:T(1,128)S(1)}, u32[]{:S(2)}, u32[]{:S(2)}) collective-permute-start(f32[1,128]{1,0:T(1,128)S(1)} %fusion.2.rest_0_), channel_id=1, source_target_pairs={{0,17},{1,25},{8,9},{9,24},{16,0},{17,16},{24,8},{25,1},{2,19},{3,... | collective-permute-start | bytes 1544 | tf_op jit(solution)/shard_map/ppermute | solution.py:344
  10.9 0.7 %collective-permute-start.3 = (f32[2,40,128]{2,1,0:T(8,128)S(1)}, f32[2,40,128]{2,1,0:T(8,128)S(1)}, u32[]{:S(2)}, u32[]{:S(2)}) collective-permute-start(f32[2,40,128]{2,1,0:T(8,128)S(1)} %dynamic_update_slice.3), channel_id=1, source_target_pairs={{0,1},{1,0},{8,16},{9,17},{16,8},{17,9},{24,25},{25,24},{2,3},{3,2... | collective-permute-start | bytes 122888 | tf_op jit(solution)/shard_map/ppermute | solution.py:346
  11.5 0.1 collective-permute-done.4.one_ref
  11.6 1.0 %src_operator.1 = (bf16[1,256,256]{2,1,0:T(8,128)(2,1)S(1)}, bf16[1,256,256]{2,1,0:T(8,128)(2,1)S(1)}) custom-call(f32[2,32,128]{2,1,0:T(8,128)S(1)} %get-tuple-element.31.found_ref), custom_call_target="tpu_custom_call" | custom-call | flops 1048576 | bytes 1024 | tf_op jit(solution)/shard_map/src_operator/pallas_call | solution.py:348
  12.6 0.5 %collective-permute-done.5 = f32[1,128]{1,0:T(1,128)S(1)} collective-permute-done((f32[1,128]{1,0:T(1,128)S(1)}, f32[1,128]{1,0:T(1,128)S(1)}, u32[]{:S(2)}, u32[]{:S(2)}) %collective-permute-start.5) | collective-permute-done | bytes 544 | tf_op jit(solution)/shard_map/ppermute | solution.py:344
  13.1 0.0 collective-permute-start.6
  13.1 0.0 collective-permute-done.3.two_ref
  13.1 0.3 %sources.1.sunk_ref = f32[2,128,128]{2,1,0:T(8,128)S(1)} custom-call(f32[2,128,128]{2,1,0:T(8,128)S(1)} %get-tuple-element.25.field_ref, f32[2,40,128]{2,1,0:T(8,128)S(1)} %collective-permute-done.3.two_ref, f32[2,40,128]{2,1,0:T(8,128)S(1)} %collective-permute-done.4.one_ref, bf16[1,256,256]{2,1,0:T(8,128)(2,1)S(1)} %get-tuple-element.33.high_ref, ...), custom_call_target="tpu_custom_call" | custom-call | flops 1610612736 | bytes 1048576 | tf_op jit(solution)/shard_map/sources/pallas_call | solution.py:370
  13.4 0.8 %collective-permute-done.6.rest_2_ = f32[1,128]{1,0:T(1,128)S(1)} collective-permute-done((f32[1,128]{1,0:T(1,128)S(1)}, f32[1,128]{1,0:T(1,128)S(1)}, u32[]{:S(2)}, u32[]{:S(2)}) %collective-permute-start.6) | collective-permute-done | bytes 544 | tf_op jit(solution)/shard_map/ppermute | solution.py:365
  14.2 0.7 %store.1 = (f32[2,128,128]{2,1,0:T(8,128)}, f32[1,128]{1,0:T(1,128)}) custom-call(f32[2,128,128]{2,1,0:T(8,128)S(1)} %sources.1.sunk_ref, f32[2,40,128]{2,1,0:T(8,128)S(1)} %collective-permute-done.3.two_ref, f32[1,128]{1,0:T(1,128)S(1)} %fusion.2.rest_0_, f32[1,128]{1,0:T(1,128)S(1)} %fusion.4.rest_1_, f32[1,128]{1,0:T(1,128)S(1)} %collective-permute-done.6.rest_2_), custom_call_target="tpu_custom_call" | custom-call | tf_op jit(solution)/shard_map/store/pallas_call | solution.py:379
  (7 shorter events, 0.1 us)
Async XLA Ops:
  0.6 0.9 %copy-start = (f32[2,1,128,128]{3,2,1,0:T(8,128)S(1)}, f32[2,1,128,128]{3,2,1,0:T(8,128)}, u32[]{:S(2)}) copy-start(f32[2,1,128,128]{3,2,1,0:T(8,128)} %param.6) | copy-start | bytes 393220
  1.5 3.2 %copy-start.4 = (s32[16,2]{0,1:T(2,128)S(1)}, s32[16,2]{0,1:T(2,128)}, u32[]{:S(2)}) copy-start(s32[16,2]{0,1:T(2,128)} %param.9) | copy-start | bytes 388
  1.5 3.2 %copy-start.5 = (s32[32]{0:T(128)S(1)}, s32[32]{0:T(128)}, u32[]{:S(2)}) copy-start(s32[32]{0:T(128)} %param.8) | copy-start | bytes 388
  1.5 3.9 %copy-start.3 = (f32[16,2]{0,1:T(2,128)S(1)}, f32[16,2]{0,1:T(2,128)}, u32[]{:S(2)}) copy-start(f32[16,2]{0,1:T(2,128)} %param.10) | copy-start | bytes 388
  1.7 3.8 %copy-start.2 = (f32[2,64,19]{1,0,2:T(2,128)S(1)}, f32[2,64,19]{1,0,2:T(2,128)}, u32[]{:S(2)}) copy-start(f32[2,64,19]{1,0,2:T(2,128)} %param.7) | copy-start | bytes 29188
  1.7 5.3 %collective-permute-start = (f32[88,128]{1,0:T(8,128)S(1)}, f32[88,128]{1,0:T(8,128)S(1)}, u32[]{:S(2)}, u32[]{:S(2)}) collective-permute-start(f32[88,128]{1,0:T(8,128)S(1)} %get-tuple-element.20), channel_id=1, source_target_pairs={{0,1},{1,3},{2,0},{3,5},{4,2},{5,7},{6,4},{7,6},{8,9},{9,11},{10,8... | collective-permute-start | bytes 135176 | tf_op jit(solution)/shard_map/ppermute | solution.py:303
  2.1 4.8 %collective-permute-start.1 = (f32[88,128]{1,0:T(8,128)S(1)}, f32[88,128]{1,0:T(8,128)S(1)}, u32[]{:S(2)}, u32[]{:S(2)}) collective-permute-start(f32[88,128]{1,0:T(8,128)S(1)} %get-tuple-element.21), channel_id=1, source_target_pairs={{0,2},{1,0},{2,4},{3,1},{4,6},{5,3},{6,7},{7,5},{8,10},{9,8},{10,1... | collective-permute-start | bytes 135176 | tf_op jit(solution)/shard_map/ppermute | solution.py:304
  5.5 1.5 %copy-start.1 = (f32[2,1,128,128]{3,2,1,0:T(8,128)S(1)}, f32[2,1,128,128]{3,2,1,0:T(8,128)}, u32[]{:S(2)}) copy-start(f32[2,1,128,128]{3,2,1,0:T(8,128)} %param.6) | copy-start | bytes 393220
  7.3 2.2 %collective-permute-start.2 = (f32[2,40,128]{2,1,0:T(8,128)S(1)}, f32[2,40,128]{2,1,0:T(8,128)S(1)}, u32[]{:S(2)}, u32[]{:S(2)}) collective-permute-start(f32[2,40,128]{2,1,0:T(8,128)S(1)} %get-tuple-element.28), channel_id=1, source_target_pairs={{0,1},{1,0},{2,3},{3,2},{4,5},{5,4},{6,7},{7,6},{8,9},{9,8},{10,11... | collective-permute-start | bytes 122888 | tf_op jit(solution)/shard_map/ppermute | solution.py:337
  7.6 4.1 %collective-permute-start.4 = (f32[2,40,128]{2,1,0:T(8,128)S(1)}, f32[2,40,128]{2,1,0:T(8,128)S(1)}, u32[]{:S(2)}, u32[]{:S(2)}) collective-permute-start(f32[2,40,128]{2,1,0:T(8,128)S(1)} %get-tuple-element.28), channel_id=1, source_target_pairs={{0,8},{8,0},{16,24},{24,16},{1,9},{9,1},{17,25},{25,17},{2,10},{10... | collective-permute-start | bytes 122888 | tf_op jit(solution)/shard_map/ppermute | solution.py:341
  9.5 3.6 %collective-permute-start.5 = (f32[1,128]{1,0:T(1,128)S(1)}, f32[1,128]{1,0:T(1,128)S(1)}, u32[]{:S(2)}, u32[]{:S(2)}) collective-permute-start(f32[1,128]{1,0:T(1,128)S(1)} %fusion.2.rest_0_), channel_id=1, source_target_pairs={{0,17},{1,25},{8,9},{9,24},{16,0},{17,16},{24,8},{25,1},{2,19},{3,... | collective-permute-start | bytes 1544 | tf_op jit(solution)/shard_map/ppermute | solution.py:344
  10.9 2.3 %collective-permute-start.3 = (f32[2,40,128]{2,1,0:T(8,128)S(1)}, f32[2,40,128]{2,1,0:T(8,128)S(1)}, u32[]{:S(2)}, u32[]{:S(2)}) collective-permute-start(f32[2,40,128]{2,1,0:T(8,128)S(1)} %dynamic_update_slice.3), channel_id=1, source_target_pairs={{0,1},{1,0},{8,16},{9,17},{16,8},{17,9},{24,25},{25,24},{2,3},{3,2... | collective-permute-start | bytes 122888 | tf_op jit(solution)/shard_map/ppermute | solution.py:346
  13.1 1.1 %collective-permute-start.6 = (f32[1,128]{1,0:T(1,128)S(1)}, f32[1,128]{1,0:T(1,128)S(1)}, u32[]{:S(2)}, u32[]{:S(2)}) collective-permute-start(f32[1,128]{1,0:T(1,128)S(1)} %fusion.4.rest_1_), channel_id=1, source_target_pairs={{0,1},{1,0},{2,3},{3,2},{4,5},{5,4},{6,7},{7,6},{8,9},{9,8},{10,11... | collective-permute-start | bytes 1544 | tf_op jit(solution)/shard_map/ppermute | solution.py:365

commit v6 on v5

--- a/solution.py
+++ b/solution.py
@@ -259,7 +259,7 @@
     for slot in range(0, freq, 2):
         moves = {
             (1, 0): (1, 1), (1, 1): (3, 0), (3, 0): (1, 0),
-            (0, 0): (2, 1), (2, 1): (2, 0), (2, 0): (0, 0),
+            (0, 0): (2, 0), (2, 0): (2, 1), (2, 1): (0, 0),
             (0, 1): (3, 1), (3, 1): (0, 1),
         }
         for (at, side), (to, to_side) in sorted(moves.items()):
@@ -358,7 +358,7 @@
     if n_src == 4:
         at, slot = lax.axis_index("src"), lax.axis_index("freq")
         from_one = jnp.where(up, one[0, edge - 1 :], one[0, :1])
-        other = jnp.logical_or(jnp.logical_and(at == 1, slot == 1), jnp.logical_and(at == 2, slot == 0))
+        other = jnp.logical_or(jnp.logical_and(at == 1, slot == 1), jnp.logical_and(at == 2, slot == 1))
         from_far = jnp.where(jnp.logical_or(other, slot > 1), 0.0, far)
         near, src_high = lax.optimization_barrier((from_one + from_far, src_high))
         if n_freq == 2:

time: 15.1 us -> 14.7 us (0.974)
  waiting for transfers between devices: 1.41 us -> 0.66 us
  starting transfers between devices: 7.24 us -> 7.6 us
    ppermute x1, waiting for transfers between devices: 0.48 us -> 0.01 us  [body(): far = lax.ppermute(image, ('src', 'freq'), far_pairs(n_freq))]
    ppermute x1, starting transfers between devices: 0.01 us -> 0.36 us  [body(): images = [image, near, lax.ppermute(near, 'freq', [(0, 1), (1, 0)])]]
    ppermute x1, waiting for transfers between devices: 0.83 us -> 0.55 us  [body(): images = [image, near, lax.ppermute(near, 'freq', [(0, 1), (1, 0)])]]
    ppermute x1, starting transfers between devices: 1.33 us -> 1.58 us  [body(): far = lax.ppermute(image, ('src', 'freq'), far_pairs(n_freq))]
    ppermute x1, starting transfers between devices: 0.66 us -> 0.41 us  [body(): two = lax.ppermute(two, ('src', 'freq'), between(n_src, n_freq))]
  transfers between devices with their start and end apart: 7 -> 7, of which waited for: 3 -> 2; matrix products, arithmetic and copies ran while one was open for 0% -> 0% of each run, Pallas kernels for 19% -> 19%
where the time goes in v6:
time: 14.7 us; the launch traced here: 14.5 us
  starting transfers between devices  7.6 us (52%)
  Pallas kernels  3.87 us (26%)
  between operations  1.42 us (10%)
  local copies, waits for them, and re-layouts  0.95 us (6%)
  waiting for transfers between devices  0.66 us (4%)
    ppermute x1, starting transfers between devices, body(): second = lax.ppermute(second, ('rcv', 'freq'), around(n_rcv, n_freq, 1))  2.6 us
    ppermute x1, starting transfers between devices, body(): lax.ppermute(one, 'src', [(i, i + 1 if i % 2 == 0 else i - 1) for i in ra...  1.94 us
    ppermute x1, starting transfers between devices, body(): far = lax.ppermute(image, ('src', 'freq'), far_pairs(n_freq))  1.58 us
    pallas_call x1, Pallas kernels, body(): pl.pallas_call(functools.partial(rcv_operator_kernel, lateral), out_shape...  1.49 us
    pallas_call x1, Pallas kernels, body(): pl.pallas_call(functools.partial(src_operator_kernel, lateral, op_table.s...  1 us
    unnamed x12, local copies, waits for them, and re-layouts  0.92 us
    pallas_call x1, Pallas kernels, body(): pl.pallas_call(store_kernel, out_shape=[jax.ShapeDtypeStruct((2, rows, wi...  0.67 us
    ppermute x1, waiting for transfers between devices, body(): images = [image, near, lax.ppermute(near, 'freq', [(0, 1), (1, 0)])]  0.55 us
  transfers between devices with their start and end apart: 7, of which 2 were waited for; matrix products, arithmetic and copies ran while one was open for 0% of the time, Pallas kernels for 19%

profile of v6, /device:TPU:0, one launch (start us, length us, event | category | flops | bytes accessed | tf_op | source)
XLA Modules:
  0.0 14.5 jit_solution(9589922696123621202)
XLA Ops:
  0.6 0.0 copy-start
  0.6 0.9 %copy-done = f32[2,1,128,128]{3,2,1,0:T(8,128)S(1)} copy-done((f32[2,1,128,128]{3,2,1,0:T(8,128)S(1)}, f32[2,1,128,128]{3,2,1,0:T(8,128)}, u32[]{:S(2)}) %copy-start) | copy-done | bytes 131096
  1.5 0.0 copy-start.4
  1.5 0.0 copy-start.5
  1.5 0.0 copy-start.3
  1.5 0.1 pack.1
  1.7 0.0 copy-start.2
  1.7 0.5 %collective-permute-start = (f32[88,128]{1,0:T(8,128)S(1)}, f32[88,128]{1,0:T(8,128)S(1)}, u32[]{:S(2)}, u32[]{:S(2)}) collective-permute-start(f32[88,128]{1,0:T(8,128)S(1)} %get-tuple-element.20), channel_id=1, source_target_pairs={{0,1},{1,3},{2,0},{3,5},{4,2},{5,7},{6,4},{7,6},{8,9},{9,11},{10,8... | collective-permute-start | bytes 135176 | tf_op jit(solution)/shard_map/ppermute | solution.py:303
  2.1 2.6 %collective-permute-start.1 = (f32[88,128]{1,0:T(8,128)S(1)}, f32[88,128]{1,0:T(8,128)S(1)}, u32[]{:S(2)}, u32[]{:S(2)}) collective-permute-start(f32[88,128]{1,0:T(8,128)S(1)} %get-tuple-element.21), channel_id=1, source_target_pairs={{0,2},{1,0},{2,4},{3,1},{4,6},{5,3},{6,7},{7,5},{8,10},{9,8},{10,1... | collective-permute-start | bytes 135176 | tf_op jit(solution)/shard_map/ppermute | solution.py:304
  4.7 0.0 copy-done.4
  4.7 0.0 copy-done.5
  5.4 0.0 copy-done.3
  5.4 0.0 copy-done.2
  5.5 0.0 copy-start.1
  5.5 1.5 %rcv_operator.1 = (f32[256,256]{1,0:T(8,128)S(1)}, bf16[256,256]{1,0:T(8,128)(2,1)S(1)}, bf16[256,256]{1,0:T(8,128)(2,1)S(1)}, f32[2,32,128]{2,1,0:T(8,128)S(1)}) custom-call(f32[6,128]{1,0:T(8,128)S(1)} %select_maximum_fusion.small_ref, f32[19,2,64]{2,1,0:T(2,128)S(1)} %bitcast.25), custom_call_target="tpu_custom_call" | custom-call | flops 1610612736 | bytes 1048576 | tf_op jit(solution)/shard_map/rcv_operator/pallas_call | solution.py:307
  7.0 0.0 collective-permute-done.first_ref
  7.0 0.0 collective-permute-done.1.second_ref
  7.0 0.0 copy-done.1
  7.0 0.3 %receivers.1 = (f32[2,128,128]{2,1,0:T(8,128)S(1)}, f32[2,40,128]{2,1,0:T(8,128)S(1)}, f32[2,40,128]{2,1,0:T(8,128)S(1)}, f32[1,128]{1,0:T(1,128)S(1)}) custom-call(f32[256,128]{1,0:T(8,128)S(1)} %bitcast.23, f32[88,128]{1,0:T(8,128)S(1)} %collective-permute-done.first_ref, f32[88,128]{1,0:T(8,128)S(1)} %collective-permute-done.1.second_ref, ...), custom_call_target="tpu_custom_call" | custom-call | tf_op jit(solution)/shard_map/receivers/pallas_call | solution.py:322
  7.3 0.2 %collective-permute-start.2 = (f32[2,40,128]{2,1,0:T(8,128)S(1)}, f32[2,40,128]{2,1,0:T(8,128)S(1)}, u32[]{:S(2)}, u32[]{:S(2)}) collective-permute-start(f32[2,40,128]{2,1,0:T(8,128)S(1)} %get-tuple-element.28), channel_id=1, source_target_pairs={{0,1},{1,0},{2,3},{3,2},{4,5},{5,4},{6,7},{7,6},{8,9},{9,8},{10,11... | collective-permute-start | bytes 122888 | tf_op jit(solution)/shard_map/ppermute | solution.py:337
  7.6 1.9 %collective-permute-start.4 = (f32[2,40,128]{2,1,0:T(8,128)S(1)}, f32[2,40,128]{2,1,0:T(8,128)S(1)}, u32[]{:S(2)}, u32[]{:S(2)}) collective-permute-start(f32[2,40,128]{2,1,0:T(8,128)S(1)} %get-tuple-element.28), channel_id=1, source_target_pairs={{0,8},{8,0},{16,24},{24,16},{1,9},{9,1},{17,25},{25,17},{2,10},{10... | collective-permute-start | bytes 122888 | tf_op jit(solution)/shard_map/ppermute | solution.py:341
  9.5 0.0 collective-permute-done.2
  9.5 1.6 %collective-permute-start.5 = (f32[1,128]{1,0:T(1,128)S(1)}, f32[1,128]{1,0:T(1,128)S(1)}, u32[]{:S(2)}, u32[]{:S(2)}) collective-permute-start(f32[1,128]{1,0:T(1,128)S(1)} %fusion.2.rest_0_), channel_id=1, source_target_pairs={{0,16},{1,25},{8,9},{9,24},{16,17},{17,0},{24,8},{25,1},{2,18},{3,... | collective-permute-start | bytes 1544 | tf_op jit(solution)/shard_map/ppermute | solution.py:344
  11.1 0.4 %collective-permute-start.3 = (f32[2,40,128]{2,1,0:T(8,128)S(1)}, f32[2,40,128]{2,1,0:T(8,128)S(1)}, u32[]{:S(2)}, u32[]{:S(2)}) collective-permute-start(f32[2,40,128]{2,1,0:T(8,128)S(1)} %dynamic_update_slice.3), channel_id=1, source_target_pairs={{0,1},{1,0},{8,16},{9,17},{16,8},{17,9},{24,25},{25,24},{2,3},{3,2... | collective-permute-start | bytes 122888 | tf_op jit(solution)/shard_map/ppermute | solution.py:346
  11.5 0.1 collective-permute-done.4.one_ref
  11.6 1.0 %src_operator.1 = (bf16[1,256,256]{2,1,0:T(8,128)(2,1)S(1)}, bf16[1,256,256]{2,1,0:T(8,128)(2,1)S(1)}) custom-call(f32[2,32,128]{2,1,0:T(8,128)S(1)} %get-tuple-element.31.found_ref), custom_call_target="tpu_custom_call" | custom-call | flops 1048576 | bytes 1024 | tf_op jit(solution)/shard_map/src_operator/pallas_call | solution.py:348
  12.6 0.0 collective-permute-done.5
  12.7 0.4 %collective-permute-start.6 = (f32[1,128]{1,0:T(1,128)S(1)}, f32[1,128]{1,0:T(1,128)S(1)}, u32[]{:S(2)}, u32[]{:S(2)}) collective-permute-start(f32[1,128]{1,0:T(1,128)S(1)} %fusion.4.rest_1_), channel_id=1, source_target_pairs={{0,1},{1,0},{2,3},{3,2},{4,5},{5,4},{6,7},{7,6},{8,9},{9,8},{10,11... | collective-permute-start | bytes 1544 | tf_op jit(solution)/shard_map/ppermute | solution.py:365
  13.0 0.0 collective-permute-done.3.two_ref
  13.0 0.3 %sources.1.sunk_ref = f32[2,128,128]{2,1,0:T(8,128)S(1)} custom-call(f32[2,128,128]{2,1,0:T(8,128)S(1)} %get-tuple-element.25.field_ref, f32[2,40,128]{2,1,0:T(8,128)S(1)} %collective-permute-done.3.two_ref, f32[2,40,128]{2,1,0:T(8,128)S(1)} %collective-permute-done.4.one_ref, bf16[1,256,256]{2,1,0:T(8,128)(2,1)S(1)} %get-tuple-element.33.high_ref, ...), custom_call_target="tpu_custom_call" | custom-call | flops 1610612736 | bytes 1048576 | tf_op jit(solution)/shard_map/sources/pallas_call | solution.py:370
  13.3 0.6 %collective-permute-done.6.rest_2_ = f32[1,128]{1,0:T(1,128)S(1)} collective-permute-done((f32[1,128]{1,0:T(1,128)S(1)}, f32[1,128]{1,0:T(1,128)S(1)}, u32[]{:S(2)}, u32[]{:S(2)}) %collective-permute-start.6) | collective-permute-done | bytes 544 | tf_op jit(solution)/shard_map/ppermute | solution.py:365
  13.9 0.7 %store.1 = (f32[2,128,128]{2,1,0:T(8,128)}, f32[1,128]{1,0:T(1,128)}) custom-call(f32[2,128,128]{2,1,0:T(8,128)S(1)} %sources.1.sunk_ref, f32[2,40,128]{2,1,0:T(8,128)S(1)} %collective-permute-done.3.two_ref, f32[1,128]{1,0:T(1,128)S(1)} %fusion.2.rest_0_, f32[1,128]{1,0:T(1,128)S(1)} %fusion.4.rest_1_, f32[1,128]{1,0:T(1,128)S(1)} %collective-permute-done.6.rest_2_), custom_call_target="tpu_custom_call" | custom-call | tf_op jit(solution)/shard_map/store/pallas_call | solution.py:379
  (7 shorter events, 0.1 us)
Async XLA Ops:
  0.6 0.9 %copy-start = (f32[2,1,128,128]{3,2,1,0:T(8,128)S(1)}, f32[2,1,128,128]{3,2,1,0:T(8,128)}, u32[]{:S(2)}) copy-start(f32[2,1,128,128]{3,2,1,0:T(8,128)} %param.6) | copy-start | bytes 393220
  1.5 3.2 %copy-start.4 = (s32[16,2]{0,1:T(2,128)S(1)}, s32[16,2]{0,1:T(2,128)}, u32[]{:S(2)}) copy-start(s32[16,2]{0,1:T(2,128)} %param.9) | copy-start | bytes 388
  1.5 3.2 %copy-start.5 = (s32[32]{0:T(128)S(1)}, s32[32]{0:T(128)}, u32[]{:S(2)}) copy-start(s32[32]{0:T(128)} %param.8) | copy-start | bytes 388
  1.5 3.9 %copy-start.3 = (f32[16,2]{0,1:T(2,128)S(1)}, f32[16,2]{0,1:T(2,128)}, u32[]{:S(2)}) copy-start(f32[16,2]{0,1:T(2,128)} %param.10) | copy-start | bytes 388
  1.7 3.8 %copy-start.2 = (f32[2,64,19]{1,0,2:T(2,128)S(1)}, f32[2,64,19]{1,0,2:T(2,128)}, u32[]{:S(2)}) copy-start(f32[2,64,19]{1,0,2:T(2,128)} %param.7) | copy-start | bytes 29188
  1.7 5.3 %collective-permute-start = (f32[88,128]{1,0:T(8,128)S(1)}, f32[88,128]{1,0:T(8,128)S(1)}, u32[]{:S(2)}, u32[]{:S(2)}) collective-permute-start(f32[88,128]{1,0:T(8,128)S(1)} %get-tuple-element.20), channel_id=1, source_target_pairs={{0,1},{1,3},{2,0},{3,5},{4,2},{5,7},{6,4},{7,6},{8,9},{9,11},{10,8... | collective-permute-start | bytes 135176 | tf_op jit(solution)/shard_map/ppermute | solution.py:303
  2.1 4.8 %collective-permute-start.1 = (f32[88,128]{1,0:T(8,128)S(1)}, f32[88,128]{1,0:T(8,128)S(1)}, u32[]{:S(2)}, u32[]{:S(2)}) collective-permute-start(f32[88,128]{1,0:T(8,128)S(1)} %get-tuple-element.21), channel_id=1, source_target_pairs={{0,2},{1,0},{2,4},{3,1},{4,6},{5,3},{6,7},{7,5},{8,10},{9,8},{10,1... | collective-permute-start | bytes 135176 | tf_op jit(solution)/shard_map/ppermute | solution.py:304
  5.5 1.5 %copy-start.1 = (f32[2,1,128,128]{3,2,1,0:T(8,128)S(1)}, f32[2,1,128,128]{3,2,1,0:T(8,128)}, u32[]{:S(2)}) copy-start(f32[2,1,128,128]{3,2,1,0:T(8,128)} %param.6) | copy-start | bytes 393220
  7.3 2.2 %collective-permute-start.2 = (f32[2,40,128]{2,1,0:T(8,128)S(1)}, f32[2,40,128]{2,1,0:T(8,128)S(1)}, u32[]{:S(2)}, u32[]{:S(2)}) collective-permute-start(f32[2,40,128]{2,1,0:T(8,128)S(1)} %get-tuple-element.28), channel_id=1, source_target_pairs={{0,1},{1,0},{2,3},{3,2},{4,5},{5,4},{6,7},{7,6},{8,9},{9,8},{10,11... | collective-permute-start | bytes 122888 | tf_op jit(solution)/shard_map/ppermute | solution.py:337
  7.6 4.1 %collective-permute-start.4 = (f32[2,40,128]{2,1,0:T(8,128)S(1)}, f32[2,40,128]{2,1,0:T(8,128)S(1)}, u32[]{:S(2)}, u32[]{:S(2)}) collective-permute-start(f32[2,40,128]{2,1,0:T(8,128)S(1)} %get-tuple-element.28), channel_id=1, source_target_pairs={{0,8},{8,0},{16,24},{24,16},{1,9},{9,1},{17,25},{25,17},{2,10},{10... | collective-permute-start | bytes 122888 | tf_op jit(solution)/shard_map/ppermute | solution.py:341
  9.5 3.1 %collective-permute-start.5 = (f32[1,128]{1,0:T(1,128)S(1)}, f32[1,128]{1,0:T(1,128)S(1)}, u32[]{:S(2)}, u32[]{:S(2)}) collective-permute-start(f32[1,128]{1,0:T(1,128)S(1)} %fusion.2.rest_0_), channel_id=1, source_target_pairs={{0,16},{1,25},{8,9},{9,24},{16,17},{17,0},{24,8},{25,1},{2,18},{3,... | collective-permute-start | bytes 1544 | tf_op jit(solution)/shard_map/ppermute | solution.py:344
  11.1 1.9 %collective-permute-start.3 = (f32[2,40,128]{2,1,0:T(8,128)S(1)}, f32[2,40,128]{2,1,0:T(8,128)S(1)}, u32[]{:S(2)}, u32[]{:S(2)}) collective-permute-start(f32[2,40,128]{2,1,0:T(8,128)S(1)} %dynamic_update_slice.3), channel_id=1, source_target_pairs={{0,1},{1,0},{8,16},{9,17},{16,8},{17,9},{24,25},{25,24},{2,3},{3,2... | collective-permute-start | bytes 122888 | tf_op jit(solution)/shard_map/ppermute | solution.py:346
  12.7 1.2 %collective-permute-start.6 = (f32[1,128]{1,0:T(1,128)S(1)}, f32[1,128]{1,0:T(1,128)S(1)}, u32[]{:S(2)}, u32[]{:S(2)}) collective-permute-start(f32[1,128]{1,0:T(1,128)S(1)} %fusion.4.rest_1_), channel_id=1, source_target_pairs={{0,1},{1,0},{2,3},{3,2},{4,5},{5,4},{6,7},{7,6},{8,9},{9,8},{10,11... | collective-permute-start | bytes 1544 | tf_op jit(solution)/shard_map/ppermute | solution.py:365

commit v7 on v6

--- a/solution.py
+++ b/solution.py
@@ -191,13 +191,12 @@
         two_ref[part] = jnp.where(up, head[part], tail[part])
 
 
-def source_kernel(field_ref, two_ref, one_ref, high_ref, low_ref, out_ref):
+def inner_kernel(field_ref, one_ref, high_ref, low_ref, out_ref, part_ref):
     rows, width = field_ref.shape[1], field_ref.shape[2]
     half = width // 2
     chunks = rows // width
-    edge = one_ref.shape[1]
     up = lax.axis_index("src") % 2 == 0
-    gap = jnp.zeros((half - edge, width), F32)
+    gap = jnp.zeros((half - one_ref.shape[1], width), F32)
     for chunk in range(chunks):
         low, high = chunk * width, (chunk + 1) * width
         extended = []
@@ -205,30 +204,62 @@
             if chunk + 1 < chunks:
                 after = field_ref[part, high : high + half]
             else:
-                after = jnp.concatenate([jnp.where(up, one_ref[part], two_ref[part]), gap], axis=0)
+                after = jnp.concatenate([jnp.where(up, one_ref[part], 0.0), gap], axis=0)
             if chunk > 0:
                 before = field_ref[part, low - half : low]
             else:
-                before = jnp.concatenate([gap, jnp.where(up, two_ref[part], one_ref[part])], axis=0)
+                before = jnp.concatenate([gap, jnp.where(up, 0.0, one_ref[part])], axis=0)
             extended.append(jnp.concatenate([field_ref[part, low:high], after, before], axis=0))
         full = dot3((high_ref[chunk], low_ref[chunk]), halves(jnp.concatenate(extended, axis=1)))
+        part_ref[chunk] = full
         out_ref[0, low:high] = full[:width, :width] - full[width:, width:]
         out_ref[1, low:high] = full[:width, width:] + full[width:, :width]
 
 
-def store_kernel(sunk_ref, two_ref, *rest):
-    *image_refs, sunk_hbm, image_hbm, image_ref, sems = rest
-    sunk_copy = pltpu.make_async_copy(sunk_ref, sunk_hbm, sems.at[0])
-    sunk_copy.start()
+def source_kernel(sunk_hbm, part_ref, two_ref, high_ref, low_ref, *rest):
+    *image_refs, out_hbm, image_hbm, edge_ref, image_ref, sems = rest
+    del sunk_hbm
+    chunks, width = part_ref.shape[0], two_ref.shape[2]
+    half, edge, span = width // 2, two_ref.shape[1], edge_ref.shape[1]
+    at = lax.axis_index("src")
+    up = at % 2 == 0
+    inner = jnp.logical_and(at > 0, at < lax.axis_size("src") - 1)
     image = functools.reduce(jnp.add, [ref[...] for ref in image_refs])
     if len(image_refs) > 1:
-        at, edge = lax.axis_index("src"), two_ref.shape[1]
-        from_two = jnp.where(at % 2 == 0, two_ref[0, :1], two_ref[0, edge - 1 :])
-        image = image + jnp.where(jnp.logical_and(at > 0, at < lax.axis_size("src") - 1), from_two, 0.0)
+        from_two = jnp.where(up, two_ref[0, :1], two_ref[0, edge - 1 :])
+        image = image + jnp.where(inner, from_two, 0.0)
     image_ref[...] = image
-    image_copy = pltpu.make_async_copy(image_ref, image_hbm, sems.at[1])
+    image_copy = pltpu.make_async_copy(image_ref, image_hbm, sems.at[0])
     image_copy.start()
-    sunk_copy.wait()
+
+    @pl.when(inner)
+    def _():
+        none = jnp.zeros((half, width), F32)
+        gap = none[: half - edge]
+        first, last = slice(0, span), slice(width - span, width)
+
+        def pick(ref, columns):
+            chosen = [
+                jnp.concatenate([ref[chunk, :width, columns][rows], ref[chunk, width:, columns][rows]], axis=0)
+                for chunk, rows in ((0, first), (chunks - 1, last))
+            ]
+            return jnp.where(up, *chosen)
+
+        halo = []
+        for part in range(2):
+            before = jnp.concatenate([none, gap, two_ref[part]], axis=0)
+            after = jnp.concatenate([two_ref[part], gap, none], axis=0)
+            halo.append(jnp.where(up, before, after))
+        beside = slice(width, 2 * width)
+        operator = (pick(high_ref, beside), pick(low_ref, beside))
+        full = pick(part_ref, slice(None)) + dot3(operator, halves(jnp.concatenate(halo, axis=1)))
+        edge_ref[0] = full[:span, :width] - full[span:, width:]
+        edge_ref[1] = full[:span, width:] + full[span:, :width]
+        rows = pl.ds(pl.multiple_of(jnp.where(up, 0, chunks * width - span), 8), span)
+        copy = pltpu.make_async_copy(edge_ref, out_hbm.at[:, rows, :], sems.at[1])
+        copy.start()
+        copy.wait()
+
     image_copy.wait()
 
 
@@ -367,24 +398,31 @@
             images = [image, lax.psum(near, "freq")]
     else:
         images = [lax.psum(image, "src")]
-    sunk = pl.pallas_call(
+    sunk, parts = pl.pallas_call(
+        inner_kernel,
+        out_shape=[jax.ShapeDtypeStruct((2, rows, width), F32), jax.ShapeDtypeStruct((chunks,) + square, F32)],
+        in_specs=[vmem] * 4,
+        out_specs=[vmem] * 2,
+        compiler_params=params,
+        cost_estimate=cost,
+        name="inner",
+    )(field, one, src_high, src_low)
+    span = -(-edge // 16) * 16
+    anywhere = pl.BlockSpec(memory_space=pl.ANY)
+    sunk, image = pl.pallas_call(
         source_kernel,
-        out_shape=jax.ShapeDtypeStruct((2, rows, width), F32),
-        in_specs=[vmem] * 5,
-        out_specs=vmem,
-        compiler_params=params,
-        cost_estimate=cost,
+        out_shape=[jax.ShapeDtypeStruct((2, rows, width), F32), jax.ShapeDtypeStruct((1, width), F32)],
+        in_specs=[anywhere] + [vmem] * (4 + len(images)),
+        out_specs=[anywhere] * 2,
+        scratch_shapes=[
+            pltpu.VMEM((2, span, width), F32),
+            pltpu.VMEM((1, width), F32),
+            pltpu.SemaphoreType.DMA((2,)),
+        ],
+        input_output_aliases={0: 0},
+        compiler_params=params,
         name="sources",
-    )(field, two, one, src_high, src_low)
-    sunk, image = pl.pallas_call(
-        store_kernel,
-        out_shape=[jax.ShapeDtypeStruct((2, rows, width), F32), jax.ShapeDtypeStruct((1, width), F32)],
-        in_specs=[vmem] * (2 + len(images)),
-        out_specs=[pl.BlockSpec(memory_space=pl.ANY)] * 2,
-        scratch_shapes=[pltpu.VMEM((1, width), F32), pltpu.SemaphoreType.DMA((2,))],
-        compiler_params=params,
-        name="store",
-    )(sunk, two, *images)
+    )(sunk, parts, two, src_high, src_low, *images)
     return sunk.reshape(wavefield.shape), image.reshape(width)
 
 

time: 14.7 us -> 14.7 us (level)
  waiting for transfers between devices: 0.66 us -> 0.11 us
  Pallas kernels: 3.87 us -> 4.4 us
    ppermute x1, waiting for transfers between devices: 0.55 us -> 0.01 us  [body(): images = [image, near, lax.ppermute(near, 'freq', [(0, 1), (1, 0)])]]
    pallas_call x2, Pallas kernels: 0.94 us -> 1.47 us  [the longest x1 0.93 us: body(): pl.pallas_call(inner_kernel, out_shape=[jax.ShapeDtypeStruct((2, rows, wi...]
  transfers between devices with their start and end apart: 7 -> 7, of which waited for: 2 -> 1; matrix products, arithmetic and copies ran while one was open for 0% -> 0% of each run, Pallas kernels for 19% -> 24%
where the time goes in v7:
time: 14.7 us; the launch traced here: 14.5 us
  starting transfers between devices  7.58 us (52%)
  Pallas kernels  4.4 us (30%)
  between operations  1.43 us (10%)
  local copies, waits for them, and re-layouts  0.95 us (6%)
    ppermute x1, starting transfers between devices, body(): second = lax.ppermute(second, ('rcv', 'freq'), around(n_rcv, n_freq, 1))  2.6 us
    ppermute x1, starting transfers between devices, body(): lax.ppermute(one, 'src', [(i, i + 1 if i % 2 == 0 else i - 1) for i in ra...  1.94 us
    ppermute x1, starting transfers between devices, body(): far = lax.ppermute(image, ('src', 'freq'), far_pairs(n_freq))  1.58 us
    pallas_call x1, Pallas kernels, body(): pl.pallas_call(functools.partial(rcv_operator_kernel, lateral), out_shape...  1.49 us
    pallas_call x1, Pallas kernels, body(): pl.pallas_call(functools.partial(src_operator_kernel, lateral, op_table.s...  1 us
    pallas_call x1, Pallas kernels, body(): pl.pallas_call(inner_kernel, out_shape=[jax.ShapeDtypeStruct((2, rows, wi...  0.93 us
    unnamed x12, local copies, waits for them, and re-layouts  0.92 us
    pallas_call x1, Pallas kernels, body(): pl.pallas_call(source_kernel, out_shape=[jax.ShapeDtypeStruct((2, rows, w...  0.54 us
  transfers between devices with their start and end apart: 7, of which 1 were waited for; matrix products, arithmetic and copies ran while one was open for 0% of the time, Pallas kernels for 24%

profile of v7, /device:TPU:0, one launch (start us, length us, event | category | flops | bytes accessed | tf_op | source)
XLA Modules:
  0.0 14.5 jit_solution(4608836481743046629)
XLA Ops:
  0.6 0.0 copy-start
  0.6 0.9 %copy-done = f32[2,1,128,128]{3,2,1,0:T(8,128)S(1)} copy-done((f32[2,1,128,128]{3,2,1,0:T(8,128)S(1)}, f32[2,1,128,128]{3,2,1,0:T(8,128)}, u32[]{:S(2)}) %copy-start) | copy-done | bytes 131096
  1.5 0.0 copy-start.4
  1.5 0.0 copy-start.5
  1.5 0.0 copy-start.3
  1.5 0.1 pack.1
  1.7 0.0 copy-start.2
  1.7 0.5 %collective-permute-start = (f32[88,128]{1,0:T(8,128)S(1)}, f32[88,128]{1,0:T(8,128)S(1)}, u32[]{:S(2)}, u32[]{:S(2)}) collective-permute-start(f32[88,128]{1,0:T(8,128)S(1)} %get-tuple-element.22), channel_id=1, source_target_pairs={{0,1},{1,3},{2,0},{3,5},{4,2},{5,7},{6,4},{7,6},{8,9},{9,11},{10,8... | collective-permute-start | bytes 135176 | tf_op jit(solution)/shard_map/ppermute | solution.py:334
  2.1 2.6 %collective-permute-start.1 = (f32[88,128]{1,0:T(8,128)S(1)}, f32[88,128]{1,0:T(8,128)S(1)}, u32[]{:S(2)}, u32[]{:S(2)}) collective-permute-start(f32[88,128]{1,0:T(8,128)S(1)} %get-tuple-element.23), channel_id=1, source_target_pairs={{0,2},{1,0},{2,4},{3,1},{4,6},{5,3},{6,7},{7,5},{8,10},{9,8},{10,1... | collective-permute-start | bytes 135176 | tf_op jit(solution)/shard_map/ppermute | solution.py:335
  4.7 0.0 copy-done.4
  5.4 0.0 copy-done.5
  5.4 0.0 copy-done.3
  5.5 0.0 copy-done.2
  5.5 0.0 copy-start.1
  5.5 1.5 %rcv_operator.1 = (f32[256,256]{1,0:T(8,128)S(1)}, bf16[256,256]{1,0:T(8,128)(2,1)S(1)}, bf16[256,256]{1,0:T(8,128)(2,1)S(1)}, f32[2,32,128]{2,1,0:T(8,128)S(1)}) custom-call(f32[6,128]{1,0:T(8,128)S(1)} %select_maximum_fusion.small_ref, f32[19,2,64]{2,1,0:T(2,128)S(1)} %bitcast.25), custom_call_target="tpu_custom_call" | custom-call | flops 1610612736 | bytes 1048576 | tf_op jit(solution)/shard_map/rcv_operator/pallas_call | solution.py:338
  7.0 0.0 collective-permute-done.first_ref
  7.0 0.0 collective-permute-done.1.second_ref
  7.0 0.0 copy-done.1
  7.0 0.3 %receivers.1 = (f32[2,128,128]{2,1,0:T(8,128)S(1)}, f32[2,40,128]{2,1,0:T(8,128)S(1)}, f32[2,40,128]{2,1,0:T(8,128)S(1)}, f32[1,128]{1,0:T(1,128)S(1)}) custom-call(f32[256,128]{1,0:T(8,128)S(1)} %bitcast.23, f32[88,128]{1,0:T(8,128)S(1)} %collective-permute-done.first_ref, f32[88,128]{1,0:T(8,128)S(1)} %collective-permute-done.1.second_ref, ...), custom_call_target="tpu_custom_call" | custom-call | tf_op jit(solution)/shard_map/receivers/pallas_call | solution.py:353
  7.3 0.2 %collective-permute-start.3 = (f32[2,40,128]{2,1,0:T(8,128)S(1)}, f32[2,40,128]{2,1,0:T(8,128)S(1)}, u32[]{:S(2)}, u32[]{:S(2)}) collective-permute-start(f32[2,40,128]{2,1,0:T(8,128)S(1)} %get-tuple-element.28), channel_id=1, source_target_pairs={{0,1},{1,0},{2,3},{3,2},{4,5},{5,4},{6,7},{7,6},{8,9},{9,8},{10,11... | collective-permute-start | bytes 122888 | tf_op jit(solution)/shard_map/ppermute | solution.py:368
  7.6 1.9 %collective-permute-start.2 = (f32[2,40,128]{2,1,0:T(8,128)S(1)}, f32[2,40,128]{2,1,0:T(8,128)S(1)}, u32[]{:S(2)}, u32[]{:S(2)}) collective-permute-start(f32[2,40,128]{2,1,0:T(8,128)S(1)} %get-tuple-element.28), channel_id=1, source_target_pairs={{0,8},{8,0},{16,24},{24,16},{1,9},{9,1},{17,25},{25,17},{2,10},{10... | collective-permute-start | bytes 122888 | tf_op jit(solution)/shard_map/ppermute | solution.py:372
  9.5 0.0 collective-permute-done.3
  9.5 1.6 %collective-permute-start.4 = (f32[1,128]{1,0:T(1,128)S(1)}, f32[1,128]{1,0:T(1,128)S(1)}, u32[]{:S(2)}, u32[]{:S(2)}) collective-permute-start(f32[1,128]{1,0:T(1,128)S(1)} %fusion.4.rest_0_), channel_id=1, source_target_pairs={{0,16},{1,25},{8,9},{9,24},{16,17},{17,0},{24,8},{25,1},{2,18},{3,... | collective-permute-start | bytes 1544 | tf_op jit(solution)/shard_map/ppermute | solution.py:375
  11.1 0.4 %collective-permute-start.5 = (f32[2,40,128]{2,1,0:T(8,128)S(1)}, f32[2,40,128]{2,1,0:T(8,128)S(1)}, u32[]{:S(2)}, u32[]{:S(2)}) collective-permute-start(f32[2,40,128]{2,1,0:T(8,128)S(1)} %dynamic_update_slice.3), channel_id=1, source_target_pairs={{0,1},{1,0},{8,16},{9,17},{16,8},{17,9},{24,25},{25,24},{2,3},{3,2... | collective-permute-start | bytes 122888 | tf_op jit(solution)/shard_map/ppermute | solution.py:377
  11.5 0.1 collective-permute-done.2.one_ref
  11.6 1.0 %src_operator.1 = (bf16[1,256,256]{2,1,0:T(8,128)(2,1)S(1)}, bf16[1,256,256]{2,1,0:T(8,128)(2,1)S(1)}) custom-call(f32[2,32,128]{2,1,0:T(8,128)S(1)} %get-tuple-element.32.found_ref), custom_call_target="tpu_custom_call" | custom-call | flops 1048576 | bytes 1024 | tf_op jit(solution)/shard_map/src_operator/pallas_call | solution.py:379
  12.6 0.0 collective-permute-done.4
  12.7 0.4 %collective-permute-start.6 = (f32[1,128]{1,0:T(1,128)S(1)}, f32[1,128]{1,0:T(1,128)S(1)}, u32[]{:S(2)}, u32[]{:S(2)}) collective-permute-start(f32[1,128]{1,0:T(1,128)S(1)} %fusion.2.rest_1_), channel_id=1, source_target_pairs={{0,1},{1,0},{2,3},{3,2},{4,5},{5,4},{6,7},{7,6},{8,9},{9,8},{10,11... | collective-permute-start | bytes 1544 | tf_op jit(solution)/shard_map/ppermute | solution.py:396
  13.0 0.9 %inner.1 = (f32[2,128,128]{2,1,0:T(8,128)}, f32[1,256,256]{2,1,0:T(8,128)S(1)}) custom-call(f32[2,128,128]{2,1,0:T(8,128)S(1)} %get-tuple-element.27.field_ref, f32[2,40,128]{2,1,0:T(8,128)S(1)} %collective-permute-done.2.one_ref, bf16[1,256,256]{2,1,0:T(8,128)(2,1)S(1)} %get-tuple-element.34.high_ref, bf16[1,256,256]{2,1,0:T(8,128)(2,1)S(1)} %get-tuple-element.35.low_ref), custom_call_target="tpu_custom_call" | custom-call | flops 1610612736 | bytes 1048576 | tf_op jit(solution)/shard_map/inner/pallas_call | solution.py:401
  14.0 0.0 collective-permute-done.6.rest_2_
  14.0 0.0 collective-permute-done.5.two_ref
  14.0 0.5 %sources.1 = (f32[2,128,128]{2,1,0:T(8,128)}, f32[1,128]{1,0:T(1,128)}) custom-call(f32[2,128,128]{2,1,0:T(8,128)} %get-tuple-element.36.sunk_hbm, f32[1,256,256]{2,1,0:T(8,128)S(1)} %get-tuple-element.37.part_ref, f32[2,40,128]{2,1,0:T(8,128)S(1)} %collective-permute-done.5.two_ref, ...), custom_call_target="tpu_custom_call", output_to_operand_aliasing={{0}: (0, {})} | custom-call | tf_op jit(solution)/shard_map/sources/pallas_call | solution.py:412
  (7 shorter events, 0.1 us)
Async XLA Ops:
  0.6 0.9 %copy-start = (f32[2,1,128,128]{3,2,1,0:T(8,128)S(1)}, f32[2,1,128,128]{3,2,1,0:T(8,128)}, u32[]{:S(2)}) copy-start(f32[2,1,128,128]{3,2,1,0:T(8,128)} %param.6) | copy-start | bytes 393220
  1.5 3.2 %copy-start.4 = (s32[16,2]{0,1:T(2,128)S(1)}, s32[16,2]{0,1:T(2,128)}, u32[]{:S(2)}) copy-start(s32[16,2]{0,1:T(2,128)} %param.9) | copy-start | bytes 388
  1.5 3.9 %copy-start.5 = (s32[32]{0:T(128)S(1)}, s32[32]{0:T(128)}, u32[]{:S(2)}) copy-start(s32[32]{0:T(128)} %param.8) | copy-start | bytes 388
  1.5 3.9 %copy-start.3 = (f32[16,2]{0,1:T(2,128)S(1)}, f32[16,2]{0,1:T(2,128)}, u32[]{:S(2)}) copy-start(f32[16,2]{0,1:T(2,128)} %param.10) | copy-start | bytes 388
  1.7 3.8 %copy-start.2 = (f32[2,64,19]{1,0,2:T(2,128)S(1)}, f32[2,64,19]{1,0,2:T(2,128)}, u32[]{:S(2)}) copy-start(f32[2,64,19]{1,0,2:T(2,128)} %param.7) | copy-start | bytes 29188
  1.7 5.3 %collective-permute-start = (f32[88,128]{1,0:T(8,128)S(1)}, f32[88,128]{1,0:T(8,128)S(1)}, u32[]{:S(2)}, u32[]{:S(2)}) collective-permute-start(f32[88,128]{1,0:T(8,128)S(1)} %get-tuple-element.22), channel_id=1, source_target_pairs={{0,1},{1,3},{2,0},{3,5},{4,2},{5,7},{6,4},{7,6},{8,9},{9,11},{10,8... | collective-permute-start | bytes 135176 | tf_op jit(solution)/shard_map/ppermute | solution.py:334
  2.1 4.8 %collective-permute-start.1 = (f32[88,128]{1,0:T(8,128)S(1)}, f32[88,128]{1,0:T(8,128)S(1)}, u32[]{:S(2)}, u32[]{:S(2)}) collective-permute-start(f32[88,128]{1,0:T(8,128)S(1)} %get-tuple-element.23), channel_id=1, source_target_pairs={{0,2},{1,0},{2,4},{3,1},{4,6},{5,3},{6,7},{7,5},{8,10},{9,8},{10,1... | collective-permute-start | bytes 135176 | tf_op jit(solution)/shard_map/ppermute | solution.py:335
  5.5 1.5 %copy-start.1 = (f32[2,1,128,128]{3,2,1,0:T(8,128)S(1)}, f32[2,1,128,128]{3,2,1,0:T(8,128)}, u32[]{:S(2)}) copy-start(f32[2,1,128,128]{3,2,1,0:T(8,128)} %param.6) | copy-start | bytes 393220
  7.3 2.2 %collective-permute-start.3 = (f32[2,40,128]{2,1,0:T(8,128)S(1)}, f32[2,40,128]{2,1,0:T(8,128)S(1)}, u32[]{:S(2)}, u32[]{:S(2)}) collective-permute-start(f32[2,40,128]{2,1,0:T(8,128)S(1)} %get-tuple-element.28), channel_id=1, source_target_pairs={{0,1},{1,0},{2,3},{3,2},{4,5},{5,4},{6,7},{7,6},{8,9},{9,8},{10,11... | collective-permute-start | bytes 122888 | tf_op jit(solution)/shard_map/ppermute | solution.py:368
  7.6 4.1 %collective-permute-start.2 = (f32[2,40,128]{2,1,0:T(8,128)S(1)}, f32[2,40,128]{2,1,0:T(8,128)S(1)}, u32[]{:S(2)}, u32[]{:S(2)}) collective-permute-start(f32[2,40,128]{2,1,0:T(8,128)S(1)} %get-tuple-element.28), channel_id=1, source_target_pairs={{0,8},{8,0},{16,24},{24,16},{1,9},{9,1},{17,25},{25,17},{2,10},{10... | collective-permute-start | bytes 122888 | tf_op jit(solution)/shard_map/ppermute | solution.py:372
  9.5 3.1 %collective-permute-start.4 = (f32[1,128]{1,0:T(1,128)S(1)}, f32[1,128]{1,0:T(1,128)S(1)}, u32[]{:S(2)}, u32[]{:S(2)}) collective-permute-start(f32[1,128]{1,0:T(1,128)S(1)} %fusion.4.rest_0_), channel_id=1, source_target_pairs={{0,16},{1,25},{8,9},{9,24},{16,17},{17,0},{24,8},{25,1},{2,18},{3,... | collective-permute-start | bytes 1544 | tf_op jit(solution)/shard_map/ppermute | solution.py:375
  11.1 2.8 %collective-permute-start.5 = (f32[2,40,128]{2,1,0:T(8,128)S(1)}, f32[2,40,128]{2,1,0:T(8,128)S(1)}, u32[]{:S(2)}, u32[]{:S(2)}) collective-permute-start(f32[2,40,128]{2,1,0:T(8,128)S(1)} %dynamic_update_slice.3), channel_id=1, source_target_pairs={{0,1},{1,0},{8,16},{9,17},{16,8},{17,9},{24,25},{25,24},{2,3},{3,2... | collective-permute-start | bytes 122888 | tf_op jit(solution)/shard_map/ppermute | solution.py:377
  12.7 1.3 %collective-permute-start.6 = (f32[1,128]{1,0:T(1,128)S(1)}, f32[1,128]{1,0:T(1,128)S(1)}, u32[]{:S(2)}, u32[]{:S(2)}) collective-permute-start(f32[1,128]{1,0:T(1,128)S(1)} %fusion.2.rest_1_), channel_id=1, source_target_pairs={{0,1},{1,0},{2,3},{3,2},{4,5},{5,4},{6,7},{7,6},{8,9},{9,8},{10,11... | collective-permute-start | bytes 1544 | tf_op jit(solution)/shard_map/ppermute | solution.py:396

commit v8 on v7

--- a/solution.py
+++ b/solution.py
@@ -374,8 +374,8 @@
     if n_src == 4:
         far = lax.ppermute(image, ("src", "freq"), far_pairs(n_freq))
         two = lax.dynamic_update_slice(two, image[None], (0, jnp.where(up, edge - 1, 0), 0))
+    two, found = lax.optimization_barrier((two, found))
     two = lax.ppermute(two, ("src", "freq"), between(n_src, n_freq))
-    one, found = lax.optimization_barrier((one, found))
     src_high, src_low = pl.pallas_call(
         functools.partial(src_operator_kernel, lateral, op_table.shape[2]),
         out_shape=[jax.ShapeDtypeStruct((chunks,) + square, BF16)] * 2,

time: 14.7 us -> 14.7 us (level)
  transfers between devices with their start and end apart: 7 -> 7, of which waited for: 1 -> 0; matrix products, arithmetic and copies ran while one was open for 0% -> 0% of each run, Pallas kernels for 24% -> 24%
where the time goes in v8:
time: 14.7 us; the launch traced here: 14.5 us
  starting transfers between devices  7.67 us (52%)
  Pallas kernels  4.4 us (30%)
  between operations  1.44 us (10%)
  local copies, waits for them, and re-layouts  0.95 us (6%)
    ppermute x1, starting transfers between devices, body(): second = lax.ppermute(second, ('rcv', 'freq'), around(n_rcv, n_freq, 1))  2.6 us
    ppermute x1, starting transfers between devices, body(): lax.ppermute(one, 'src', [(i, i + 1 if i % 2 == 0 else i - 1) for i in ra...  1.94 us
    ppermute x1, starting transfers between devices, body(): far = lax.ppermute(image, ('src', 'freq'), far_pairs(n_freq))  1.58 us
    pallas_call x1, Pallas kernels, body(): pl.pallas_call(functools.partial(rcv_operator_kernel, lateral), out_shape...  1.49 us
    pallas_call x1, Pallas kernels, body(): pl.pallas_call(functools.partial(src_operator_kernel, lateral, op_table.s...  1 us
    pallas_call x1, Pallas kernels, body(): pl.pallas_call(inner_kernel, out_shape=[jax.ShapeDtypeStruct((2, rows, wi...  0.93 us
    unnamed x12, local copies, waits for them, and re-layouts  0.92 us
    pallas_call x1, Pallas kernels, body(): pl.pallas_call(source_kernel, out_shape=[jax.ShapeDtypeStruct((2, rows, w...  0.54 us
  transfers between devices with their start and end apart: 7, of which 0 were waited for; matrix products, arithmetic and copies ran while one was open for 0% of the time, Pallas kernels for 24%

profile of v8, /device:TPU:0, one launch (start us, length us, event | category | flops | bytes accessed | tf_op | source)
XLA Modules:
  0.0 14.5 jit_solution(14284699762741375844)
XLA Ops:
  0.6 0.0 copy-start
  0.6 0.9 %copy-done = f32[2,1,128,128]{3,2,1,0:T(8,128)S(1)} copy-done((f32[2,1,128,128]{3,2,1,0:T(8,128)S(1)}, f32[2,1,128,128]{3,2,1,0:T(8,128)}, u32[]{:S(2)}) %copy-start) | copy-done | bytes 131096
  1.5 0.0 copy-start.4
  1.5 0.0 copy-start.5
  1.5 0.0 copy-start.3
  1.5 0.1 pack.1
  1.7 0.0 copy-start.2
  1.7 0.5 %collective-permute-start = (f32[88,128]{1,0:T(8,128)S(1)}, f32[88,128]{1,0:T(8,128)S(1)}, u32[]{:S(2)}, u32[]{:S(2)}) collective-permute-start(f32[88,128]{1,0:T(8,128)S(1)} %get-tuple-element.22), channel_id=1, source_target_pairs={{0,1},{1,3},{2,0},{3,5},{4,2},{5,7},{6,4},{7,6},{8,9},{9,11},{10,8... | collective-permute-start | bytes 135176 | tf_op jit(solution)/shard_map/ppermute | solution.py:334
  2.1 2.6 %collective-permute-start.1 = (f32[88,128]{1,0:T(8,128)S(1)}, f32[88,128]{1,0:T(8,128)S(1)}, u32[]{:S(2)}, u32[]{:S(2)}) collective-permute-start(f32[88,128]{1,0:T(8,128)S(1)} %get-tuple-element.23), channel_id=1, source_target_pairs={{0,2},{1,0},{2,4},{3,1},{4,6},{5,3},{6,7},{7,5},{8,10},{9,8},{10,1... | collective-permute-start | bytes 135176 | tf_op jit(solution)/shard_map/ppermute | solution.py:335
  4.7 0.0 copy-done.4
  5.4 0.0 copy-done.5
  5.4 0.0 copy-done.3
  5.5 0.0 copy-done.2
  5.5 0.0 copy-start.1
  5.5 1.5 %rcv_operator.1 = (f32[256,256]{1,0:T(8,128)S(1)}, bf16[256,256]{1,0:T(8,128)(2,1)S(1)}, bf16[256,256]{1,0:T(8,128)(2,1)S(1)}, f32[2,32,128]{2,1,0:T(8,128)S(1)}) custom-call(f32[6,128]{1,0:T(8,128)S(1)} %select_maximum_fusion.small_ref, f32[19,2,64]{2,1,0:T(2,128)S(1)} %bitcast.25), custom_call_target="tpu_custom_call" | custom-call | flops 1610612736 | bytes 1048576 | tf_op jit(solution)/shard_map/rcv_operator/pallas_call | solution.py:338
  7.0 0.0 collective-permute-done.first_ref
  7.0 0.0 collective-permute-done.1.second_ref
  7.0 0.0 copy-done.1
  7.0 0.3 %receivers.1 = (f32[2,128,128]{2,1,0:T(8,128)S(1)}, f32[2,40,128]{2,1,0:T(8,128)S(1)}, f32[2,40,128]{2,1,0:T(8,128)S(1)}, f32[1,128]{1,0:T(1,128)S(1)}) custom-call(f32[256,128]{1,0:T(8,128)S(1)} %bitcast.23, f32[88,128]{1,0:T(8,128)S(1)} %collective-permute-done.first_ref, f32[88,128]{1,0:T(8,128)S(1)} %collective-permute-done.1.second_ref, ...), custom_call_target="tpu_custom_call" | custom-call | tf_op jit(solution)/shard_map/receivers/pallas_call | solution.py:353
  7.3 0.2 %collective-permute-start.3 = (f32[2,40,128]{2,1,0:T(8,128)S(1)}, f32[2,40,128]{2,1,0:T(8,128)S(1)}, u32[]{:S(2)}, u32[]{:S(2)}) collective-permute-start(f32[2,40,128]{2,1,0:T(8,128)S(1)} %get-tuple-element.28), channel_id=1, source_target_pairs={{0,1},{1,0},{2,3},{3,2},{4,5},{5,4},{6,7},{7,6},{8,9},{9,8},{10,11... | collective-permute-start | bytes 122888 | tf_op jit(solution)/shard_map/ppermute | solution.py:368
  7.6 1.9 %collective-permute-start.2 = (f32[2,40,128]{2,1,0:T(8,128)S(1)}, f32[2,40,128]{2,1,0:T(8,128)S(1)}, u32[]{:S(2)}, u32[]{:S(2)}) collective-permute-start(f32[2,40,128]{2,1,0:T(8,128)S(1)} %get-tuple-element.28), channel_id=1, source_target_pairs={{0,8},{8,0},{16,24},{24,16},{1,9},{9,1},{17,25},{25,17},{2,10},{10... | collective-permute-start | bytes 122888 | tf_op jit(solution)/shard_map/ppermute | solution.py:372
  9.5 0.0 collective-permute-done.3
  9.5 1.6 %collective-permute-start.4 = (f32[1,128]{1,0:T(1,128)S(1)}, f32[1,128]{1,0:T(1,128)S(1)}, u32[]{:S(2)}, u32[]{:S(2)}) collective-permute-start(f32[1,128]{1,0:T(1,128)S(1)} %fusion.4.rest_0_), channel_id=1, source_target_pairs={{0,16},{1,25},{8,9},{9,24},{16,17},{17,0},{24,8},{25,1},{2,18},{3,... | collective-permute-start | bytes 1544 | tf_op jit(solution)/shard_map/ppermute | solution.py:375
  11.1 0.4 %collective-permute-start.5 = (f32[2,40,128]{2,1,0:T(8,128)S(1)}, f32[2,40,128]{2,1,0:T(8,128)S(1)}, u32[]{:S(2)}, u32[]{:S(2)}) collective-permute-start(f32[2,40,128]{2,1,0:T(8,128)S(1)} %dynamic_update_slice.3), channel_id=1, source_target_pairs={{0,1},{1,0},{8,16},{9,17},{16,8},{17,9},{24,25},{25,24},{2,3},{3,2... | collective-permute-start | bytes 122888 | tf_op jit(solution)/shard_map/ppermute | solution.py:378
  11.5 1.0 %src_operator.1 = (bf16[1,256,256]{2,1,0:T(8,128)(2,1)S(1)}, bf16[1,256,256]{2,1,0:T(8,128)(2,1)S(1)}) custom-call(f32[2,32,128]{2,1,0:T(8,128)S(1)} %get-tuple-element.32.found_ref), custom_call_target="tpu_custom_call" | custom-call | flops 1048576 | bytes 1024 | tf_op jit(solution)/shard_map/src_operator/pallas_call | solution.py:379
  12.5 0.0 collective-permute-done.2.one_ref
  12.6 0.0 collective-permute-done.4
  12.6 0.4 %collective-permute-start.6 = (f32[1,128]{1,0:T(1,128)S(1)}, f32[1,128]{1,0:T(1,128)S(1)}, u32[]{:S(2)}, u32[]{:S(2)}) collective-permute-start(f32[1,128]{1,0:T(1,128)S(1)} %fusion.2.rest_1_), channel_id=1, source_target_pairs={{0,1},{1,0},{2,3},{3,2},{4,5},{5,4},{6,7},{7,6},{8,9},{9,8},{10,11... | collective-permute-start | bytes 1544 | tf_op jit(solution)/shard_map/ppermute | solution.py:396
  13.0 0.9 %inner.1 = (f32[2,128,128]{2,1,0:T(8,128)}, f32[1,256,256]{2,1,0:T(8,128)S(1)}) custom-call(f32[2,128,128]{2,1,0:T(8,128)S(1)} %get-tuple-element.27.field_ref, f32[2,40,128]{2,1,0:T(8,128)S(1)} %collective-permute-done.2.one_ref, bf16[1,256,256]{2,1,0:T(8,128)(2,1)S(1)} %get-tuple-element.34.high_ref, bf16[1,256,256]{2,1,0:T(8,128)(2,1)S(1)} %get-tuple-element.35.low_ref), custom_call_target="tpu_custom_call" | custom-call | flops 1610612736 | bytes 1048576 | tf_op jit(solution)/shard_map/inner/pallas_call | solution.py:401
  14.0 0.0 collective-permute-done.6.rest_2_
  14.0 0.0 collective-permute-done.5.two_ref
  14.0 0.5 %sources.1 = (f32[2,128,128]{2,1,0:T(8,128)}, f32[1,128]{1,0:T(1,128)}) custom-call(f32[2,128,128]{2,1,0:T(8,128)} %get-tuple-element.36.sunk_hbm, f32[1,256,256]{2,1,0:T(8,128)S(1)} %get-tuple-element.37.part_ref, f32[2,40,128]{2,1,0:T(8,128)S(1)} %collective-permute-done.5.two_ref, ...), custom_call_target="tpu_custom_call", output_to_operand_aliasing={{0}: (0, {})} | custom-call | tf_op jit(solution)/shard_map/sources/pallas_call | solution.py:412
  (7 shorter events, 0.1 us)
Async XLA Ops:
  0.6 0.9 %copy-start = (f32[2,1,128,128]{3,2,1,0:T(8,128)S(1)}, f32[2,1,128,128]{3,2,1,0:T(8,128)}, u32[]{:S(2)}) copy-start(f32[2,1,128,128]{3,2,1,0:T(8,128)} %param.6) | copy-start | bytes 393220
  1.5 3.2 %copy-start.4 = (s32[16,2]{0,1:T(2,128)S(1)}, s32[16,2]{0,1:T(2,128)}, u32[]{:S(2)}) copy-start(s32[16,2]{0,1:T(2,128)} %param.9) | copy-start | bytes 388
  1.5 3.9 %copy-start.5 = (s32[32]{0:T(128)S(1)}, s32[32]{0:T(128)}, u32[]{:S(2)}) copy-start(s32[32]{0:T(128)} %param.8) | copy-start | bytes 388
  1.5 3.9 %copy-start.3 = (f32[16,2]{0,1:T(2,128)S(1)}, f32[16,2]{0,1:T(2,128)}, u32[]{:S(2)}) copy-start(f32[16,2]{0,1:T(2,128)} %param.10) | copy-start | bytes 388
  1.7 3.8 %copy-start.2 = (f32[2,64,19]{1,0,2:T(2,128)S(1)}, f32[2,64,19]{1,0,2:T(2,128)}, u32[]{:S(2)}) copy-start(f32[2,64,19]{1,0,2:T(2,128)} %param.7) | copy-start | bytes 29188
  1.7 5.3 %collective-permute-start = (f32[88,128]{1,0:T(8,128)S(1)}, f32[88,128]{1,0:T(8,128)S(1)}, u32[]{:S(2)}, u32[]{:S(2)}) collective-permute-start(f32[88,128]{1,0:T(8,128)S(1)} %get-tuple-element.22), channel_id=1, source_target_pairs={{0,1},{1,3},{2,0},{3,5},{4,2},{5,7},{6,4},{7,6},{8,9},{9,11},{10,8... | collective-permute-start | bytes 135176 | tf_op jit(solution)/shard_map/ppermute | solution.py:334
  2.1 4.8 %collective-permute-start.1 = (f32[88,128]{1,0:T(8,128)S(1)}, f32[88,128]{1,0:T(8,128)S(1)}, u32[]{:S(2)}, u32[]{:S(2)}) collective-permute-start(f32[88,128]{1,0:T(8,128)S(1)} %get-tuple-element.23), channel_id=1, source_target_pairs={{0,2},{1,0},{2,4},{3,1},{4,6},{5,3},{6,7},{7,5},{8,10},{9,8},{10,1... | collective-permute-start | bytes 135176 | tf_op jit(solution)/shard_map/ppermute | solution.py:335
  5.5 1.5 %copy-start.1 = (f32[2,1,128,128]{3,2,1,0:T(8,128)S(1)}, f32[2,1,128,128]{3,2,1,0:T(8,128)}, u32[]{:S(2)}) copy-start(f32[2,1,128,128]{3,2,1,0:T(8,128)} %param.6) | copy-start | bytes 393220
  7.3 2.2 %collective-permute-start.3 = (f32[2,40,128]{2,1,0:T(8,128)S(1)}, f32[2,40,128]{2,1,0:T(8,128)S(1)}, u32[]{:S(2)}, u32[]{:S(2)}) collective-permute-start(f32[2,40,128]{2,1,0:T(8,128)S(1)} %get-tuple-element.28), channel_id=1, source_target_pairs={{0,1},{1,0},{2,3},{3,2},{4,5},{5,4},{6,7},{7,6},{8,9},{9,8},{10,11... | collective-permute-start | bytes 122888 | tf_op jit(solution)/shard_map/ppermute | solution.py:368
  7.6 5.0 %collective-permute-start.2 = (f32[2,40,128]{2,1,0:T(8,128)S(1)}, f32[2,40,128]{2,1,0:T(8,128)S(1)}, u32[]{:S(2)}, u32[]{:S(2)}) collective-permute-start(f32[2,40,128]{2,1,0:T(8,128)S(1)} %get-tuple-element.28), channel_id=1, source_target_pairs={{0,8},{8,0},{16,24},{24,16},{1,9},{9,1},{17,25},{25,17},{2,10},{10... | collective-permute-start | bytes 122888 | tf_op jit(solution)/shard_map/ppermute | solution.py:372
  9.5 3.0 %collective-permute-start.4 = (f32[1,128]{1,0:T(1,128)S(1)}, f32[1,128]{1,0:T(1,128)S(1)}, u32[]{:S(2)}, u32[]{:S(2)}) collective-permute-start(f32[1,128]{1,0:T(1,128)S(1)} %fusion.4.rest_0_), channel_id=1, source_target_pairs={{0,16},{1,25},{8,9},{9,24},{16,17},{17,0},{24,8},{25,1},{2,18},{3,... | collective-permute-start | bytes 1544 | tf_op jit(solution)/shard_map/ppermute | solution.py:375
  11.1 2.8 %collective-permute-start.5 = (f32[2,40,128]{2,1,0:T(8,128)S(1)}, f32[2,40,128]{2,1,0:T(8,128)S(1)}, u32[]{:S(2)}, u32[]{:S(2)}) collective-permute-start(f32[2,40,128]{2,1,0:T(8,128)S(1)} %dynamic_update_slice.3), channel_id=1, source_target_pairs={{0,1},{1,0},{8,16},{9,17},{16,8},{17,9},{24,25},{25,24},{2,3},{3,2... | collective-permute-start | bytes 122888 | tf_op jit(solution)/shard_map/ppermute | solution.py:378
  12.6 1.4 %collective-permute-start.6 = (f32[1,128]{1,0:T(1,128)S(1)}, f32[1,128]{1,0:T(1,128)S(1)}, u32[]{:S(2)}, u32[]{:S(2)}) collective-permute-start(f32[1,128]{1,0:T(1,128)S(1)} %fusion.2.rest_1_), channel_id=1, source_target_pairs={{0,1},{1,0},{2,3},{3,2},{4,5},{5,4},{6,7},{7,6},{8,9},{9,8},{10,11... | collective-permute-start | bytes 1544 | tf_op jit(solution)/shard_map/ppermute | solution.py:396

commit v9 on v8

--- a/solution.py
+++ b/solution.py
@@ -192,6 +192,7 @@
 
 
 def inner_kernel(field_ref, one_ref, high_ref, low_ref, out_ref, part_ref):
+    inner = jnp.logical_and(lax.axis_index("src") > 0, lax.axis_index("src") < lax.axis_size("src") - 1)
     rows, width = field_ref.shape[1], field_ref.shape[2]
     half = width // 2
     chunks = rows // width
@@ -211,7 +212,12 @@
                 before = jnp.concatenate([gap, jnp.where(up, 0.0, one_ref[part])], axis=0)
             extended.append(jnp.concatenate([field_ref[part, low:high], after, before], axis=0))
         full = dot3((high_ref[chunk], low_ref[chunk]), halves(jnp.concatenate(extended, axis=1)))
-        part_ref[chunk] = full
+        if chunk in (0, chunks - 1):
+
+            @pl.when(inner)
+            def _(chunk=chunk, full=full):
+                part_ref[chunk] = full
+
         out_ref[0, low:high] = full[:width, :width] - full[width:, width:]
         out_ref[1, low:high] = full[:width, width:] + full[width:, :width]
 

time: 14.7 us -> 14.7 us (level)
  no operation moved by 1% of the time
where the time goes in v9:
time: 14.7 us; the launch traced here: 14.5 us
  starting transfers between devices  7.67 us (52%)
  Pallas kernels  4.41 us (30%)
  between operations  1.44 us (10%)
  local copies, waits for them, and re-layouts  0.95 us (6%)
    ppermute x1, starting transfers between devices, body(): second = lax.ppermute(second, ('rcv', 'freq'), around(n_rcv, n_freq, 1))  2.6 us
    ppermute x1, starting transfers between devices, body(): lax.ppermute(one, 'src', [(i, i + 1 if i % 2 == 0 else i - 1) for i in ra...  1.94 us
    ppermute x1, starting transfers between devices, body(): far = lax.ppermute(image, ('src', 'freq'), far_pairs(n_freq))  1.58 us
    pallas_call x1, Pallas kernels, body(): pl.pallas_call(functools.partial(rcv_operator_kernel, lateral), out_shape...  1.49 us
    pallas_call x1, Pallas kernels, body(): pl.pallas_call(functools.partial(src_operator_kernel, lateral, op_table.s...  1 us
    pallas_call x1, Pallas kernels, body(): pl.pallas_call(inner_kernel, out_shape=[jax.ShapeDtypeStruct((2, rows, wi...  0.94 us
    unnamed x12, local copies, waits for them, and re-layouts  0.92 us
    pallas_call x1, Pallas kernels, body(): pl.pallas_call(source_kernel, out_shape=[jax.ShapeDtypeStruct((2, rows, w...  0.54 us
  transfers between devices with their start and end apart: 7, of which 0 were waited for; matrix products, arithmetic and copies ran while one was open for 0% of the time, Pallas kernels for 24%

profile of v9, /device:TPU:0, one launch (start us, length us, event | category | flops | bytes accessed | tf_op | source)
XLA Modules:
  0.0 14.5 jit_solution(9033546401875581581)
XLA Ops:
  0.6 0.0 copy-start
  0.6 0.9 %copy-done = f32[2,1,128,128]{3,2,1,0:T(8,128)S(1)} copy-done((f32[2,1,128,128]{3,2,1,0:T(8,128)S(1)}, f32[2,1,128,128]{3,2,1,0:T(8,128)}, u32[]{:S(2)}) %copy-start) | copy-done | bytes 131096
  1.5 0.0 copy-start.4
  1.5 0.0 copy-start.5
  1.5 0.0 copy-start.3
  1.5 0.1 pack.1
  1.7 0.0 copy-start.2
  1.7 0.5 %collective-permute-start = (f32[88,128]{1,0:T(8,128)S(1)}, f32[88,128]{1,0:T(8,128)S(1)}, u32[]{:S(2)}, u32[]{:S(2)}) collective-permute-start(f32[88,128]{1,0:T(8,128)S(1)} %get-tuple-element.22), channel_id=1, source_target_pairs={{0,1},{1,3},{2,0},{3,5},{4,2},{5,7},{6,4},{7,6},{8,9},{9,11},{10,8... | collective-permute-start | bytes 135176 | tf_op jit(solution)/shard_map/ppermute | solution.py:340
  2.1 2.6 %collective-permute-start.1 = (f32[88,128]{1,0:T(8,128)S(1)}, f32[88,128]{1,0:T(8,128)S(1)}, u32[]{:S(2)}, u32[]{:S(2)}) collective-permute-start(f32[88,128]{1,0:T(8,128)S(1)} %get-tuple-element.23), channel_id=1, source_target_pairs={{0,2},{1,0},{2,4},{3,1},{4,6},{5,3},{6,7},{7,5},{8,10},{9,8},{10,1... | collective-permute-start | bytes 135176 | tf_op jit(solution)/shard_map/ppermute | solution.py:341
  4.7 0.0 copy-done.4
  5.4 0.0 copy-done.5
  5.4 0.0 copy-done.3
  5.5 0.0 copy-done.2
  5.5 0.0 copy-start.1
  5.5 1.5 %rcv_operator.1 = (f32[256,256]{1,0:T(8,128)S(1)}, bf16[256,256]{1,0:T(8,128)(2,1)S(1)}, bf16[256,256]{1,0:T(8,128)(2,1)S(1)}, f32[2,32,128]{2,1,0:T(8,128)S(1)}) custom-call(f32[6,128]{1,0:T(8,128)S(1)} %select_maximum_fusion.small_ref, f32[19,2,64]{2,1,0:T(2,128)S(1)} %bitcast.25), custom_call_target="tpu_custom_call" | custom-call | flops 1610612736 | bytes 1048576 | tf_op jit(solution)/shard_map/rcv_operator/pallas_call | solution.py:344
  7.0 0.0 collective-permute-done.first_ref
  7.0 0.0 collective-permute-done.1.second_ref
  7.0 0.0 copy-done.1
  7.0 0.3 %receivers.1 = (f32[2,128,128]{2,1,0:T(8,128)S(1)}, f32[2,40,128]{2,1,0:T(8,128)S(1)}, f32[2,40,128]{2,1,0:T(8,128)S(1)}, f32[1,128]{1,0:T(1,128)S(1)}) custom-call(f32[256,128]{1,0:T(8,128)S(1)} %bitcast.23, f32[88,128]{1,0:T(8,128)S(1)} %collective-permute-done.first_ref, f32[88,128]{1,0:T(8,128)S(1)} %collective-permute-done.1.second_ref, ...), custom_call_target="tpu_custom_call" | custom-call | tf_op jit(solution)/shard_map/receivers/pallas_call | solution.py:359
  7.3 0.2 %collective-permute-start.3 = (f32[2,40,128]{2,1,0:T(8,128)S(1)}, f32[2,40,128]{2,1,0:T(8,128)S(1)}, u32[]{:S(2)}, u32[]{:S(2)}) collective-permute-start(f32[2,40,128]{2,1,0:T(8,128)S(1)} %get-tuple-element.28), channel_id=1, source_target_pairs={{0,1},{1,0},{2,3},{3,2},{4,5},{5,4},{6,7},{7,6},{8,9},{9,8},{10,11... | collective-permute-start | bytes 122888 | tf_op jit(solution)/shard_map/ppermute | solution.py:374
  7.6 1.9 %collective-permute-start.2 = (f32[2,40,128]{2,1,0:T(8,128)S(1)}, f32[2,40,128]{2,1,0:T(8,128)S(1)}, u32[]{:S(2)}, u32[]{:S(2)}) collective-permute-start(f32[2,40,128]{2,1,0:T(8,128)S(1)} %get-tuple-element.28), channel_id=1, source_target_pairs={{0,8},{8,0},{16,24},{24,16},{1,9},{9,1},{17,25},{25,17},{2,10},{10... | collective-permute-start | bytes 122888 | tf_op jit(solution)/shard_map/ppermute | solution.py:378
  9.5 0.0 collective-permute-done.3
  9.5 1.6 %collective-permute-start.4 = (f32[1,128]{1,0:T(1,128)S(1)}, f32[1,128]{1,0:T(1,128)S(1)}, u32[]{:S(2)}, u32[]{:S(2)}) collective-permute-start(f32[1,128]{1,0:T(1,128)S(1)} %fusion.4.rest_0_), channel_id=1, source_target_pairs={{0,16},{1,25},{8,9},{9,24},{16,17},{17,0},{24,8},{25,1},{2,18},{3,... | collective-permute-start | bytes 1544 | tf_op jit(solution)/shard_map/ppermute | solution.py:381
  11.1 0.4 %collective-permute-start.5 = (f32[2,40,128]{2,1,0:T(8,128)S(1)}, f32[2,40,128]{2,1,0:T(8,128)S(1)}, u32[]{:S(2)}, u32[]{:S(2)}) collective-permute-start(f32[2,40,128]{2,1,0:T(8,128)S(1)} %dynamic_update_slice.3), channel_id=1, source_target_pairs={{0,1},{1,0},{8,16},{9,17},{16,8},{17,9},{24,25},{25,24},{2,3},{3,2... | collective-permute-start | bytes 122888 | tf_op jit(solution)/shard_map/ppermute | solution.py:384
  11.5 1.0 %src_operator.1 = (bf16[1,256,256]{2,1,0:T(8,128)(2,1)S(1)}, bf16[1,256,256]{2,1,0:T(8,128)(2,1)S(1)}) custom-call(f32[2,32,128]{2,1,0:T(8,128)S(1)} %get-tuple-element.32.found_ref), custom_call_target="tpu_custom_call" | custom-call | flops 1048576 | bytes 1024 | tf_op jit(solution)/shard_map/src_operator/pallas_call | solution.py:385
  12.5 0.0 collective-permute-done.2.one_ref
  12.6 0.0 collective-permute-done.4
  12.6 0.4 %collective-permute-start.6 = (f32[1,128]{1,0:T(1,128)S(1)}, f32[1,128]{1,0:T(1,128)S(1)}, u32[]{:S(2)}, u32[]{:S(2)}) collective-permute-start(f32[1,128]{1,0:T(1,128)S(1)} %fusion.2.rest_1_), channel_id=1, source_target_pairs={{0,1},{1,0},{2,3},{3,2},{4,5},{5,4},{6,7},{7,6},{8,9},{9,8},{10,11... | collective-permute-start | bytes 1544 | tf_op jit(solution)/shard_map/ppermute | solution.py:402
  13.0 0.9 %inner.1 = (f32[2,128,128]{2,1,0:T(8,128)}, f32[1,256,256]{2,1,0:T(8,128)S(1)}) custom-call(f32[2,128,128]{2,1,0:T(8,128)S(1)} %get-tuple-element.27.field_ref, f32[2,40,128]{2,1,0:T(8,128)S(1)} %collective-permute-done.2.one_ref, bf16[1,256,256]{2,1,0:T(8,128)(2,1)S(1)} %get-tuple-element.34.high_ref, bf16[1,256,256]{2,1,0:T(8,128)(2,1)S(1)} %get-tuple-element.35.low_ref), custom_call_target="tpu_custom_call" | custom-call | flops 1610612736 | bytes 1048576 | tf_op jit(solution)/shard_map/inner/pallas_call | solution.py:407
  14.0 0.0 collective-permute-done.6.rest_2_
  14.0 0.0 collective-permute-done.5.two_ref
  14.0 0.5 %sources.1 = (f32[2,128,128]{2,1,0:T(8,128)}, f32[1,128]{1,0:T(1,128)}) custom-call(f32[2,128,128]{2,1,0:T(8,128)} %get-tuple-element.36.sunk_hbm, f32[1,256,256]{2,1,0:T(8,128)S(1)} %get-tuple-element.37.part_ref, f32[2,40,128]{2,1,0:T(8,128)S(1)} %collective-permute-done.5.two_ref, ...), custom_call_target="tpu_custom_call", output_to_operand_aliasing={{0}: (0, {})} | custom-call | tf_op jit(solution)/shard_map/sources/pallas_call | solution.py:418
  (7 shorter events, 0.1 us)
Async XLA Ops:
  0.6 0.9 %copy-start = (f32[2,1,128,128]{3,2,1,0:T(8,128)S(1)}, f32[2,1,128,128]{3,2,1,0:T(8,128)}, u32[]{:S(2)}) copy-start(f32[2,1,128,128]{3,2,1,0:T(8,128)} %param.6) | copy-start | bytes 393220
  1.5 3.2 %copy-start.4 = (s32[16,2]{0,1:T(2,128)S(1)}, s32[16,2]{0,1:T(2,128)}, u32[]{:S(2)}) copy-start(s32[16,2]{0,1:T(2,128)} %param.9) | copy-start | bytes 388
  1.5 3.9 %copy-start.5 = (s32[32]{0:T(128)S(1)}, s32[32]{0:T(128)}, u32[]{:S(2)}) copy-start(s32[32]{0:T(128)} %param.8) | copy-start | bytes 388
  1.5 3.9 %copy-start.3 = (f32[16,2]{0,1:T(2,128)S(1)}, f32[16,2]{0,1:T(2,128)}, u32[]{:S(2)}) copy-start(f32[16,2]{0,1:T(2,128)} %param.10) | copy-start | bytes 388
  1.7 3.8 %copy-start.2 = (f32[2,64,19]{1,0,2:T(2,128)S(1)}, f32[2,64,19]{1,0,2:T(2,128)}, u32[]{:S(2)}) copy-start(f32[2,64,19]{1,0,2:T(2,128)} %param.7) | copy-start | bytes 29188
  1.7 5.3 %collective-permute-start = (f32[88,128]{1,0:T(8,128)S(1)}, f32[88,128]{1,0:T(8,128)S(1)}, u32[]{:S(2)}, u32[]{:S(2)}) collective-permute-start(f32[88,128]{1,0:T(8,128)S(1)} %get-tuple-element.22), channel_id=1, source_target_pairs={{0,1},{1,3},{2,0},{3,5},{4,2},{5,7},{6,4},{7,6},{8,9},{9,11},{10,8... | collective-permute-start | bytes 135176 | tf_op jit(solution)/shard_map/ppermute | solution.py:340
  2.1 4.8 %collective-permute-start.1 = (f32[88,128]{1,0:T(8,128)S(1)}, f32[88,128]{1,0:T(8,128)S(1)}, u32[]{:S(2)}, u32[]{:S(2)}) collective-permute-start(f32[88,128]{1,0:T(8,128)S(1)} %get-tuple-element.23), channel_id=1, source_target_pairs={{0,2},{1,0},{2,4},{3,1},{4,6},{5,3},{6,7},{7,5},{8,10},{9,8},{10,1... | collective-permute-start | bytes 135176 | tf_op jit(solution)/shard_map/ppermute | solution.py:341
  5.5 1.5 %copy-start.1 = (f32[2,1,128,128]{3,2,1,0:T(8,128)S(1)}, f32[2,1,128,128]{3,2,1,0:T(8,128)}, u32[]{:S(2)}) copy-start(f32[2,1,128,128]{3,2,1,0:T(8,128)} %param.6) | copy-start | bytes 393220
  7.3 2.2 %collective-permute-start.3 = (f32[2,40,128]{2,1,0:T(8,128)S(1)}, f32[2,40,128]{2,1,0:T(8,128)S(1)}, u32[]{:S(2)}, u32[]{:S(2)}) collective-permute-start(f32[2,40,128]{2,1,0:T(8,128)S(1)} %get-tuple-element.28), channel_id=1, source_target_pairs={{0,1},{1,0},{2,3},{3,2},{4,5},{5,4},{6,7},{7,6},{8,9},{9,8},{10,11... | collective-permute-start | bytes 122888 | tf_op jit(solution)/shard_map/ppermute | solution.py:374
  7.6 5.0 %collective-permute-start.2 = (f32[2,40,128]{2,1,0:T(8,128)S(1)}, f32[2,40,128]{2,1,0:T(8,128)S(1)}, u32[]{:S(2)}, u32[]{:S(2)}) collective-permute-start(f32[2,40,128]{2,1,0:T(8,128)S(1)} %get-tuple-element.28), channel_id=1, source_target_pairs={{0,8},{8,0},{16,24},{24,16},{1,9},{9,1},{17,25},{25,17},{2,10},{10... | collective-permute-start | bytes 122888 | tf_op jit(solution)/shard_map/ppermute | solution.py:378
  9.5 3.0 %collective-permute-start.4 = (f32[1,128]{1,0:T(1,128)S(1)}, f32[1,128]{1,0:T(1,128)S(1)}, u32[]{:S(2)}, u32[]{:S(2)}) collective-permute-start(f32[1,128]{1,0:T(1,128)S(1)} %fusion.4.rest_0_), channel_id=1, source_target_pairs={{0,16},{1,25},{8,9},{9,24},{16,17},{17,0},{24,8},{25,1},{2,18},{3,... | collective-permute-start | bytes 1544 | tf_op jit(solution)/shard_map/ppermute | solution.py:381
  11.1 2.8 %collective-permute-start.5 = (f32[2,40,128]{2,1,0:T(8,128)S(1)}, f32[2,40,128]{2,1,0:T(8,128)S(1)}, u32[]{:S(2)}, u32[]{:S(2)}) collective-permute-start(f32[2,40,128]{2,1,0:T(8,128)S(1)} %dynamic_update_slice.3), channel_id=1, source_target_pairs={{0,1},{1,0},{8,16},{9,17},{16,8},{17,9},{24,25},{25,24},{2,3},{3,2... | collective-permute-start | bytes 122888 | tf_op jit(solution)/shard_map/ppermute | solution.py:384
  12.6 1.4 %collective-permute-start.6 = (f32[1,128]{1,0:T(1,128)S(1)}, f32[1,128]{1,0:T(1,128)S(1)}, u32[]{:S(2)}, u32[]{:S(2)}) collective-permute-start(f32[1,128]{1,0:T(1,128)S(1)} %fusion.2.rest_1_), channel_id=1, source_target_pairs={{0,1},{1,0},{2,3},{3,2},{4,5},{5,4},{6,7},{7,6},{8,9},{9,8},{10,11... | collective-permute-start | bytes 1544 | tf_op jit(solution)/shard_map/ppermute | solution.py:402

commit v10 on v9

--- a/solution.py
+++ b/solution.py
@@ -294,11 +294,7 @@
 def far_pairs(freq):
     pairs = []
     for slot in range(0, freq, 2):
-        moves = {
-            (1, 0): (1, 1), (1, 1): (3, 0), (3, 0): (1, 0),
-            (0, 0): (2, 0), (2, 0): (2, 1), (2, 1): (0, 0),
-            (0, 1): (3, 1), (3, 1): (0, 1),
-        }
+        moves = {(1, 0): (1, 1), (2, 0): (2, 1), (0, 0): (3, 1), (3, 1): (0, 1), (0, 1): (2, 0), (2, 1): (0, 0), (3, 0): (1, 0), (1, 1): (3, 0)}
         for (at, side), (to, to_side) in sorted(moves.items()):
             pairs.append((at * freq + slot + side, to * freq + slot + to_side))
     return pairs

time: 14.7 us -> 14.7 us (level)
  waiting for transfers between devices: 0.02 us -> 0.2 us
  starting transfers between devices: 7.67 us -> 7.51 us
    ppermute x1, starting transfers between devices: 0.41 us -> 0.06 us  [body(): two = lax.ppermute(two, ('src', 'freq'), between(n_src, n_freq))]
    ppermute x1, starting transfers between devices: 1.58 us -> 1.82 us  [body(): far = lax.ppermute(image, ('src', 'freq'), far_pairs(n_freq))]
    ppermute x1, waiting for transfers between devices: 0.01 us -> 0.18 us  [body(): far = lax.ppermute(image, ('src', 'freq'), far_pairs(n_freq))]
  transfers between devices with their start and end apart: 7 -> 7, of which waited for: 0 -> 1; matrix products, arithmetic and copies ran while one was open for 0% -> 0% of each run, Pallas kernels for 24% -> 24%
where the time goes in v10:
time: 14.7 us; the launch traced here: 14.5 us
  starting transfers between devices  7.51 us (51%)
  Pallas kernels  4.41 us (30%)
  between operations  1.43 us (10%)
  local copies, waits for them, and re-layouts  0.95 us (6%)
  waiting for transfers between devices  0.2 us (1%)
    ppermute x1, starting transfers between devices, body(): second = lax.ppermute(second, ('rcv', 'freq'), around(n_rcv, n_freq, 1))  2.6 us
    ppermute x1, starting transfers between devices, body(): lax.ppermute(one, 'src', [(i, i + 1 if i % 2 == 0 else i - 1) for i in ra...  1.94 us
    ppermute x1, starting transfers between devices, body(): far = lax.ppermute(image, ('src', 'freq'), far_pairs(n_freq))  1.82 us
    pallas_call x1, Pallas kernels, body(): pl.pallas_call(functools.partial(rcv_operator_kernel, lateral), out_shape...  1.49 us
    pallas_call x1, Pallas kernels, body(): pl.pallas_call(functools.partial(src_operator_kernel, lateral, op_table.s...  1 us
    pallas_call x1, Pallas kernels, body(): pl.pallas_call(inner_kernel, out_shape=[jax.ShapeDtypeStruct((2, rows, wi...  0.94 us
    unnamed x12, local copies, waits for them, and re-layouts  0.92 us
    pallas_call x1, Pallas kernels, body(): pl.pallas_call(source_kernel, out_shape=[jax.ShapeDtypeStruct((2, rows, w...  0.54 us
  transfers between devices with their start and end apart: 7, of which 1 were waited for; matrix products, arithmetic and copies ran while one was open for 0% of the time, Pallas kernels for 24%

profile of v10, /device:TPU:0, one launch (start us, length us, event | category | flops | bytes accessed | tf_op | source)
XLA Modules:
  0.0 14.5 jit_solution(5737794906284279552)
XLA Ops:
  0.6 0.0 copy-start
  0.6 0.9 %copy-done = f32[2,1,128,128]{3,2,1,0:T(8,128)S(1)} copy-done((f32[2,1,128,128]{3,2,1,0:T(8,128)S(1)}, f32[2,1,128,128]{3,2,1,0:T(8,128)}, u32[]{:S(2)}) %copy-start) | copy-done | bytes 131096
  1.5 0.0 copy-start.4
  1.5 0.0 copy-start.5
  1.5 0.0 copy-start.3
  1.5 0.1 pack.1
  1.7 0.0 copy-start.2
  1.7 0.5 %collective-permute-start = (f32[88,128]{1,0:T(8,128)S(1)}, f32[88,128]{1,0:T(8,128)S(1)}, u32[]{:S(2)}, u32[]{:S(2)}) collective-permute-start(f32[88,128]{1,0:T(8,128)S(1)} %get-tuple-element.22), channel_id=1, source_target_pairs={{0,1},{1,3},{2,0},{3,5},{4,2},{5,7},{6,4},{7,6},{8,9},{9,11},{10,8... | collective-permute-start | bytes 135176 | tf_op jit(solution)/shard_map/ppermute | solution.py:336
  2.1 2.6 %collective-permute-start.1 = (f32[88,128]{1,0:T(8,128)S(1)}, f32[88,128]{1,0:T(8,128)S(1)}, u32[]{:S(2)}, u32[]{:S(2)}) collective-permute-start(f32[88,128]{1,0:T(8,128)S(1)} %get-tuple-element.23), channel_id=1, source_target_pairs={{0,2},{1,0},{2,4},{3,1},{4,6},{5,3},{6,7},{7,5},{8,10},{9,8},{10,1... | collective-permute-start | bytes 135176 | tf_op jit(solution)/shard_map/ppermute | solution.py:337
  4.7 0.0 copy-done.4
  5.4 0.0 copy-done.5
  5.4 0.0 copy-done.3
  5.5 0.0 copy-done.2
  5.5 0.0 copy-start.1
  5.5 1.5 %rcv_operator.1 = (f32[256,256]{1,0:T(8,128)S(1)}, bf16[256,256]{1,0:T(8,128)(2,1)S(1)}, bf16[256,256]{1,0:T(8,128)(2,1)S(1)}, f32[2,32,128]{2,1,0:T(8,128)S(1)}) custom-call(f32[6,128]{1,0:T(8,128)S(1)} %select_maximum_fusion.small_ref, f32[19,2,64]{2,1,0:T(2,128)S(1)} %bitcast.25), custom_call_target="tpu_custom_call" | custom-call | flops 1610612736 | bytes 1048576 | tf_op jit(solution)/shard_map/rcv_operator/pallas_call | solution.py:340
  7.0 0.0 collective-permute-done.first_ref
  7.0 0.0 collective-permute-done.1.second_ref
  7.0 0.0 copy-done.1
  7.0 0.3 %receivers.1 = (f32[2,128,128]{2,1,0:T(8,128)S(1)}, f32[2,40,128]{2,1,0:T(8,128)S(1)}, f32[2,40,128]{2,1,0:T(8,128)S(1)}, f32[1,128]{1,0:T(1,128)S(1)}) custom-call(f32[256,128]{1,0:T(8,128)S(1)} %bitcast.23, f32[88,128]{1,0:T(8,128)S(1)} %collective-permute-done.first_ref, f32[88,128]{1,0:T(8,128)S(1)} %collective-permute-done.1.second_ref, ...), custom_call_target="tpu_custom_call" | custom-call | tf_op jit(solution)/shard_map/receivers/pallas_call | solution.py:355
  7.3 0.2 %collective-permute-start.3 = (f32[2,40,128]{2,1,0:T(8,128)S(1)}, f32[2,40,128]{2,1,0:T(8,128)S(1)}, u32[]{:S(2)}, u32[]{:S(2)}) collective-permute-start(f32[2,40,128]{2,1,0:T(8,128)S(1)} %get-tuple-element.28), channel_id=1, source_target_pairs={{0,1},{1,0},{2,3},{3,2},{4,5},{5,4},{6,7},{7,6},{8,9},{9,8},{10,11... | collective-permute-start | bytes 122888 | tf_op jit(solution)/shard_map/ppermute | solution.py:370
  7.6 1.9 %collective-permute-start.2 = (f32[2,40,128]{2,1,0:T(8,128)S(1)}, f32[2,40,128]{2,1,0:T(8,128)S(1)}, u32[]{:S(2)}, u32[]{:S(2)}) collective-permute-start(f32[2,40,128]{2,1,0:T(8,128)S(1)} %get-tuple-element.28), channel_id=1, source_target_pairs={{0,8},{8,0},{16,24},{24,16},{1,9},{9,1},{17,25},{25,17},{2,10},{10... | collective-permute-start | bytes 122888 | tf_op jit(solution)/shard_map/ppermute | solution.py:374
  9.5 0.0 collective-permute-done.3
  9.5 1.8 %collective-permute-start.4 = (f32[1,128]{1,0:T(1,128)S(1)}, f32[1,128]{1,0:T(1,128)S(1)}, u32[]{:S(2)}, u32[]{:S(2)}) collective-permute-start(f32[1,128]{1,0:T(1,128)S(1)} %fusion.4.rest_0_), channel_id=1, source_target_pairs={{0,25},{1,16},{8,9},{9,24},{16,17},{17,0},{24,8},{25,1},{2,27},{3,... | collective-permute-start | bytes 1544 | tf_op jit(solution)/shard_map/ppermute | solution.py:377
  11.4 0.1 collective-permute-start.5
  11.4 1.0 %src_operator.1 = (bf16[1,256,256]{2,1,0:T(8,128)(2,1)S(1)}, bf16[1,256,256]{2,1,0:T(8,128)(2,1)S(1)}) custom-call(f32[2,32,128]{2,1,0:T(8,128)S(1)} %get-tuple-element.32.found_ref), custom_call_target="tpu_custom_call" | custom-call | flops 1048576 | bytes 1024 | tf_op jit(solution)/shard_map/src_operator/pallas_call | solution.py:381
  12.4 0.0 collective-permute-done.2.one_ref
  12.5 0.2 %collective-permute-done.4 = f32[1,128]{1,0:T(1,128)S(1)} collective-permute-done((f32[1,128]{1,0:T(1,128)S(1)}, f32[1,128]{1,0:T(1,128)S(1)}, u32[]{:S(2)}, u32[]{:S(2)}) %collective-permute-start.4) | collective-permute-done | bytes 544 | tf_op jit(solution)/shard_map/ppermute | solution.py:377
  12.6 0.4 %collective-permute-start.6 = (f32[1,128]{1,0:T(1,128)S(1)}, f32[1,128]{1,0:T(1,128)S(1)}, u32[]{:S(2)}, u32[]{:S(2)}) collective-permute-start(f32[1,128]{1,0:T(1,128)S(1)} %fusion.2.rest_1_), channel_id=1, source_target_pairs={{0,1},{1,0},{2,3},{3,2},{4,5},{5,4},{6,7},{7,6},{8,9},{9,8},{10,11... | collective-permute-start | bytes 1544 | tf_op jit(solution)/shard_map/ppermute | solution.py:398
  13.0 0.9 %inner.1 = (f32[2,128,128]{2,1,0:T(8,128)}, f32[1,256,256]{2,1,0:T(8,128)S(1)}) custom-call(f32[2,128,128]{2,1,0:T(8,128)S(1)} %get-tuple-element.27.field_ref, f32[2,40,128]{2,1,0:T(8,128)S(1)} %collective-permute-done.2.one_ref, bf16[1,256,256]{2,1,0:T(8,128)(2,1)S(1)} %get-tuple-element.34.high_ref, bf16[1,256,256]{2,1,0:T(8,128)(2,1)S(1)} %get-tuple-element.35.low_ref), custom_call_target="tpu_custom_call" | custom-call | flops 1610612736 | bytes 1048576 | tf_op jit(solution)/shard_map/inner/pallas_call | solution.py:403
  14.0 0.0 collective-permute-done.6.rest_2_
  14.0 0.0 collective-permute-done.5.two_ref
  14.0 0.5 %sources.1 = (f32[2,128,128]{2,1,0:T(8,128)}, f32[1,128]{1,0:T(1,128)}) custom-call(f32[2,128,128]{2,1,0:T(8,128)} %get-tuple-element.36.sunk_hbm, f32[1,256,256]{2,1,0:T(8,128)S(1)} %get-tuple-element.37.part_ref, f32[2,40,128]{2,1,0:T(8,128)S(1)} %collective-permute-done.5.two_ref, ...), custom_call_target="tpu_custom_call", output_to_operand_aliasing={{0}: (0, {})} | custom-call | tf_op jit(solution)/shard_map/sources/pallas_call | solution.py:414
  (7 shorter events, 0.1 us)
Async XLA Ops:
  0.6 0.9 %copy-start = (f32[2,1,128,128]{3,2,1,0:T(8,128)S(1)}, f32[2,1,128,128]{3,2,1,0:T(8,128)}, u32[]{:S(2)}) copy-start(f32[2,1,128,128]{3,2,1,0:T(8,128)} %param.6) | copy-start | bytes 393220
  1.5 3.2 %copy-start.4 = (s32[16,2]{0,1:T(2,128)S(1)}, s32[16,2]{0,1:T(2,128)}, u32[]{:S(2)}) copy-start(s32[16,2]{0,1:T(2,128)} %param.9) | copy-start | bytes 388
  1.5 3.9 %copy-start.5 = (s32[32]{0:T(128)S(1)}, s32[32]{0:T(128)}, u32[]{:S(2)}) copy-start(s32[32]{0:T(128)} %param.8) | copy-start | bytes 388
  1.5 3.9 %copy-start.3 = (f32[16,2]{0,1:T(2,128)S(1)}, f32[16,2]{0,1:T(2,128)}, u32[]{:S(2)}) copy-start(f32[16,2]{0,1:T(2,128)} %param.10) | copy-start | bytes 388
  1.7 3.8 %copy-start.2 = (f32[2,64,19]{1,0,2:T(2,128)S(1)}, f32[2,64,19]{1,0,2:T(2,128)}, u32[]{:S(2)}) copy-start(f32[2,64,19]{1,0,2:T(2,128)} %param.7) | copy-start | bytes 29188
  1.7 5.3 %collective-permute-start = (f32[88,128]{1,0:T(8,128)S(1)}, f32[88,128]{1,0:T(8,128)S(1)}, u32[]{:S(2)}, u32[]{:S(2)}) collective-permute-start(f32[88,128]{1,0:T(8,128)S(1)} %get-tuple-element.22), channel_id=1, source_target_pairs={{0,1},{1,3},{2,0},{3,5},{4,2},{5,7},{6,4},{7,6},{8,9},{9,11},{10,8... | collective-permute-start | bytes 135176 | tf_op jit(solution)/shard_map/ppermute | solution.py:336
  2.1 4.8 %collective-permute-start.1 = (f32[88,128]{1,0:T(8,128)S(1)}, f32[88,128]{1,0:T(8,128)S(1)}, u32[]{:S(2)}, u32[]{:S(2)}) collective-permute-start(f32[88,128]{1,0:T(8,128)S(1)} %get-tuple-element.23), channel_id=1, source_target_pairs={{0,2},{1,0},{2,4},{3,1},{4,6},{5,3},{6,7},{7,5},{8,10},{9,8},{10,1... | collective-permute-start | bytes 135176 | tf_op jit(solution)/shard_map/ppermute | solution.py:337
  5.5 1.5 %copy-start.1 = (f32[2,1,128,128]{3,2,1,0:T(8,128)S(1)}, f32[2,1,128,128]{3,2,1,0:T(8,128)}, u32[]{:S(2)}) copy-start(f32[2,1,128,128]{3,2,1,0:T(8,128)} %param.6) | copy-start | bytes 393220
  7.3 2.2 %collective-permute-start.3 = (f32[2,40,128]{2,1,0:T(8,128)S(1)}, f32[2,40,128]{2,1,0:T(8,128)S(1)}, u32[]{:S(2)}, u32[]{:S(2)}) collective-permute-start(f32[2,40,128]{2,1,0:T(8,128)S(1)} %get-tuple-element.28), channel_id=1, source_target_pairs={{0,1},{1,0},{2,3},{3,2},{4,5},{5,4},{6,7},{7,6},{8,9},{9,8},{10,11... | collective-permute-start | bytes 122888 | tf_op jit(solution)/shard_map/ppermute | solution.py:370
  7.6 4.9 %collective-permute-start.2 = (f32[2,40,128]{2,1,0:T(8,128)S(1)}, f32[2,40,128]{2,1,0:T(8,128)S(1)}, u32[]{:S(2)}, u32[]{:S(2)}) collective-permute-start(f32[2,40,128]{2,1,0:T(8,128)S(1)} %get-tuple-element.28), channel_id=1, source_target_pairs={{0,8},{8,0},{16,24},{24,16},{1,9},{9,1},{17,25},{25,17},{2,10},{10... | collective-permute-start | bytes 122888 | tf_op jit(solution)/shard_map/ppermute | solution.py:374
  9.5 3.1 %collective-permute-start.4 = (f32[1,128]{1,0:T(1,128)S(1)}, f32[1,128]{1,0:T(1,128)S(1)}, u32[]{:S(2)}, u32[]{:S(2)}) collective-permute-start(f32[1,128]{1,0:T(1,128)S(1)} %fusion.4.rest_0_), channel_id=1, source_target_pairs={{0,25},{1,16},{8,9},{9,24},{16,17},{17,0},{24,8},{25,1},{2,27},{3,... | collective-permute-start | bytes 1544 | tf_op jit(solution)/shard_map/ppermute | solution.py:377
  11.4 2.6 %collective-permute-start.5 = (f32[2,40,128]{2,1,0:T(8,128)S(1)}, f32[2,40,128]{2,1,0:T(8,128)S(1)}, u32[]{:S(2)}, u32[]{:S(2)}) collective-permute-start(f32[2,40,128]{2,1,0:T(8,128)S(1)} %dynamic_update_slice.3), channel_id=1, source_target_pairs={{0,1},{1,0},{8,16},{9,17},{16,8},{17,9},{24,25},{25,24},{2,3},{3,2... | collective-permute-start | bytes 122888 | tf_op jit(solution)/shard_map/ppermute | solution.py:380
  12.6 1.3 %collective-permute-start.6 = (f32[1,128]{1,0:T(1,128)S(1)}, f32[1,128]{1,0:T(1,128)S(1)}, u32[]{:S(2)}, u32[]{:S(2)}) collective-permute-start(f32[1,128]{1,0:T(1,128)S(1)} %fusion.2.rest_1_), channel_id=1, source_target_pairs={{0,1},{1,0},{2,3},{3,2},{4,5},{5,4},{6,7},{7,6},{8,9},{9,8},{10,11... | collective-permute-start | bytes 1544 | tf_op jit(solution)/shard_map/ppermute | solution.py:398
